TPU v7x, 32 devices: a whole 2x2x4 slice. The times are simulated.
32 devices in a mesh: fsdp: 16 (over z, y, x), tp: 2 (over core).
Axes of the slice: x: 2, y: 2, z: 4, core: 2. Of those that a mesh axis runs over, the one named last changes fastest.
Arguments:
- tokens: bfloat16 [8192, 2048], P(('fsdp', 'tp'))
- cotangent: bfloat16 [8192, 2048], P(('fsdp', 'tp')), may hold values from -6 to 6
- seg_ids: int32 [8192], P('fsdp'), may hold values from 0 to 12, as said below
- parents: int32 [16, 13], P('fsdp'), may hold values from 0 to 11, as said below
- valid_mask: int32 [8192], P('fsdp'), may hold values from 0 to 1, as said below
- ln1_gain: float32 [2048], replicated, may hold values from 0.5 to 1.5
- ln1_bias: float32 [2048], replicated, may hold values from -1.5 to 1.5
- w_qkv: bfloat16 [2048, 3, 2048], P('fsdp', None, 'tp')
- qkv_bias: float32 [3, 2048], P(None, 'tp'), may hold values from -1.5 to 1.5
- w_out: bfloat16 [2048, 2048], P('fsdp', 'tp'), may hold values from -0.25 to 0.25
- ln2_gain: float32 [2048], replicated, may hold values from 0.5 to 1.5
- ln2_bias: float32 [2048], replicated, may hold values from -1.5 to 1.5
- w_gate_up: bfloat16 [2048, 2, 5632], P('fsdp', None, 'tp')
- w_down: bfloat16 [2048, 5632], P('fsdp', 'tp'), may hold values from -0.15625 to 0.15625
Outputs:
- output: bfloat16 [8192, 2048], P(('fsdp', 'tp'))
- tokens_grad: float32 [8192, 2048], P(('fsdp', 'tp'))
- ln1_gain_grad: float32 [2048], replicated
- ln1_bias_grad: float32 [2048], replicated
- qkv_grad: float32 [2048, 3, 2048], P('fsdp', None, 'tp')
- qkv_bias_grad: float32 [3, 2048], P(None, 'tp')
- out_grad: float32 [2048, 2048], P('fsdp', 'tp')
- ln2_gain_grad: float32 [2048], replicated
- ln2_bias_grad: float32 [2048], replicated
- gate_up_grad: float32 [2048, 2, 5632], P('fsdp', None, 'tp')
- down_grad: float32 [2048, 5632], P('fsdp', 'tp')
- stream_rms: float32 [3], replicated
Inputs may be any that keep to these rules, and one draw needn't show every extreme that they name: `seg_ids`: in each group of 512 rows the segment numbers never fall, start at 0, and each of 0 to 12 occurs on some valid row. parents[g, 0] = 0 and parents[g, 1] = 0; any other segment's parent is 0 or an earlier segment whose parent is 0. `valid_mask`: padding slots of a group lie right after the tokens of its segment 0 and carry segment 0; the first and the last row of every group are valid.
All inputs are finite; a program needn't handle non-finite values.
Results may differ from a plain program's by a relative error of at most 0.015.
Values may be sent and summed in bfloat16 or wider, within the bound.
No kernel may reach another device: no remote copies, remote signals or barrier semaphores. Data moves between devices by JAX's collectives and lax.ppermute only.
A program may use at most 256 MiB of HBM per device.

v0:
```python
from functools import partial
import math

import jax
import jax.numpy as jnp
from jax import lax
from jax.sharding import PartitionSpec as P

HD = 64
ROT = 16


epsilon = 1e-05
score_scale = 0.125
masked_fill = -1e30


def tree_mask(seg_ids, parents, valid_mask):
    row_count = seg_ids.shape[0]
    labels = jnp.arange(parents.shape[0], dtype=jnp.int32)
    parent_one = jnp.sum(
        jnp.where(seg_ids[:, None] == labels[None, :], parents[None, :], 0), axis=1
    )
    parent_two = jnp.sum(
        jnp.where(parent_one[:, None] == labels[None, :], parents[None, :], 0), axis=1
    )
    row_ids = jnp.arange(row_count, dtype=jnp.int32)
    key_segs = seg_ids[None, :]
    related = (
        (key_segs == seg_ids[:, None])
        | (key_segs == parent_one[:, None])
        | (key_segs == parent_two[:, None])
    )
    allowed = related & (row_ids[None, :] <= row_ids[:, None]) & (valid_mask[None, :] > 0)
    allowed = allowed | (row_ids[None, :] == row_ids[:, None])
    positions = jnp.sum(allowed.astype(jnp.int32), axis=1) - 1
    return (allowed, positions)


def rotary_tables(positions, rot_width):
    half_width = rot_width // 2
    inverse_freq = jnp.exp(
        jnp.arange(half_width, dtype=jnp.float32) * (-2.0 * math.log(10000.0) / rot_width)
    )
    angles = positions.astype(jnp.float32)[:, None] * inverse_freq[None, :]
    return (jnp.cos(angles), jnp.sin(angles))


def rotate(values, cosine, sine):
    half_width = cosine.shape[1]
    first_half = values[..., :half_width]
    second_half = values[..., half_width : 2 * half_width]
    remainder = values[..., 2 * half_width :]
    cos_b = cosine[:, None, :]
    sin_b = sine[:, None, :]
    return jnp.concatenate(
        [
            first_half * cos_b - second_half * sin_b,
            second_half * cos_b + first_half * sin_b,
            remainder,
        ],
        axis=-1,
    )


def layer_norm(values, gain, shift):
    centre = values - jnp.mean(values, axis=-1, keepdims=True)
    inverse = lax.rsqrt(jnp.mean(centre * centre, axis=-1, keepdims=True) + epsilon)
    normed = centre * inverse
    return (normed * gain + shift, normed, inverse)


def norm_back(grad_out, normed, inverse, gain):
    scaled = grad_out * gain
    centred = (
        scaled
        - jnp.mean(scaled, axis=-1, keepdims=True)
        - normed * jnp.mean(scaled * normed, axis=-1, keepdims=True)
    )
    return (inverse * centred, jnp.sum(grad_out * normed, axis=0), jnp.sum(grad_out, axis=0))


def fetch_attention(w_qkv, w_out):
    return (
        lax.all_gather(w_qkv, "fsdp", axis=0, tiled=True),
        lax.all_gather(w_out, "fsdp", axis=0, tiled=True),
    )


def fetch_mlp(w_gate_up, w_down):
    return (
        lax.all_gather(w_gate_up, "fsdp", axis=0, tiled=True),
        lax.all_gather(w_down, "fsdp", axis=0, tiled=True),
    )


def by_pairs(values, pair_count):
    return values.reshape(values.shape[0], pair_count, -1).transpose(1, 0, 2)


def from_pairs(values):
    return values.transpose(1, 0, 2).reshape(values.shape[1], -1)


def pair_heads(values):
    return values.reshape(values.shape[0], -1, HD)


def flat_heads(values):
    return values.reshape(values.shape[0], -1)


def attend_forward(allowed, packed):
    query_rows = pair_heads(packed[0])
    key_rows = pair_heads(packed[1])
    value_rows = pair_heads(packed[2])
    scores = (
        jnp.einsum("rhe,khe->hrk", query_rows, key_rows, preferred_element_type=jnp.float32)
        * score_scale
    )
    scores = jnp.where(allowed[None], scores, masked_fill)
    row_max = jnp.max(scores, axis=-1, keepdims=True)
    exponent = jnp.exp(scores - row_max)
    row_sum = jnp.sum(exponent, axis=-1, keepdims=True)
    attn_probs = (exponent / row_sum).astype(jnp.bfloat16)
    context = jnp.einsum("hrk,khe->rhe", attn_probs, value_rows, preferred_element_type=jnp.float32)
    return (flat_heads(context), (row_max + jnp.log(row_sum))[..., 0])


def attend_backward(allowed, packed):
    query_rows = pair_heads(packed[0])
    key_rows = pair_heads(packed[1])
    value_rows = pair_heads(packed[2])
    grad_rows = pair_heads(packed[3])
    log_total = packed[4]
    scores = (
        jnp.einsum("rhe,khe->hrk", query_rows, key_rows, preferred_element_type=jnp.float32)
        * score_scale
    )
    scores = jnp.where(allowed[None], scores, masked_fill)
    attn_probs = jnp.exp(scores - log_total[..., None])
    grad_probs = jnp.einsum(
        "rhe,khe->hrk", grad_rows, value_rows, preferred_element_type=jnp.float32
    )
    grad_values = jnp.einsum(
        "hrk,rhe->khe",
        attn_probs.astype(jnp.bfloat16),
        grad_rows,
        preferred_element_type=jnp.float32,
    )
    inner_sum = jnp.sum(attn_probs * grad_probs, axis=-1, keepdims=True)
    grad_scores = (attn_probs * (grad_probs - inner_sum)).astype(jnp.bfloat16)
    grad_queries = (
        jnp.einsum("hrk,khe->rhe", grad_scores, key_rows, preferred_element_type=jnp.float32)
        * score_scale
    )
    grad_keys = (
        jnp.einsum("hrk,rhe->khe", grad_scores, query_rows, preferred_element_type=jnp.float32)
        * score_scale
    )
    return (flat_heads(grad_queries), flat_heads(grad_keys), flat_heads(grad_values))


def shards(
    tokens,
    cotangent,
    seg_ids,
    parents,
    valid_mask,
    ln1_gain,
    ln1_bias,
    w_qkv,
    qkv_bias,
    w_out,
    ln2_gain,
    ln2_bias,
    w_gate_up,
    w_down,
):
    model_width = tokens.shape[1]
    own_rows = tokens.shape[0]
    tp_index = lax.axis_index("tp")
    local_width = w_qkv.shape[2]
    pair_count = local_width // (2 * HD)
    allowed, positions = tree_mask(seg_ids, parents[0], valid_mask)
    cosine, sine = rotary_tables(positions, ROT)
    keep_rows = valid_mask.astype(jnp.float32)[:, None]
    own_valid = lax.dynamic_slice_in_dim(keep_rows, tp_index * own_rows, own_rows, 0)
    stream = tokens.astype(jnp.float32)
    normed1, norm_hat1, inv_std1 = layer_norm(stream, ln1_gain, ln1_bias)
    spread1 = lax.all_gather(normed1.astype(jnp.bfloat16), "tp", axis=0, tiled=True)
    qkv_full, out_full = fetch_attention(w_qkv, w_out)
    linear = (
        jnp.einsum("rd,dcf->rcf", spread1, qkv_full, preferred_element_type=jnp.float32)
        + qkv_bias[None]
    )
    group_rows = linear.shape[0]
    queries = (
        rotate(pair_heads(linear[:, 0]), cosine, sine)
        .astype(jnp.bfloat16)
        .reshape(group_rows, local_width)
    )
    keys_all = (
        rotate(pair_heads(linear[:, 1]), cosine, sine)
        .astype(jnp.bfloat16)
        .reshape(group_rows, local_width)
    )
    values_all = linear[:, 2].astype(jnp.bfloat16)
    query_pairs = by_pairs(queries, pair_count)
    key_pairs = by_pairs(keys_all, pair_count)
    value_pairs = by_pairs(values_all, pair_count)
    context_pairs, log_totals = lax.map(
        partial(attend_forward, allowed), (query_pairs, key_pairs, value_pairs)
    )
    context = (from_pairs(context_pairs) * keep_rows).astype(jnp.bfloat16)
    attn_partial = jnp.einsum("rf,df->rd", context, out_full, preferred_element_type=jnp.float32)
    attn_out = lax.psum_scatter(attn_partial, "tp", scatter_dimension=0, tiled=True)
    residual = stream + attn_out
    normed2, norm_hat2, inv_std2 = layer_norm(residual, ln2_gain, ln2_bias)
    spread2, cot_full = (
        lax.all_gather(normed2.astype(jnp.bfloat16), "tp", axis=0, tiled=True),
        lax.all_gather(cotangent, "tp", axis=0, tiled=True),
    )
    gate_up_full, down_full = fetch_mlp(w_gate_up, w_down)
    gate_up = jnp.einsum("rd,dcf->rcf", spread2, gate_up_full, preferred_element_type=jnp.float32)
    gate_part = gate_up[:, 0]
    up_part = gate_up[:, 1]
    activated = jax.nn.silu(gate_part)
    hidden = (activated * up_part).astype(jnp.bfloat16)
    mlp_partial = jnp.einsum("rf,df->rd", hidden, down_full, preferred_element_type=jnp.float32)
    mlp_out = lax.psum_scatter(
        mlp_partial.astype(jnp.bfloat16), "tp", scatter_dimension=0, tiled=True
    ).astype(jnp.float32)
    stream_out = residual + mlp_out
    output = stream_out.astype(jnp.bfloat16)
    squares = jnp.stack(
        [
            jnp.sum(own_valid * stream_out * stream_out),
            jnp.sum(own_valid * attn_out * attn_out),
            jnp.sum(own_valid * mlp_out * mlp_out),
        ]
    )
    square_sums, valid_count = lax.psum((squares, jnp.sum(own_valid)), ("fsdp", "tp"))
    stream_rms = jnp.sqrt(square_sums / (valid_count * model_width))
    gate_up_full, down_full = fetch_mlp(w_gate_up, w_down)
    d_hidden = jnp.einsum("rd,df->rf", cot_full, down_full, preferred_element_type=jnp.float32)
    down_term = jnp.einsum("rd,rf->df", cot_full, hidden, preferred_element_type=jnp.float32)
    sigmoid_gate = jax.nn.sigmoid(gate_part)
    d_gate = d_hidden * up_part * sigmoid_gate * (1.0 + gate_part * (1.0 - sigmoid_gate))
    d_up = d_hidden * activated
    d_gate_up = jnp.stack([d_gate, d_up], axis=1).astype(jnp.bfloat16)
    gate_up_term = jnp.einsum("rd,rcf->dcf", spread2, d_gate_up, preferred_element_type=jnp.float32)
    d_normed2 = lax.psum_scatter(
        jnp.einsum("rcf,dcf->rd", d_gate_up, gate_up_full, preferred_element_type=jnp.float32),
        "tp",
        scatter_dimension=0,
        tiled=True,
    )
    gate_up_grad, down_grad = (
        lax.psum_scatter(gate_up_term, "fsdp", scatter_dimension=0, tiled=True),
        lax.psum_scatter(down_term, "fsdp", scatter_dimension=0, tiled=True),
    )
    d_resid_norm, gain_two_grad, bias_two_grad = norm_back(d_normed2, norm_hat2, inv_std2, ln2_gain)
    d_residual = cotangent.astype(jnp.float32) + d_resid_norm
    spread_grad = lax.all_gather(d_residual.astype(jnp.bfloat16), "tp", axis=0, tiled=True)
    qkv_full, out_full = fetch_attention(w_qkv, w_out)
    out_term = jnp.einsum("rd,rf->df", spread_grad, context, preferred_element_type=jnp.float32)
    d_context = (
        jnp.einsum("rd,df->rf", spread_grad, out_full, preferred_element_type=jnp.float32)
        * keep_rows
    ).astype(jnp.bfloat16)
    grad_pairs = lax.map(
        partial(attend_backward, allowed),
        (query_pairs, key_pairs, value_pairs, by_pairs(d_context, pair_count), log_totals),
    )
    d_queries = rotate(pair_heads(from_pairs(grad_pairs[0])), cosine, -sine).reshape(
        group_rows, local_width
    )
    d_keys = rotate(pair_heads(from_pairs(grad_pairs[1])), cosine, -sine).reshape(
        group_rows, local_width
    )
    d_values = from_pairs(grad_pairs[2])
    d_linear = jnp.stack([d_queries, d_keys, d_values], axis=1).astype(jnp.bfloat16)
    qkv_term = jnp.einsum("rd,rcf->dcf", spread1, d_linear, preferred_element_type=jnp.float32)
    bias_local = jnp.sum(d_linear, axis=0, dtype=jnp.float32)
    d_normed1 = lax.psum_scatter(
        jnp.einsum("rcf,dcf->rd", d_linear, qkv_full, preferred_element_type=jnp.float32).astype(
            jnp.bfloat16
        ),
        "tp",
        scatter_dimension=0,
        tiled=True,
    ).astype(jnp.float32)
    qkv_grad, out_grad = (
        lax.psum_scatter(qkv_term, "fsdp", scatter_dimension=0, tiled=True),
        lax.psum_scatter(out_term, "fsdp", scatter_dimension=0, tiled=True),
    )
    d_stream_norm, gain_one_grad, bias_one_grad = norm_back(
        d_normed1, norm_hat1, inv_std1, ln1_gain
    )
    tokens_grad = d_residual + d_stream_norm
    norm_terms = jnp.stack([gain_one_grad, bias_one_grad, gain_two_grad, bias_two_grad])
    bias_spread = lax.dynamic_update_slice(
        jnp.zeros((3, model_width), jnp.float32), bias_local, (0, tp_index * local_width)
    )
    norm_sums, bias_sums = lax.psum((norm_terms, bias_spread), ("fsdp", "tp"))
    qkv_bias_grad = lax.dynamic_slice(bias_sums, (0, tp_index * local_width), (3, local_width))
    return (
        output,
        tokens_grad,
        norm_sums[0],
        norm_sums[1],
        qkv_grad,
        qkv_bias_grad,
        out_grad,
        norm_sums[2],
        norm_sums[3],
        gate_up_grad,
        down_grad,
        stream_rms,
    )


def solution(mesh):
    return jax.shard_map(
        shards,
        mesh=mesh,
        in_specs=(
            P(("fsdp", "tp"), None),
            P(("fsdp", "tp"), None),
            P("fsdp"),
            P("fsdp", None),
            P("fsdp"),
            P(),
            P(),
            P("fsdp", None, "tp"),
            P(None, "tp"),
            P("fsdp", "tp"),
            P(),
            P(),
            P("fsdp", None, "tp"),
            P("fsdp", "tp"),
        ),
        out_specs=(
            P(("fsdp", "tp"), None),
            P(("fsdp", "tp"), None),
            P(),
            P(),
            P("fsdp", None, "tp"),
            P(None, "tp"),
            P("fsdp", "tp"),
            P(),
            P(),
            P("fsdp", None, "tp"),
            P("fsdp", "tp"),
            P(),
        ),
        check_vma=False,
    )
```

profile of v0, /device:TPU:0, one launch (start us, length us, event | category | flops | bytes accessed | tf_op | source)
XLA Modules:
  0.0 3026.4 jit_solution(4560207764650102700)
XLA Ops:
  15.0 10.5 all-gather.9.cloned.1.call-done
  25.4 155.8 %all-gather.11.cloned.1.call-done = bf16[2048,3,1024]{2,0,1:T(8,128)(2,1)} async-done(((bf16[128,3,1024]{2,0,1:T(8,128)(2,1)}), bf16[2048,3,1024]{2,0,1:T(8,128)(2,1)}) %all-gather.11.cloned.1.call-update) | async-done | bytes 12582928 | tf_op jit(solution)/shard_map/all_gather | solution.py:85
  181.3 9.9 broadcast_add_fusion
  207.3 33.3 %while.28 = (s32[]{:T(128)}, f32[8,512,128]{1,2,0:T(8,128)S(1)}, f32[8,2,512]{2,1,0:T(2,128)S(1)}, bf16[8,512,128]{1,2,0:T(8,128)(2,1)}, bf16[8,512,128]{1,2,0:T...) while((s32[]{:T(128)}, f32[8,512,128]{1,2,0:T(8,128)S(1)}, ...), condition=%wide.region_8.9_spmd.clone, body=%wide.region_5.8_spmd.clone.sunk | while | flops 143129600 | bytes 9345661 | solution.py:212
  242.4 15.9 all-gather.13.cloned.1.call-done
  265.5 10.8 reduce-scatter.9.cloned.1.call-done
  292.4 256.1 %all-gather.17.cloned.1.call-done = bf16[2048,2,2816]{2,0,1:T(8,128)(2,1)} async-done(((bf16[128,2,2816]{2,0,1:T(8,128)(2,1)}), bf16[2048,2,2816]{2,0,1:T(8,128)(2,1)}) %all-gather.17.cloned.1.call-update) | async-done | bytes 23068688 | tf_op jit(solution)/shard_map/all_gather | solution.py:92
  548.4 19.6 fusion.42
  568.1 137.3 %all-gather.19.cloned.1.call-done = bf16[2048,2816]{1,0:T(8,128)(2,1)} async-done(((bf16[128,2816]{1,0:T(8,128)(2,1)}), bf16[2048,2816]{1,0:T(8,128)(2,1)}) %all-gather.19.cloned.1.call-update) | async-done | bytes 11534352 | tf_op jit(solution)/shard_map/all_gather | solution.py:93
  705.4 16.5 fusion.25
  721.9 8.7 convolution_convert_fusion
  731.1 20.4 fusion.20
  752.3 9.6 reduce-scatter.13.cloned.1.call-done
  770.4 11.7 all-gather.23.cloned.1.call-done
  790.5 63.5 %while.29 = (s32[]{:T(128)}, f32[8,512,128]{1,2,0:T(8,128)S(1)}, f32[8,512,128]{1,2,0:T(8,128)}, bf16[8,512,128]{1,2,0:T(8,128)(2,1)S(1)}, bf16[8,512,128]{1,2,0...) while((s32[]{:T(128)}, f32[8,512,128]{1,2,0:T(8,128)S(1)}, ...), condition=%wide.region_18.19_spmd.clone, body=%wide.region_16.18_spmd.clone.sunk | while | flops 343014400 | bytes 20212892 | solution.py:272
  862.7 11.1 bitcast_convert_fusion
  875.4 13.1 convolution_bitcast_fusion
  890.1 21.0 fusion.18
  921.6 13.4 fusion.44
  942.3 52.0 %all-reduce = (f32[4,2048]{1,0:T(4,128)S(1)}, f32[3,2048]{1,0:T(4,128)S(1)}, f32[3]{0:T(128)S(1)}, f32[]{:T(128)}) all-reduce(f32[4,2048]{1,0:T(4,128)S(1)} %pad_maximum_fusion.10, f32[3,2048]{1,0:T(4,128)S(1)} %constant_dynamic-update-slice_fusion.4, f32[3]{0:T(128)S(1)} %pad_maximum_fusion.11, ...), channel_id=1, replica_groups=mesh['fsdp'=16,'tp'=2] {'fsdp','tp'}, use_global_device_ids=true, to_apply=%region_26.27 | all-reduce | flops 14340 | bytes 114720 | tf_op jit(solution)/shard_map/psum | solution.py:306
  1000.1 364.3 %reduce-scatter.23.cloned.1.call-done = f32[128,2816]{0,1:T(8,128)} async-done(((f32[2048,2816]{0,1:T(8,128)}), f32[128,2816]{0,1:T(8,128)}) %reduce-scatter.23.cloned.1.call-update) | async-done | bytes 1441808 | tf_op jit(solution)/shard_map/reduce_scatter | solution.py:261
  1367.3 944.3 %reduce-scatter.21.cloned.1.call-done = f32[128,2,2816]{2,0,1:T(8,128)} async-done(((f32[2048,2,2816]{2,0,1:T(8,128)}), f32[128,2,2816]{2,0,1:T(8,128)}) %reduce-scatter.21.cloned.1.call-update) | async-done | bytes 2883600 | tf_op jit(solution)/shard_map/reduce_scatter | solution.py:260
  2317.2 180.0 %reduce-scatter.19.cloned.1.call-done = f32[128,1024]{1,0:T(8,128)} async-done(((f32[2048,1024]{1,0:T(8,128)}), f32[128,1024]{1,0:T(8,128)}) %reduce-scatter.19.cloned.1.call-update) | async-done | bytes 524304 | tf_op jit(solution)/shard_map/reduce_scatter | solution.py:296
  2497.3 522.2 %reduce-scatter.17.cloned.1.call-done = f32[128,3,1024]{2,0,1:T(8,128)} async-done(((f32[2048,3,1024]{2,0,1:T(8,128)}), f32[128,3,1024]{2,0,1:T(8,128)}) %reduce-scatter.17.cloned.1.call-update) | async-done | bytes 1572880 | tf_op jit(solution)/shard_map/reduce_scatter | solution.py:295
  (343 shorter events, 205.5 us)
Async XLA Ops:
  7.2 18.2 all-gather.9.cloned.1.call-start
  10.5 170.7 %copy-start.15 = (f32[3,1024]{1,0:T(4,128)S(1)}, f32[3,1024]{1,0:T(4,128)}, u32[]{:S(2)}) copy-start(f32[3,1024]{1,0:T(4,128)} %param.26) | copy-start | bytes 36868
  12.0 169.2 %all-gather.11.cloned.1.call-start = ((), (), s32[]{:S(2)}) async-start(), calls=%async_computation.9 | async-start | bytes 13369344 | tf_op jit(solution)/shard_map/all_gather | solution.py:85
  12.8 245.6 %all-gather.13.cloned.1.call-start = ((), (), s32[]{:S(2)}) async-start(), calls=%async_computation.10 | async-start | bytes 4456448 | tf_op jit(solution)/shard_map/all_gather | solution.py:86
  13.5 262.8 %reduce-scatter.9.cloned.1.call-start = ((), (), s32[]{:S(2)}) async-start(), calls=%async_computation.11 | async-start | bytes 6291456 | tf_op jit(solution)/shard_map/reduce_scatter | solution.py:217
  15.0 189.0 %copy-start.16 = (f32[512,8]{0,1:T(8,128)}, f32[512,8]{0,1:T(8,128)S(1)}, u32[]{:S(2)}) copy-start(f32[512,8]{0,1:T(8,128)S(1)} %get-tuple-element.308) | copy-start | bytes 49156
  265.5 26.9 all-gather.15.cloned.1.call-start
  280.4 268.1 %all-gather.17.cloned.1.call-start = ((), (), s32[]{:S(2)}) async-start(), calls=%async_computation.13 | async-start | bytes 24510464 | tf_op jit(solution)/shard_map/all_gather | solution.py:92
  283.0 285.1 %all-gather.21.cloned.1.call-start = ((), (), s32[]{:S(2)}) async-start(), calls=%async_computation.16 | async-start | bytes 3145728 | tf_op jit(solution)/shard_map/all_gather | solution.py:222
  283.8 421.6 %all-gather.19.cloned.1.call-start = ((), (), s32[]{:S(2)}) async-start(), calls=%async_computation.14 | async-start | bytes 12255232 | tf_op jit(solution)/shard_map/all_gather | solution.py:93
  284.5 467.8 %reduce-scatter.11.cloned.1.call-start = ((), (), s32[]{:S(2)}) async-start(), calls=%async_computation.15 | async-start | bytes 3145728 | tf_op jit(solution)/shard_map/reduce_scatter | solution.py:231
  705.4 16.5 copy-start.30
  730.7 31.2 %reduce-scatter.13.cloned.1.call-start = ((), (), s32[]{:S(2)}) async-start(), calls=%async_computation.17 | async-start | bytes 6291456 | tf_op jit(solution)/shard_map/reduce_scatter | solution.py:253
  751.6 30.5 %all-gather.23.cloned.1.call-start = ((), (), s32[]{:S(2)}) async-start(), calls=%async_computation.18 | async-start | bytes 3145728 | tf_op jit(solution)/shard_map/all_gather | solution.py:265
  761.9 5.6 copy-start.5
  770.1 169.9 %reduce-scatter.15.cloned.1.call-start = ((), (), s32[]{:S(2)}) async-start(), calls=%async_computation.19 | async-start | bytes 3145728 | tf_op jit(solution)/shard_map/reduce_scatter | solution.py:286
  858.6 61.8 %copy-start.6 = (bf16[512,1,1024]{2,0,1:T(8,128)(2,1)}, bf16[512,1,1024]{2,0,1:T(8,128)(2,1)S(1)}, u32[]{:S(2)}) copy-start(bf16[512,1,1024]{2,0,1:T(8,128)(2,1)S(1)} %copy.75) | copy-start | bytes 3145732
  860.8 13.0 copy-start.7
  862.7 11.1 copy-start.9
  873.9 490.5 %reduce-scatter.23.cloned.1.call-start = ((), (), s32[]{:S(2)}) async-start(), calls=%async_computation.23 | async-start | bytes 24510464 | tf_op jit(solution)/shard_map/reduce_scatter | solution.py:261
  888.6 1423.0 %reduce-scatter.21.cloned.1.call-start = ((), (), s32[]{:S(2)}) async-start(), calls=%async_computation.22 | async-start | bytes 49020928 | tf_op jit(solution)/shard_map/reduce_scatter | solution.py:260
  911.2 1586.1 %reduce-scatter.19.cloned.1.call-start = ((), (), s32[]{:S(2)}) async-start(), calls=%async_computation.21 | async-start | bytes 8912896 | tf_op jit(solution)/shard_map/reduce_scatter | solution.py:296
  920.1 2099.3 %reduce-scatter.17.cloned.1.call-start = ((), (), s32[]{:S(2)}) async-start(), calls=%async_computation.20 | async-start | bytes 26738688 | tf_op jit(solution)/shard_map/reduce_scatter | solution.py:295
  937.2 59.6 %copy-start.2 = (f32[256,2048]{1,0:T(8,128)S(1)}, f32[256,2048]{1,0:T(8,128)}, u32[]{:S(2)}) copy-start(f32[256,2048]{1,0:T(8,128)} %get-tuple-element.267) | copy-start | bytes 6291460
  (25 other events, 74.5 us)
Sparse Core Ops, SparseCore 0:
  12.1 13.2 all-gather.8
  28.2 153.0 all-gather.10
  184.0 74.2 all-gather.12
  265.6 10.6 reduce-scatter.8
  280.5 11.8 all-gather.14
  295.9 252.4 all-gather.16
  550.1 8.7 all-gather.20
  562.0 143.3 all-gather.18
  730.8 7.7 reduce-scatter.10
  751.7 10.1 reduce-scatter.12
  770.2 11.8 all-gather.22
  874.0 10.7 reduce-scatter.14
  888.7 475.6 reduce-scatter.22
  1366.6 944.9 reduce-scatter.20
  2314.3 182.8 reduce-scatter.18
  2500.0 519.3 reduce-scatter.16
where the time goes:
time: 3040 us; the launch traced here: 3030 us
  waiting for transfers between devices  2630 us (87%)
  matrix products  185 us (6%)
  local copies, waits for them, and re-layouts  93.3 us (3%)
  blocking collectives  52 us (2%)
  other arithmetic  48.7 us (2%)
    reduce_scatter x1, waiting for transfers between devices, shards(): lax.psum_scatter(gate_up_term, 'fsdp', scatter_dimension=0, tiled=True)  944 us
    reduce_scatter x1, waiting for transfers between devices, shards(): lax.psum_scatter(qkv_term, 'fsdp', scatter_dimension=0, tiled=True)  522 us
    reduce_scatter x1, waiting for transfers between devices, shards(): lax.psum_scatter(down_term, 'fsdp', scatter_dimension=0, tiled=True)  364 us
    all_gather x1, waiting for transfers between devices, fetch_mlp(): lax.all_gather(w_gate_up, 'fsdp', axis=0, tiled=True)  256 us
    reduce_scatter x1, waiting for transfers between devices, shards(): lax.psum_scatter(out_term, 'fsdp', scatter_dimension=0, tiled=True)  180 us
    all_gather x1, waiting for transfers between devices, fetch_attention(): lax.all_gather(w_qkv, 'fsdp', axis=0, tiled=True)  156 us
    all_gather x1, waiting for transfers between devices, fetch_mlp(): lax.all_gather(w_down, 'fsdp', axis=0, tiled=True)  137 us
  transfers between devices with their start and end apart: 16, of which 13 were waited for; matrix products, arithmetic and copies ran while one was open for 6% of the time, Pallas kernels for 0%

commit v1 on v0

v1 whole, which is shorter than its diff:
```python
from functools import partial
import math

import jax
import jax.numpy as jnp
from jax import lax
from jax.sharding import Mesh, PartitionSpec as P

HD = 64
ROT = 16

epsilon = 1e-05
score_scale = 0.125
masked_fill = -1e30

FAR, MID, NEAR, TP = "far", "mid", "near", "tp"
ALL = (FAR, MID, NEAR, TP)
f32 = jnp.float32
bf16 = jnp.bfloat16


def swap(values, axis):
    return lax.ppermute(values, axis, [(0, 1), (1, 0)])


def ordered(axis, mine, other):
    first = lax.axis_index(axis) == 0
    return jnp.where(first, mine, other), jnp.where(first, other, mine)


def mine_of(axis, pair):
    return ordered(axis, pair[0], pair[1])


def spread_columns(kinds):
    width = kinds[0].shape[1] // 4

    def quarters(index):
        return jnp.concatenate(
            [kind[:, q * width : (q + 1) * width] for q in (index, 2 + index) for kind in kinds], axis=1
        )

    keep, send = mine_of(NEAR, (quarters(0), quarters(1)))
    rows = jnp.concatenate(ordered(NEAR, keep, swap(send, NEAR)), axis=0)
    half = rows.shape[1] // 2
    keep, send = mine_of(MID, (rows[:, :half], rows[:, half:]))
    return jnp.concatenate(ordered(MID, keep, swap(send, MID)), axis=0)


def return_columns(values, count):
    rows = values.shape[0] // 4
    width = values.shape[1] // count
    keep, send = mine_of(MID, (values[: 2 * rows], values[2 * rows :]))
    both = jnp.concatenate(ordered(MID, keep, swap(send, MID)), axis=1)
    keep, send = mine_of(NEAR, (both[:rows], both[rows:]))
    near = ordered(NEAR, keep, swap(send, NEAR))
    kinds = []
    for kind in range(count):
        pieces = []
        for q in range(4):
            start = (q // 2) * count * width + kind * width
            pieces.append(near[q % 2][:, start : start + width])
        kinds.append(jnp.concatenate(pieces, axis=1).astype(f32))
    return kinds


def gather_rows(own):
    half = own.shape[0] // 2
    near = swap(own, NEAR)
    mid = swap(own, MID)
    diagonal_low = swap(near[:half], MID)
    diagonal_high = swap(mid[half:], NEAR)
    core = jnp.concatenate([own, near, mid, diagonal_low, diagonal_high], axis=0)
    return jnp.concatenate([core, swap(core, TP)], axis=0)


def add_low(a, b):
    return (a.astype(f32) + b.astype(f32)).astype(bf16)


def scatter_rows(total):
    core_rows = total.shape[0] // 2
    rows = core_rows // 4
    half = rows // 2
    core = add_low(total[:core_rows], swap(total[core_rows:], TP))
    own, near, mid, diagonal = [core[i * rows : (i + 1) * rows] for i in range(4)]
    to_mid = swap(diagonal[:half], MID)
    to_near = swap(diagonal[half:], NEAR)
    near = jnp.concatenate([add_low(near[:half], to_mid), near[half:]], axis=0)
    mid = jnp.concatenate([mid[:half], add_low(mid[half:], to_near)], axis=0)
    return own.astype(f32) + swap(near, NEAR).astype(f32) + swap(mid, MID).astype(f32)


def gather_far(values):
    return lax.all_gather(values, FAR, axis=0, tiled=True)


def scatter_far(values):
    return lax.psum_scatter(values, FAR, scatter_dimension=0, tiled=True)


def plane_trees(values):
    trees = lax.all_gather(values, (MID, NEAR), axis=0, tiled=False)
    trees = trees.reshape((2, 2) + values.shape)
    trees = jnp.where(lax.axis_index(MID) == 0, trees, trees[::-1])
    trees = jnp.where(lax.axis_index(NEAR) == 0, trees, trees[:, ::-1])
    return trees.reshape((4,) + values.shape)


def tree_mask(seg_ids, parents, valid_mask, row_ids):
    labels = jnp.arange(parents.shape[0], dtype=jnp.int32)
    parent_one = jnp.sum(
        jnp.where(seg_ids[:, None] == labels[None, :], parents[None, :], 0), axis=1
    )
    parent_two = jnp.sum(
        jnp.where(parent_one[:, None] == labels[None, :], parents[None, :], 0), axis=1
    )
    key_segs = seg_ids[None, :]
    related = (
        (key_segs == seg_ids[:, None])
        | (key_segs == parent_one[:, None])
        | (key_segs == parent_two[:, None])
    )
    allowed = related & (row_ids[None, :] <= row_ids[:, None]) & (valid_mask[None, :] > 0)
    allowed = allowed | (row_ids[None, :] == row_ids[:, None])
    positions = jnp.sum(allowed.astype(jnp.int32), axis=1) - 1
    return (allowed, positions)


def rotary_tables(positions, rot_width):
    half_width = rot_width // 2
    inverse_freq = jnp.exp(
        jnp.arange(half_width, dtype=f32) * (-2.0 * math.log(10000.0) / rot_width)
    )
    angles = positions.astype(f32)[:, None] * inverse_freq[None, :]
    return (jnp.cos(angles), jnp.sin(angles))


def rotate(values, cosine, sine):
    half_width = cosine.shape[1]
    first_half = values[..., :half_width]
    second_half = values[..., half_width : 2 * half_width]
    remainder = values[..., 2 * half_width :]
    cos_b = cosine[:, None, :]
    sin_b = sine[:, None, :]
    return jnp.concatenate(
        [
            first_half * cos_b - second_half * sin_b,
            second_half * cos_b + first_half * sin_b,
            remainder,
        ],
        axis=-1,
    )


def layer_norm(values, gain, shift):
    centre = values - jnp.mean(values, axis=-1, keepdims=True)
    inverse = lax.rsqrt(jnp.mean(centre * centre, axis=-1, keepdims=True) + epsilon)
    normed = centre * inverse
    return (normed * gain + shift, normed, inverse)


def norm_back(grad_out, normed, inverse, gain):
    scaled = grad_out * gain
    centred = (
        scaled
        - jnp.mean(scaled, axis=-1, keepdims=True)
        - normed * jnp.mean(scaled * normed, axis=-1, keepdims=True)
    )
    return (inverse * centred, jnp.sum(grad_out * normed, axis=0), jnp.sum(grad_out, axis=0))


def by_trees(values):
    rows = values.shape[0] // 8
    return values.reshape(2, 4, rows, -1).transpose(1, 0, 2, 3).reshape(4, 2 * rows, -1)


def from_trees(values):
    rows = values.shape[1] // 2
    return values.reshape(4, 2, rows, -1).transpose(1, 0, 2, 3).reshape(8 * rows, -1)


def pair_heads(values):
    return values.reshape(values.shape[0], -1, HD)


def flat_heads(values):
    return values.reshape(values.shape[0], -1)


def attend_forward(packed):
    allowed = packed[3]
    query_rows = pair_heads(packed[0])
    key_rows = pair_heads(packed[1])
    value_rows = pair_heads(packed[2])
    scores = (
        jnp.einsum("rhe,khe->hrk", query_rows, key_rows, preferred_element_type=f32) * score_scale
    )
    scores = jnp.where(allowed[None], scores, masked_fill)
    row_max = jnp.max(scores, axis=-1, keepdims=True)
    exponent = jnp.exp(scores - row_max)
    row_sum = jnp.sum(exponent, axis=-1, keepdims=True)
    attn_probs = (exponent / row_sum).astype(bf16)
    context = jnp.einsum("hrk,khe->rhe", attn_probs, value_rows, preferred_element_type=f32)
    return (flat_heads(context), (row_max + jnp.log(row_sum))[..., 0])


def attend_backward(packed):
    allowed = packed[5]
    query_rows = pair_heads(packed[0])
    key_rows = pair_heads(packed[1])
    value_rows = pair_heads(packed[2])
    grad_rows = pair_heads(packed[3])
    log_total = packed[4]
    scores = (
        jnp.einsum("rhe,khe->hrk", query_rows, key_rows, preferred_element_type=f32) * score_scale
    )
    scores = jnp.where(allowed[None], scores, masked_fill)
    attn_probs = jnp.exp(scores - log_total[..., None])
    grad_probs = jnp.einsum("rhe,khe->hrk", grad_rows, value_rows, preferred_element_type=f32)
    grad_values = jnp.einsum(
        "hrk,rhe->khe", attn_probs.astype(bf16), grad_rows, preferred_element_type=f32
    )
    inner_sum = jnp.sum(attn_probs * grad_probs, axis=-1, keepdims=True)
    grad_scores = (attn_probs * (grad_probs - inner_sum)).astype(bf16)
    grad_queries = (
        jnp.einsum("hrk,khe->rhe", grad_scores, key_rows, preferred_element_type=f32) * score_scale
    )
    grad_keys = (
        jnp.einsum("hrk,rhe->khe", grad_scores, query_rows, preferred_element_type=f32)
        * score_scale
    )
    return (flat_heads(grad_queries), flat_heads(grad_keys), flat_heads(grad_values))


def shards(
    tokens,
    cotangent,
    seg_ids,
    parents,
    valid_mask,
    ln1_gain,
    ln1_bias,
    w_qkv,
    qkv_bias,
    w_out,
    ln2_gain,
    ln2_bias,
    w_gate_up,
    w_down,
):
    own_rows, model_width = tokens.shape
    tp_index = lax.axis_index(TP)
    quarter = lax.axis_index(MID) * 2 + lax.axis_index(NEAR)
    local_width = w_qkv.shape[2]
    width = local_width // 4
    units = w_down.shape[1] // 4

    own_ints = jnp.concatenate([seg_ids, valid_mask, parents[0]])
    plane_ints = plane_trees(own_ints)
    group_rows = seg_ids.shape[0]

    def halves(values):
        parts = values.reshape(4, 2, own_rows)
        return jnp.where(tp_index == 0, parts, parts[:, ::-1]).reshape(4, group_rows)

    plane_segs = halves(plane_ints[:, :group_rows])
    plane_valid = halves(plane_ints[:, group_rows : 2 * group_rows])
    plane_parents = plane_ints[:, 2 * group_rows :]
    row_ids = (jnp.arange(group_rows, dtype=jnp.int32) + tp_index * own_rows) % group_rows
    allowed, positions = jax.vmap(tree_mask, in_axes=(0, 0, 0, None))(
        plane_segs, plane_parents, plane_valid, row_ids
    )
    cosine, sine = rotary_tables(from_trees(positions[..., None])[:, 0], ROT)
    keep_rows = from_trees(plane_valid.astype(f32)[..., None])
    own_valid = keep_rows[:own_rows]

    attn_spread = spread_columns([w_qkv[:, 0], w_qkv[:, 1], w_qkv[:, 2], w_out])
    attn_full = gather_far(attn_spread)
    mlp_spread = spread_columns([w_gate_up[:, 0], w_gate_up[:, 1], w_down])
    mlp_full = gather_far(mlp_spread)
    qkv_full = attn_full[:, : 3 * width]
    out_full = attn_full[:, 3 * width :]
    gate_up_full = mlp_full[:, : 2 * units]
    down_full = mlp_full[:, 2 * units :]

    stream = tokens.astype(f32)
    normed1, norm_hat1, inv_std1 = layer_norm(stream, ln1_gain, ln1_bias)
    spread1 = gather_rows(normed1.astype(bf16))
    own_bias = lax.dynamic_slice(qkv_bias, (0, quarter * width), (3, width))
    linear = jnp.dot(spread1, qkv_full, preferred_element_type=f32) + own_bias.reshape(1, -1)
    queries = flat_heads(rotate(pair_heads(linear[:, :width]), cosine, sine)).astype(bf16)
    keys_all = flat_heads(rotate(pair_heads(linear[:, width : 2 * width]), cosine, sine)).astype(
        bf16
    )
    values_all = linear[:, 2 * width :].astype(bf16)
    trees = (by_trees(queries), by_trees(keys_all), by_trees(values_all))
    context_trees, log_totals = lax.map(attend_forward, trees + (allowed,))
    context = (from_trees(context_trees) * keep_rows).astype(bf16)
    attn_partial = jnp.einsum("rf,df->rd", context, out_full, preferred_element_type=f32)
    attn_out = scatter_rows(attn_partial.astype(bf16))
    residual = stream + attn_out

    normed2, norm_hat2, inv_std2 = layer_norm(residual, ln2_gain, ln2_bias)
    cot_full = gather_rows(cotangent)
    spread2 = gather_rows(normed2.astype(bf16))
    gate_up = jnp.dot(spread2, gate_up_full, preferred_element_type=f32)
    gate_part = gate_up[:, :units]
    up_part = gate_up[:, units:]
    sigmoid_gate = jax.nn.sigmoid(gate_part)
    activated = gate_part * sigmoid_gate
    hidden = (activated * up_part).astype(bf16)
    mlp_partial = jnp.einsum("rf,df->rd", hidden, down_full, preferred_element_type=f32)
    mlp_out = scatter_rows(mlp_partial.astype(bf16))
    stream_out = residual + mlp_out
    output = stream_out.astype(bf16)

    d_hidden = jnp.dot(cot_full, down_full, preferred_element_type=f32)
    d_gate = d_hidden * up_part * sigmoid_gate * (1.0 + gate_part * (1.0 - sigmoid_gate))
    d_up = d_hidden * activated
    d_gate_up = jnp.concatenate([d_gate, d_up], axis=1).astype(bf16)
    d_normed2 = scatter_rows(
        jnp.einsum("rf,df->rd", d_gate_up, gate_up_full, preferred_element_type=f32).astype(bf16)
    )
    down_term = jnp.einsum("rd,rf->df", cot_full, hidden, preferred_element_type=f32)
    gate_up_term = jnp.einsum("rd,rf->df", spread2, d_gate_up, preferred_element_type=f32)
    mlp_grads = return_columns(
        scatter_far(
            jnp.concatenate([gate_up_term.astype(bf16), down_term.astype(bf16)], axis=1)
        ),
        3,
    )
    gate_up_grad = jnp.stack(mlp_grads[:2], axis=1)
    down_grad = mlp_grads[2]

    d_resid_norm, gain_two_grad, bias_two_grad = norm_back(d_normed2, norm_hat2, inv_std2, ln2_gain)
    d_residual = cotangent.astype(f32) + d_resid_norm
    spread_grad = gather_rows(d_residual.astype(bf16))
    out_term = jnp.einsum("rd,rf->df", spread_grad, context, preferred_element_type=f32)
    d_context = (
        jnp.dot(spread_grad, out_full, preferred_element_type=f32) * keep_rows
    ).astype(bf16)
    grad_trees = lax.map(
        attend_backward, trees + (by_trees(d_context), log_totals, allowed)
    )
    d_queries = flat_heads(rotate(pair_heads(from_trees(grad_trees[0])), cosine, -sine))
    d_keys = flat_heads(rotate(pair_heads(from_trees(grad_trees[1])), cosine, -sine))
    d_values = from_trees(grad_trees[2])
    d_linear = jnp.concatenate([d_queries, d_keys, d_values], axis=1).astype(bf16)
    d_normed1 = scatter_rows(
        jnp.einsum("rf,df->rd", d_linear, qkv_full, preferred_element_type=f32).astype(bf16)
    )
    qkv_term = jnp.einsum("rd,rf->df", spread1, d_linear, preferred_element_type=f32)
    attn_grads = return_columns(
        scatter_far(jnp.concatenate([qkv_term.astype(bf16), out_term.astype(bf16)], axis=1)), 4
    )
    qkv_grad = jnp.stack(attn_grads[:3], axis=1)
    out_grad = attn_grads[3]
    bias_local = jnp.sum(d_linear.astype(f32), axis=0).reshape(3, width)
    d_stream_norm, gain_one_grad, bias_one_grad = norm_back(
        d_normed1, norm_hat1, inv_std1, ln1_gain
    )
    tokens_grad = d_residual + d_stream_norm

    squares = jnp.stack(
        [
            jnp.sum(own_valid * stream_out * stream_out),
            jnp.sum(own_valid * attn_out * attn_out),
            jnp.sum(own_valid * mlp_out * mlp_out),
            jnp.sum(own_valid),
        ]
    )
    norm_terms = jnp.stack([gain_one_grad, bias_one_grad, gain_two_grad, bias_two_grad])
    bias_spread = lax.dynamic_update_slice(
        jnp.zeros((3, model_width), f32), bias_local, (0, tp_index * local_width + quarter * width)
    )
    norm_sums, bias_sums, square_sums = lax.psum((norm_terms, bias_spread, squares), ALL)
    stream_rms = jnp.sqrt(square_sums[:3] / (square_sums[3] * model_width))
    qkv_bias_grad = lax.dynamic_slice(bias_sums, (0, tp_index * local_width), (3, local_width))
    return (
        output,
        tokens_grad,
        norm_sums[0],
        norm_sums[1],
        qkv_grad,
        qkv_bias_grad,
        out_grad,
        norm_sums[2],
        norm_sums[3],
        gate_up_grad,
        down_grad,
        stream_rms,
    )


def solution(mesh):
    planes = mesh.shape["fsdp"] // 4
    grid = Mesh(mesh.devices.reshape(planes, 2, 2, mesh.shape["tp"]), ALL)
    fsdp = (FAR, MID, NEAR)
    return jax.shard_map(
        shards,
        mesh=grid,
        in_specs=(
            P(ALL, None),
            P(ALL, None),
            P(fsdp),
            P(fsdp, None),
            P(fsdp),
            P(),
            P(),
            P(fsdp, None, TP),
            P(None, TP),
            P(fsdp, TP),
            P(),
            P(),
            P(fsdp, None, TP),
            P(fsdp, TP),
        ),
        out_specs=(
            P(ALL, None),
            P(ALL, None),
            P(),
            P(),
            P(fsdp, None, TP),
            P(None, TP),
            P(fsdp, TP),
            P(),
            P(),
            P(fsdp, None, TP),
            P(fsdp, TP),
            P(),
        ),
        check_vma=False,
    )
```

time: 3040 us -> 952 us (0.31)
  waiting for transfers between devices: 2630 us -> 314 us
  local copies, waits for them, and re-layouts: 93.3 us -> 206 us
  other arithmetic: 48.7 us -> 113 us
  starting transfers between devices: 1.9 us -> 47.7 us
  blocking collectives: 52 us -> 91.6 us
  matrix products: 185 us -> 154 us
    reduce_scatter x8 -> x2, waiting for transfers between devices: 2030 us -> 0.02 us  [scatter_far(): return lax.psum_scatter(values, FAR, scatter_dimension=0, tiled=True)]
    all_gather x8 -> x2, waiting for transfers between devices: 595 us -> 51.8 us  [gather_far(): return lax.all_gather(values, FAR, axis=0, tiled=True)]
    ppermute x0 -> x48, waiting for transfers between devices: none -> 262 us  [swap(): return lax.ppermute(values, axis, [(0, 1), (1, 0)])]
    ppermute x0 -> x48, starting transfers between devices: none -> 47.6 us  [swap(): return lax.ppermute(values, axis, [(0, 1), (1, 0)])]
    unnamed x69 -> x195, local copies, waits for them, and re-layouts: 17.2 us -> 56.4 us
    unnamed x0 -> x1, blocking collectives: none -> 34.3 us
    dot_general x36 -> x24, matrix products: 169 us -> 138 us  [the longest x1 19.1 us: shards(): gate_up = jnp.dot(spread2, gate_up_full, preferred_element_type=f32)]
  transfers between devices with their start and end apart: 16 -> 52, of which waited for: 13 -> 32; matrix products, arithmetic and copies ran while one was open for 6% -> 42% of each run, Pallas kernels for 0% -> 0%
where the time goes in v1:
time: 952 us; the launch traced here: 944 us
  waiting for transfers between devices  314 us (33%)
  local copies, waits for them, and re-layouts  206 us (22%)
  matrix products  154 us (16%)
  other arithmetic  113 us (12%)
  blocking collectives  91.6 us (10%)
  starting transfers between devices  47.7 us (5%)
  between operations  16.8 us (2%)
    ppermute x48, waiting for transfers between devices, swap(): return lax.ppermute(values, axis, [(0, 1), (1, 0)])  262 us
    psum x1, blocking collectives, shards(): lax.psum((norm_terms, bias_spread, squares), ALL)  57.3 us
    unnamed x195, local copies, waits for them, and re-layouts  56.4 us
    all_gather x2, waiting for transfers between devices, gather_far(): return lax.all_gather(values, FAR, axis=0, tiled=True)  51.8 us
    ppermute x48, starting transfers between devices, swap(): return lax.ppermute(values, axis, [(0, 1), (1, 0)])  47.6 us
    unnamed x1, blocking collectives  34.3 us
    reshape x8, local copies, waits for them, and re-layouts, from_trees(): values.reshape(4, 2, rows, -1).transpose(1, 0, 2, 3).reshape(8 * rows, -1)  23.4 us
    convert_element_type x8, other arithmetic, add_low(): return (a.astype(f32) + b.astype(f32)).astype(bf16)  23 us
  transfers between devices with their start and end apart: 52, of which 32 were waited for; matrix products, arithmetic and copies ran while one was open for 42% of the time, Pallas kernels for 0%

profile of v1, /device:TPU:0, one launch (start us, length us, event | category | flops | bytes accessed | tf_op | source)
XLA Modules:
  0.0 943.8 jit_solution(2235984893534795494)
XLA Ops:
  40.3 10.9 %collective-permute-done.5 = bf16[128,2048]{0,1:T(8,128)(2,1)} collective-permute-done((bf16[128,2048]{0,1:T(8,128)(2,1)}, bf16[128,2048]{0,1:T(8,128)(2,1)}, u32[]{:S(2)}, u32[]{:S(2)}) %collective-permute-start.5) | collective-permute-done | bytes 524320 | tf_op jit(solution)/shard_map/ppermute | solution.py:23
  86.5 34.3 %all-reduce = s32[4148]{0:T(1024)S(1)} all-reduce(s32[4148]{0:T(1024)S(1)} %add_dynamic-update-slice_fusion), channel_id=2, replica_groups=mesh['far'=4,'mid'=2,'near'=2,'tp'=2] {'mid','near'}, use_global_device_ids=true, to_apply=%add | all-reduce | flops 4148 | bytes 33184
  130.7 22.2 %all-gather.4.cloned.1.call-done = bf16[2048,1024]{0,1:T(8,128)(2,1)} async-done(((bf16[512,1024]{0,1:T(8,128)(2,1)}), bf16[2048,1024]{0,1:T(8,128)(2,1)}) %all-gather.4.cloned.1.call-update) | async-done | bytes 4194320 | tf_op jit(solution)/shard_map/all_gather | solution.py:95
  152.9 10.1 %broadcast_add_fusion = f32[2048,768]{0,1:T(8,128)S(1)} fusion(f32[768]{0:T(1024)S(1)} %add.220, bf16[2048,2048]{1,0:T(8,128)(2,1)} %constant_dynamic-update-slice_fusion.9, bf16[2048,1024]{0,1:T(8,128)(2,1)} %all-gather.4.cloned.1.call-done), kind=kOutput, calls=%fused_computation.62 | convolution fusion | flops 6444023808 | bytes 17828864 | tf_op jit(solution)/shard_map/dot_general | solution.py:291
  193.6 23.3 %while.26 = (s32[]{:T(128)}, f32[4,512,256]{1,2,0:T(8,128)}, f32[4,4,512]{2,1,0:T(4,128)}, bf16[4,512,256]{1,2,0:T(8,128)(2,1)S(1)}, pred[4,512,512]{1,2,0:T(8,1...) while((s32[]{:T(128)}, f32[4,512,256]{1,2,0:T(8,128)}, ...), condition=%wide.region_8.9_spmd, body=%wide.region_5.8_spmd.sunk | while | flops 281016320 | bytes 17891440 | solution.py:298
  239.5 24.8 %collective-permute-done.18 = bf16[256,2112]{0,1:T(8,128)(2,1)S(1)} collective-permute-done((bf16[256,2112]{0,1:T(8,128)(2,1)S(1)}, bf16[256,2112]{0,1:T(8,128)(2,1)S(1)}, u32[]{:S(2)}, u32[]{:S(2)}) %collective-permute-start.18) | collective-permute-done | bytes 1081376 | tf_op jit(solution)/shard_map/ppermute | solution.py:23
  277.0 10.1 %collective-permute-done.8 = bf16[128,2048]{1,0:T(8,128)(2,1)S(1)} collective-permute-done((bf16[128,2048]{1,0:T(8,128)(2,1)S(1)}, bf16[128,2048]{1,0:T(8,128)(2,1)S(1)}, u32[]{:S(2)}, u32[]{:S(2)}) %collective-permute-start.8) | collective-permute-done | bytes 524320 | tf_op jit(solution)/shard_map/ppermute | solution.py:23
  291.6 19.5 %collective-permute-done.24 = bf16[256,2048]{1,0:T(8,128)(2,1)S(1)} collective-permute-done((bf16[256,2048]{1,0:T(8,128)(2,1)S(1)}, bf16[256,2048]{1,0:T(8,128)(2,1)S(1)}, u32[]{:S(2)}, u32[]{:S(2)}) %collective-permute-start.24) | collective-permute-done | bytes 1048608 | tf_op jit(solution)/shard_map/ppermute | solution.py:23
  313.4 18.7 %collective-permute-done.11 = bf16[256,2048]{1,0:T(8,128)(2,1)S(1)} collective-permute-done((bf16[256,2048]{1,0:T(8,128)(2,1)S(1)}, bf16[256,2048]{1,0:T(8,128)(2,1)S(1)}, u32[]{:S(2)}, u32[]{:S(2)}) %collective-permute-start.11) | collective-permute-done | bytes 1048608 | tf_op jit(solution)/shard_map/ppermute | solution.py:23
  346.2 19.5 %collective-permute-done.12 = bf16[256,2048]{1,0:T(8,128)(2,1)S(1)} collective-permute-done((bf16[256,2048]{1,0:T(8,128)(2,1)S(1)}, bf16[256,2048]{1,0:T(8,128)(2,1)S(1)}, u32[]{:S(2)}, u32[]{:S(2)}) %collective-permute-start.12) | collective-permute-done | bytes 1048608 | tf_op jit(solution)/shard_map/ppermute | solution.py:23
  389.6 29.6 %all-gather.6.cloned.1.call-done = bf16[2048,2112]{0,1:T(8,128)(2,1)} async-done(((bf16[512,2112]{0,1:T(8,128)(2,1)}), bf16[2048,2112]{0,1:T(8,128)(2,1)}) %all-gather.6.cloned.1.call-update) | async-done | bytes 8650768 | tf_op jit(solution)/shard_map/all_gather | solution.py:95
  419.1 19.1 %fusion.13 = f32[2048,1408]{0,1:T(8,128)} fusion(bf16[2048,2048]{1,0:T(8,128)(2,1)} %constant_dynamic-update-slice_fusion.36, bf16[2048,2112]{0,1:T(8,128)(2,1)} %all-gather.6.cloned.1.call-done), kind=kOutput, calls=%fused_computation.51 | convolution fusion | flops 11811160064 | bytes 25690112 | tf_op jit(solution)/shard_map/dot_general | solution.py:307
  438.3 13.6 %multiply_convert_fusion.2 = (bf16[2048,704]{0,1:T(8,128)(2,1)}, bf16[2048,704]{0,1:T(8,128)(2,1)}, bf16[2048,704]{0,1:T(8,128)(2,1)S(1)}) fusion(f32[2048,1408]{0,1:T(8,128)} %fusion.13, bf16[2048,2048]{1,0:T(8,128)(2,1)S(1)} %copy-done.47, bf16[2048,2112]{0,1:T(8,128)(2,1)} %all-gather.6.cloned.1.call-done), kind=kOutput, calls=%fused_computation.46 | convolution fusion | flops 5927206912 | bytes 31457280 | tf_op jit(solution)/shard_map/dot_general | solution.py:318
  451.9 10.1 %convolution_convert_fusion.3 = bf16[2048,2048]{1,0:T(8,128)(2,1)S(1)} fusion(bf16[2048,704]{0,1:T(8,128)(2,1)S(1)} %get-tuple-element.242, bf16[2048,2112]{0,1:T(8,128)(2,1)} %all-gather.6.cloned.1.call-done), kind=kOutput, calls=%fused_computation.41 | convolution fusion | flops 5909774336 | bytes 14155776 | tf_op jit(solution)/shard_map/rf,df->rd/dot_general | solution.py:313
  466.7 17.5 %convolution_convert_fusion.2 = bf16[2048,2048]{1,0:T(8,128)(2,1)S(1)} fusion(bf16[2048,2112]{0,1:T(8,128)(2,1)} %all-gather.6.cloned.1.call-done, bf16[2048,704]{0,1:T(8,128)(2,1)} %get-tuple-element.241, bf16[2048,704]{0,1:T(8,128)(2,1)} %get-tuple-element.240), kind=kOutput, calls=%fused_computation.40 | convolution fusion | flops 11826888704 | bytes 19922944 | tf_op jit(solution)/shard_map/rf,df->rd/dot_general | solution.py:323
  525.0 15.9 %collective-permute-done.23 = bf16[256,2048]{1,0:T(8,128)(2,1)} collective-permute-done((bf16[256,2048]{1,0:T(8,128)(2,1)}, bf16[256,2048]{1,0:T(8,128)(2,1)}, u32[]{:S(2)}, u32[]{:S(2)}) %collective-permute-start.23) | collective-permute-done | bytes 1048608 | tf_op jit(solution)/shard_map/ppermute | solution.py:23
  542.4 20.0 %collective-permute-done.33 = bf16[256,2048]{1,0:T(8,128)(2,1)} collective-permute-done((bf16[256,2048]{1,0:T(8,128)(2,1)}, bf16[256,2048]{1,0:T(8,128)(2,1)}, u32[]{:S(2)}, u32[]{:S(2)}) %collective-permute-start.33) | collective-permute-done | bytes 1048608 | tf_op jit(solution)/shard_map/ppermute | solution.py:23
  576.9 21.8 %collective-permute-done.34 = bf16[256,2048]{1,0:T(8,128)(2,1)S(1)} collective-permute-done((bf16[256,2048]{1,0:T(8,128)(2,1)S(1)}, bf16[256,2048]{1,0:T(8,128)(2,1)S(1)}, u32[]{:S(2)}, u32[]{:S(2)}) %collective-permute-start.34) | collective-permute-done | bytes 1048608 | tf_op jit(solution)/shard_map/ppermute | solution.py:23
  625.1 14.6 %convolution_convert_fusion = bf16[2048,1408]{0,1:T(8,128)(2,1)S(1)} fusion(bf16[2048,2048]{1,0:T(8,128)(2,1)} %constant_dynamic-update-slice_fusion.36, bf16[2048,704]{0,1:T(8,128)(2,1)S(1)} %copy-done.69, bf16[2048,704]{0,1:T(8,128)(2,1)S(1)} %copy-done.68), kind=kOutput, calls=%fused_computation.38 | convolution fusion | flops 11825577984 | bytes 19922944 | tf_op jit(solution)/shard_map/rd,rf->df/dot_general | solution.py:326
  659.1 53.6 %while.27 = (s32[]{:T(128)}, f32[4,512,256]{1,2,0:T(8,128)S(1)}, f32[4,512,256]{1,2,0:T(8,128)}, bf16[4,512,256]{2,1,0:T(8,128)(2,1)}, bf16[4,512,256]{1,2,0:T(8...) while((s32[]{:T(128)}, f32[4,512,256]{1,2,0:T(8,128)S(1)}, ...), condition=%wide.region_15.16_spmd, body=%wide.region_13.15_spmd.sunk | while | flops 687077376 | bytes 41214100 | solution.py:343
  780.8 11.8 %collective-permute-done.40 = bf16[128,2048]{1,0:T(8,128)(2,1)S(1)} collective-permute-done((bf16[128,2048]{1,0:T(8,128)(2,1)S(1)}, bf16[128,2048]{1,0:T(8,128)(2,1)S(1)}, u32[]{:S(2)}, u32[]{:S(2)}) %collective-permute-start.40) | collective-permute-done | bytes 524320 | tf_op jit(solution)/shard_map/ppermute | solution.py:23
  803.0 16.4 %collective-permute-done.43 = bf16[256,2048]{1,0:T(8,128)(2,1)S(1)} collective-permute-done((bf16[256,2048]{1,0:T(8,128)(2,1)}, bf16[256,2048]{1,0:T(8,128)(2,1)S(1)}, u32[]{:S(2)}, u32[]{:S(2)}) %collective-permute-start.43) | collective-permute-done | bytes 1048608 | tf_op jit(solution)/shard_map/ppermute | solution.py:23
  827.8 57.3 %all-reduce.1 = (f32[4,2048]{1,0:T(4,128)S(1)}, f32[3,2048]{1,0:T(4,128)S(1)}, f32[4]{0:T(128)S(1)}) all-reduce(f32[4,2048]{1,0:T(4,128)S(1)} %pad_maximum_fusion.24, f32[3,2048]{1,0:T(4,128)S(1)} %constant_dynamic-update-slice_fusion.68, ...), channel_id=1, replica_groups=mesh['far'=4,'mid'=2,'near'=2,'tp'=2] {'far','mid','near','tp'}, use_global_device_ids=true, to_apply=%region_22.23 | all-reduce | flops 14340 | bytes 114720 | tf_op jit(solution)/shard_map/psum | solution.py:377
  899.4 16.8 %collective-permute-done.47 = bf16[128,4224]{0,1:T(8,128)(2,1)} collective-permute-done((bf16[128,4224]{0,1:T(8,128)(2,1)}, bf16[128,4224]{0,1:T(8,128)(2,1)}, u32[]{:S(2)}, u32[]{:S(2)}) %collective-permute-start.47) | collective-permute-done | bytes 1081376 | tf_op jit(solution)/shard_map/ppermute | solution.py:23
  (559 shorter events, 491.5 us)
Async XLA Ops:
  7.2 145.7 %all-gather.4.cloned.1.call-start = ((), (), s32[]{:S(2)}) async-start(), calls=%async_computation.2 | async-start | bytes 5242880 | tf_op jit(solution)/shard_map/all_gather | solution.py:95
  13.5 49.1 %collective-permute-start = (bf16[256,2048]{1,0:T(8,128)(2,1)}, bf16[256,2048]{1,0:T(8,128)(2,1)}, u32[]{:S(2)}, u32[]{:S(2)}) collective-permute-start(bf16[256,2048]{1,0:T(8,128)(2,1)} %get-tuple-element.231), channel_id=1, source_target_pairs={{0,2},{2,0},{1,3},{3,1},{4,6},{6,4},{5,7},{7,5},{8,10},{10,8},{9,1... | collective-permute-start | bytes 3145736 | tf_op jit(solution)/shard_map/ppermute | solution.py:23
  16.5 48.3 %collective-permute-start.1 = (bf16[256,2048]{1,0:T(8,128)(2,1)}, bf16[256,2048]{1,0:T(8,128)(2,1)}, u32[]{:S(2)}, u32[]{:S(2)}) collective-permute-start(bf16[256,2048]{1,0:T(8,128)(2,1)} %get-tuple-element.231), channel_id=1, source_target_pairs={{0,4},{4,0},{1,5},{5,1},{2,6},{6,2},{3,7},{7,3},{8,12},{12,8},{9,1... | collective-permute-start | bytes 3145736 | tf_op jit(solution)/shard_map/ppermute | solution.py:23
  22.7 28.4 %collective-permute-start.5 = (bf16[128,2048]{0,1:T(8,128)(2,1)}, bf16[128,2048]{0,1:T(8,128)(2,1)}, u32[]{:S(2)}, u32[]{:S(2)}) collective-permute-start(bf16[128,2048]{0,1:T(8,128)(2,1)} %broadcast_select_fusion.22), channel_id=1, source_target_pairs={{0,2},{2,0},{1,3},{3,1},{4,6},{6,4},{5,7},{7,5},{8,10},{10,8},{9,1... | collective-permute-start | bytes 1572872 | tf_op jit(solution)/shard_map/ppermute | solution.py:23
  70.8 348.3 %all-gather.6.cloned.1.call-start = ((), (), s32[]{:S(2)}) async-start(), calls=%async_computation.3 | async-start | bytes 10813440 | tf_op jit(solution)/shard_map/all_gather | solution.py:95
  82.5 43.3 %collective-permute-start.4 = (bf16[1024,2048]{1,0:T(8,128)(2,1)}, bf16[1024,2048]{1,0:T(8,128)(2,1)}, u32[]{:S(2)}, u32[]{:S(2)}) collective-permute-start(bf16[1024,2048]{1,0:T(8,128)(2,1)} %get-tuple-element.369), channel_id=1, source_target_pairs={{0,1},{1,0},{2,3},{3,2},{4,5},{5,4},{6,7},{7,6},{8,9},{9,8},{10,11... | collective-permute-start | bytes 12582920 | tf_op jit(solution)/shard_map/ppermute | solution.py:23
  83.6 152.5 %collective-permute-start.17 = (bf16[128,4224]{0,1:T(8,128)(2,1)}, bf16[128,4224]{0,1:T(8,128)(2,1)}, u32[]{:S(2)}, u32[]{:S(2)}) collective-permute-start(bf16[128,4224]{0,1:T(8,128)(2,1)} %broadcast_select_fusion.6), channel_id=1, source_target_pairs={{0,2},{2,0},{1,3},{3,1},{4,6},{6,4},{5,7},{7,5},{8,10},{10,8},{9,1... | collective-permute-start | bytes 3244040 | tf_op jit(solution)/shard_map/ppermute | solution.py:23
  236.2 30.4 %collective-permute-start.7 = (bf16[1024,2048]{1,0:T(8,128)(2,1)}, bf16[1024,2048]{1,0:T(8,128)(2,1)}, u32[]{:S(2)}, u32[]{:S(2)}) collective-permute-start(bf16[1024,2048]{1,0:T(8,128)(2,1)} %slice.664), channel_id=1, source_target_pairs={{0,1},{1,0},{2,3},{3,2},{4,5},{5,4},{6,7},{7,6},{8,9},{9,8},{10,11... | collective-permute-start | bytes 12582920 | tf_op jit(solution)/shard_map/ppermute | solution.py:23
  266.5 557.5 %reduce-scatter.5.cloned.1.call-start = ((), (), s32[]{:S(2)}) async-start(), calls=%async_computation.5 | async-start | bytes 10813440 | tf_op jit(solution)/shard_map/reduce_scatter | solution.py:99
  275.3 35.9 %collective-permute-start.24 = (bf16[256,2048]{1,0:T(8,128)(2,1)S(1)}, bf16[256,2048]{1,0:T(8,128)(2,1)S(1)}, u32[]{:S(2)}, u32[]{:S(2)}) collective-permute-start(bf16[256,2048]{1,0:T(8,128)(2,1)S(1)} %copy-done.34), channel_id=1, source_target_pairs={{0,2},{2,0},{1,3},{3,1},{4,6},{6,4},{5,7},{7,5},{8,10},{10,8},{9,1... | collective-permute-start | bytes 3145736 | tf_op jit(solution)/shard_map/ppermute | solution.py:23
  275.8 36.0 %collective-permute-start.25 = (bf16[256,2048]{1,0:T(8,128)(2,1)S(1)}, bf16[256,2048]{1,0:T(8,128)(2,1)S(1)}, u32[]{:S(2)}, u32[]{:S(2)}) collective-permute-start(bf16[256,2048]{1,0:T(8,128)(2,1)S(1)} %copy-done.34), channel_id=1, source_target_pairs={{0,4},{4,0},{1,5},{5,1},{2,6},{6,2},{3,7},{7,3},{8,12},{12,8},{9,1... | collective-permute-start | bytes 3145736 | tf_op jit(solution)/shard_map/ppermute | solution.py:23
  289.2 42.9 %collective-permute-start.11 = (bf16[256,2048]{1,0:T(8,128)(2,1)S(1)}, bf16[256,2048]{1,0:T(8,128)(2,1)S(1)}, u32[]{:S(2)}, u32[]{:S(2)}) collective-permute-start(bf16[256,2048]{1,0:T(8,128)(2,1)S(1)} %pad_maximum_fusion.13), channel_id=1, source_target_pairs={{0,4},{4,0},{1,5},{5,1},{2,6},{6,2},{3,7},{7,3},{8,12},{12,8},{9,1... | collective-permute-start | bytes 3145736 | tf_op jit(solution)/shard_map/ppermute | solution.py:23
  289.9 43.7 %collective-permute-start.9 = (bf16[256,2048]{1,0:T(8,128)(2,1)S(1)}, bf16[256,2048]{1,0:T(8,128)(2,1)S(1)}, u32[]{:S(2)}, u32[]{:S(2)}) collective-permute-start(bf16[256,2048]{1,0:T(8,128)(2,1)S(1)} %pad_maximum_fusion.12), channel_id=1, source_target_pairs={{0,2},{2,0},{1,3},{3,1},{4,6},{6,4},{5,7},{7,5},{8,10},{10,8},{9,1... | collective-permute-start | bytes 3145736 | tf_op jit(solution)/shard_map/ppermute | solution.py:23
  311.2 32.1 %collective-permute-start.26 = (bf16[128,2048]{1,0:T(8,128)(2,1)S(1)}, bf16[128,2048]{1,0:T(8,128)(2,1)S(1)}, u32[]{:S(2)}, u32[]{:S(2)}) collective-permute-start(bf16[128,2048]{1,0:T(8,128)(2,1)S(1)} %slice.697), channel_id=1, source_target_pairs={{0,4},{4,0},{1,5},{5,1},{2,6},{6,2},{3,7},{7,3},{8,12},{12,8},{9,1... | collective-permute-start | bytes 1572872 | tf_op jit(solution)/shard_map/ppermute | solution.py:23
  311.9 33.0 %collective-permute-start.27 = (bf16[128,2048]{1,0:T(8,128)(2,1)S(1)}, bf16[128,2048]{1,0:T(8,128)(2,1)S(1)}, u32[]{:S(2)}, u32[]{:S(2)}) collective-permute-start(bf16[128,2048]{1,0:T(8,128)(2,1)S(1)} %slice.698), channel_id=1, source_target_pairs={{0,2},{2,0},{1,3},{3,1},{4,6},{6,4},{5,7},{7,5},{8,10},{10,8},{9,1... | collective-permute-start | bytes 1572872 | tf_op jit(solution)/shard_map/ppermute | solution.py:23
  335.5 30.2 %collective-permute-start.12 = (bf16[256,2048]{1,0:T(8,128)(2,1)S(1)}, bf16[256,2048]{1,0:T(8,128)(2,1)S(1)}, u32[]{:S(2)}, u32[]{:S(2)}) collective-permute-start(bf16[256,2048]{1,0:T(8,128)(2,1)S(1)} %get-tuple-element.225), channel_id=1, source_target_pairs={{0,2},{2,0},{1,3},{3,1},{4,6},{6,4},{5,7},{7,5},{8,10},{10,8},{9,1... | collective-permute-start | bytes 3145736 | tf_op jit(solution)/shard_map/ppermute | solution.py:23
  337.0 29.4 %collective-permute-start.13 = (bf16[256,2048]{1,0:T(8,128)(2,1)S(1)}, bf16[256,2048]{1,0:T(8,128)(2,1)S(1)}, u32[]{:S(2)}, u32[]{:S(2)}) collective-permute-start(bf16[256,2048]{1,0:T(8,128)(2,1)S(1)} %get-tuple-element.225), channel_id=1, source_target_pairs={{0,4},{4,0},{1,5},{5,1},{2,6},{6,2},{3,7},{7,3},{8,12},{12,8},{9,1... | collective-permute-start | bytes 3145736 | tf_op jit(solution)/shard_map/ppermute | solution.py:23
  344.9 35.1 %collective-permute-start.28 = (bf16[1024,2048]{1,0:T(8,128)(2,1)S(1)}, bf16[1024,2048]{1,0:T(8,128)(2,1)S(1)}, u32[]{:S(2)}, u32[]{:S(2)}) collective-permute-start(bf16[1024,2048]{1,0:T(8,128)(2,1)S(1)} %get-tuple-element.361), channel_id=1, source_target_pairs={{0,1},{1,0},{2,3},{3,2},{4,5},{5,4},{6,7},{7,6},{8,9},{9,8},{10,11... | collective-permute-start | bytes 12582920 | tf_op jit(solution)/shard_map/ppermute | solution.py:23
  511.3 29.6 %collective-permute-start.23 = (bf16[256,2048]{1,0:T(8,128)(2,1)}, bf16[256,2048]{1,0:T(8,128)(2,1)}, u32[]{:S(2)}, u32[]{:S(2)}) collective-permute-start(bf16[256,2048]{1,0:T(8,128)(2,1)} %pad_maximum_fusion.15), channel_id=1, source_target_pairs={{0,4},{4,0},{1,5},{5,1},{2,6},{6,2},{3,7},{7,3},{8,12},{12,8},{9,1... | collective-permute-start | bytes 3145736 | tf_op jit(solution)/shard_map/ppermute | solution.py:23
  512.9 29.5 %collective-permute-start.21 = (bf16[256,2048]{1,0:T(8,128)(2,1)}, bf16[256,2048]{1,0:T(8,128)(2,1)}, u32[]{:S(2)}, u32[]{:S(2)}) collective-permute-start(bf16[256,2048]{1,0:T(8,128)(2,1)} %pad_maximum_fusion.14), channel_id=1, source_target_pairs={{0,2},{2,0},{1,3},{3,1},{4,6},{6,4},{5,7},{7,5},{8,10},{10,8},{9,1... | collective-permute-start | bytes 3145736 | tf_op jit(solution)/shard_map/ppermute | solution.py:23
  521.3 41.2 %collective-permute-start.33 = (bf16[256,2048]{1,0:T(8,128)(2,1)}, bf16[256,2048]{1,0:T(8,128)(2,1)}, u32[]{:S(2)}, u32[]{:S(2)}) collective-permute-start(bf16[256,2048]{1,0:T(8,128)(2,1)} %pad_maximum_fusion.17), channel_id=1, source_target_pairs={{0,4},{4,0},{1,5},{5,1},{2,6},{6,2},{3,7},{7,3},{8,12},{12,8},{9,1... | collective-permute-start | bytes 3145736 | tf_op jit(solution)/shard_map/ppermute | solution.py:23
  522.9 40.8 %collective-permute-start.31 = (bf16[256,2048]{1,0:T(8,128)(2,1)}, bf16[256,2048]{1,0:T(8,128)(2,1)}, u32[]{:S(2)}, u32[]{:S(2)}) collective-permute-start(bf16[256,2048]{1,0:T(8,128)(2,1)} %pad_maximum_fusion.16), channel_id=1, source_target_pairs={{0,2},{2,0},{1,3},{3,1},{4,6},{6,4},{5,7},{7,5},{8,10},{10,8},{9,1... | collective-permute-start | bytes 3145736 | tf_op jit(solution)/shard_map/ppermute | solution.py:23
  643.9 253.6 %reduce-scatter.3.cloned.1.call-start = ((), (), s32[]{:S(2)}) async-start(), calls=%async_computation.4 | async-start | bytes 5242880 | tf_op jit(solution)/shard_map/reduce_scatter | solution.py:99
  826.6 61.0 %collective-permute-start.46 = (bf16[256,2112]{0,1:T(8,128)(2,1)}, bf16[256,2112]{0,1:T(8,128)(2,1)}, u32[]{:S(2)}, u32[]{:S(2)}) collective-permute-start(bf16[256,2112]{0,1:T(8,128)(2,1)} %broadcast_select_fusion.10), channel_id=1, source_target_pairs={{0,4},{4,0},{1,5},{5,1},{2,6},{6,2},{3,7},{7,3},{8,12},{12,8},{9,1... | collective-permute-start | bytes 3244040 | tf_op jit(solution)/shard_map/ppermute | solution.py:23
  (100 other events, 1493.2 us)
Sparse Core Ops, SparseCore 0:
  71.0 81.9 all-gather.3
  266.6 152.4 all-gather.5
  644.0 145.7 reduce-scatter.4
  791.9 78.2 reduce-scatter.2

commit v2 on v1

v2 whole, which is shorter than its diff:
```python
from functools import partial
import math

import jax
import jax.numpy as jnp
from jax import lax
from jax.experimental import pallas as pl
from jax.experimental.pallas import tpu as pltpu
from jax.sharding import Mesh, PartitionSpec as P

HD = 64
ROT = 16

epsilon = 1e-05
score_scale = 0.125
masked_fill = -1e30

FAR, MID, NEAR, TP = "far", "mid", "near", "tp"
ALL = (FAR, MID, NEAR, TP)
f32 = jnp.float32
bf16 = jnp.bfloat16
LIGHT = pl.CostEstimate(flops=0, bytes_accessed=0, transcendentals=0)


def swap(values, axis):
    return lax.ppermute(values, axis, [(0, 1), (1, 0)])


def place():
    return lax.axis_index(MID) * 2 + lax.axis_index(NEAR)


def swap_diagonal(values):
    return lax.ppermute(values, (MID, NEAR), [(0, 3), (1, 2), (2, 1), (3, 0)])


def after(values, *others):
    return lax.optimization_barrier((values,) + others)[0]


def crossed(pieces):
    other = lax.axis_index(NEAR) == 1
    p = [jnp.where(other, pieces[i ^ 1], pieces[i]) for i in range(4)]
    other = lax.axis_index(MID) == 1
    return [jnp.where(other, p[i ^ 2], p[i]) for i in range(4)]


def exchange(pieces):
    return [pieces[0], swap(pieces[1], NEAR), swap(pieces[2], MID), swap_diagonal(pieces[3])]


def place():
    return lax.axis_index(MID) * 2 + lax.axis_index(NEAR)


def quarter_parts(width):
    tiles, rest = divmod(width // 4, 128)
    return tiles - tiles // 2, tiles // 2, rest


def half_tile(values, odd):
    values = values.astype(f32)
    return jnp.where(odd, pltpu.roll(values, 64, 1), values)


def low_lanes(low, high):
    lane = lax.broadcasted_iota(jnp.int32, (1, 128), 1)
    return jnp.where(lane < 64, low, high)


def pack_heads_kernel(place_ref, stack_ref, last_ref, *piece_refs):
    width = last_ref.shape[1] // 4
    for i, piece_ref in enumerate(piece_refs):
        part = pl.ds(pl.multiple_of((place_ref[0] ^ i) * width, 128), width)
        for kind in range(4):
            piece_ref[:, kind * width : (kind + 1) * width] = (
                stack_ref[:, kind, part] if kind < 3 else last_ref[:, part]
            )


def unpack_heads_kernel(place_ref, *refs):
    piece_refs, stack_ref, last_ref = refs[:4], refs[4], refs[5]
    width = last_ref.shape[1] // 4
    for i, piece_ref in enumerate(piece_refs):
        part = pl.ds(pl.multiple_of((place_ref[0] ^ i) * width, 128), width)
        for kind in range(4):
            piece = piece_ref[:, kind * width : (kind + 1) * width].astype(f32)
            if kind < 3:
                stack_ref[:, kind, part] = piece
            else:
                last_ref[:, part] = piece


def unit_columns(width):
    first, second, rest = quarter_parts(width)
    return first * 128, second * 128, rest, 4 * 128 * (first + second)


def pack_units_kernel(place_ref, stack_ref, last_ref, *piece_refs):
    first, second, rest, rest_start = unit_columns(last_ref.shape[1])

    def read(kind, part):
        return stack_ref[:, kind, part] if kind < 2 else last_ref[:, part]

    for i in range(4):
        chip = place_ref[0] ^ i
        first_ref, second_ref = piece_refs[i], piece_refs[4 + i]
        part = pl.ds(pl.multiple_of(chip * first, 128), first)
        for kind in range(3):
            first_ref[:, kind * first : (kind + 1) * first] = read(kind, part)
        part = pl.ds(pl.multiple_of(4 * first + chip * second, 128), second)
        mixed = 2 * second
        down = mixed + (128 if rest else 0)
        for kind, start in enumerate((0, second, down)):
            second_ref[:, start : start + second] = read(kind, part)
        if rest:
            part = pl.ds(pl.multiple_of(rest_start + (chip // 2) * 128, 128), 128)
            gate, up, last = [half_tile(read(kind, part), chip % 2 == 1) for kind in range(3)]
            second_ref[:, mixed : mixed + 128] = low_lanes(gate, pltpu.roll(up, 64, 1)).astype(bf16)
            second_ref[:, down + second :] = low_lanes(last, 0.0).astype(bf16)


def unpack_units_kernel(place_ref, *refs):
    piece_refs, stack_ref, last_ref = refs[:8], refs[8], refs[9]
    first, second, rest, rest_start = unit_columns(last_ref.shape[1])

    def write(kind, part, values):
        if kind < 2:
            stack_ref[:, kind, part] = values
        else:
            last_ref[:, part] = values

    for i in range(4):
        chip = place_ref[0] ^ i
        first_ref, second_ref = piece_refs[i], piece_refs[4 + i]
        part = pl.ds(pl.multiple_of(chip * first, 128), first)
        for kind in range(3):
            write(kind, part, first_ref[:, kind * first : (kind + 1) * first].astype(f32))
        part = pl.ds(pl.multiple_of(4 * first + chip * second, 128), second)
        mixed = 2 * second
        down = mixed + (128 if rest else 0)
        for kind, start in enumerate((0, second, down)):
            write(kind, part, second_ref[:, start : start + second].astype(f32))
        if rest:
            part = pl.ds(pl.multiple_of(rest_start + (chip // 2) * 128, 128), 128)
            odd = chip % 2 == 1
            lane = lax.broadcasted_iota(jnp.int32, (1, 128), 1)
            mine = (lane >= 64) == odd
            both = second_ref[:, mixed : mixed + 128].astype(f32)
            turned = pltpu.roll(both, 64, 1)
            last = second_ref[:, down + second :].astype(f32)
            last = jnp.where(odd, pltpu.roll(last, 64, 1), last)
            for kind, values in enumerate(
                (jnp.where(odd, turned, both), jnp.where(odd, both, turned), last)
            ):
                held = stack_ref[:, kind, part] if kind < 2 else last_ref[:, part]
                write(kind, part, jnp.where(mine, values, held))


def on_place(kernel, name, operands, outs):
    vmem = pl.BlockSpec(memory_space=pltpu.VMEM)
    return pl.pallas_call(
        kernel,
        in_specs=[pl.BlockSpec(memory_space=pltpu.SMEM)] + [vmem] * len(operands),
        out_specs=[vmem] * len(outs),
        out_shape=[jax.ShapeDtypeStruct(*out) for out in outs],
        compiler_params=pltpu.CompilerParams(vmem_limit_bytes=32 << 20),
        cost_estimate=LIGHT,
        name=name,
    )(place().reshape(1), *operands)


def collected(pieces):
    return jnp.concatenate(crossed(pieces), axis=0)


def spread(pieces):
    return collected(exchange(pieces))


def returned(values):
    rows = values.shape[0] // 4
    return exchange(
        [lax.dynamic_slice_in_dim(values, (place() ^ i) * rows, rows, 0) for i in range(4)]
    )


def gather_begin(own):
    return own, swap(own, NEAR), swap(own, MID)


def gather_end(state):
    own, near, mid = state
    half = own.shape[0] // 2
    diagonal_low = swap(near[:half], MID)
    diagonal_high = swap(mid[half:], NEAR)
    core = jnp.concatenate([own, near, mid, diagonal_low, diagonal_high], axis=0)
    return core, swap(core, TP)


def gather_rows(own):
    return gather_end(gather_begin(own))


def add_low(a, b):
    return (a.astype(f32) + b.astype(f32)).astype(bf16)


def scatter_begin(mine, others):
    return add_low(mine, swap(others, TP))


def scatter_middle(core):
    rows = core.shape[0] // 4
    half = rows // 2
    return swap(core[3 * rows : 3 * rows + half], MID), swap(core[3 * rows + half :], NEAR)


def scatter_end(core, middle):
    rows = core.shape[0] // 4
    half = rows // 2
    own, near, mid = [core[i * rows : (i + 1) * rows] for i in range(3)]
    near = jnp.concatenate([add_low(near[:half], middle[0]), near[half:]], axis=0)
    mid = jnp.concatenate([mid[:half], add_low(mid[half:], middle[1])], axis=0)
    return own, swap(near, NEAR), swap(mid, MID)


def scatter_rest(core):
    return scatter_end(core, scatter_middle(core))


def stage(always, step, *operands):
    shapes = jax.eval_shape(step, *operands)

    def never(*_):
        return jax.tree.map(lambda s: jnp.zeros(s.shape, s.dtype), shapes)

    return lax.cond(always, step, never, *operands)


def gather_far(values):
    return lax.all_gather(values, FAR, axis=0, tiled=True)


def scatter_far(values):
    return lax.psum_scatter(values, FAR, scatter_dimension=0, tiled=True)


def plane_trees(values):
    return jnp.stack(exchange([values] * 4))


def sum_over(values, axes):
    for axis in axes:
        size = lax.axis_size(axis)
        if size & (size - 1):
            values = lax.psum(values, axis)
            continue
        step = 1
        while step < size:
            values = values + lax.ppermute(values, axis, [(i, i ^ step) for i in range(size)])
            step *= 2
    return values


def tree_rows(seg_ids, parents, valid_mask, row_ids):
    labels = jnp.arange(parents.shape[0], dtype=jnp.int32)
    parent_one = jnp.sum(
        jnp.where(seg_ids[:, None] == labels[None, :], parents[None, :], 0), axis=1
    )
    parent_two = jnp.sum(
        jnp.where(parent_one[:, None] == labels[None, :], parents[None, :], 0), axis=1
    )
    key_segs = seg_ids[None, :]
    related = (
        (key_segs == seg_ids[:, None])
        | (key_segs == parent_one[:, None])
        | (key_segs == parent_two[:, None])
    )
    allowed = related & (row_ids[None, :] <= row_ids[:, None]) & (valid_mask[None, :] > 0)
    allowed = allowed | (row_ids[None, :] == row_ids[:, None])
    positions = jnp.sum(allowed.astype(jnp.int32), axis=1) - 1
    return (parent_one, parent_two, positions)


def normalised(values):
    centre = values - jnp.mean(values, axis=-1, keepdims=True)
    inverse = lax.rsqrt(jnp.mean(centre * centre, axis=-1, keepdims=True) + epsilon)
    return centre * inverse, inverse


def norm_kernel(*refs):
    row_ref, part_refs, gain_ref, shift_ref = refs[0], refs[1:-4], refs[-4], refs[-3]
    if len(refs) == 4:
        row_ref, gain_ref, shift_ref, normed_ref = refs
        part_refs = ()
    else:
        normed_ref, added_ref = refs[-2:]
    values = row_ref[...].astype(f32)
    if part_refs:
        added = sum(ref[...].astype(f32) for ref in part_refs)
        added_ref[...] = added
        values = values + added
    normed_ref[...] = (normalised(values)[0] * gain_ref[...] + shift_ref[...]).astype(bf16)


def norm_rows(tokens, parts, gain, shift):
    rows, width = tokens.shape
    block = min(64, rows)
    of_rows = pl.BlockSpec((block, width), lambda i: (i, 0))
    of_gain = pl.BlockSpec((1, width), lambda i: (0, 0))
    kinds = [bf16] + [f32] * bool(parts)
    return pl.pallas_call(
        norm_kernel,
        grid=(rows // block,),
        in_specs=[of_rows] * (1 + len(parts)) + [of_gain] * 2,
        out_specs=[of_rows] * len(kinds),
        out_shape=[jax.ShapeDtypeStruct((rows, width), kind) for kind in kinds],
        cost_estimate=LIGHT,
        name="norm_rows",
    )(tokens, *parts, gain[None], shift[None])


def norm_back_kernel(count, *refs):
    row_refs, part_refs = refs[:count], refs[count : count + 3]
    gain_ref, past_ref, grad_ref, low_ref, sum_ref = refs[count + 3 :]
    normed, inverse = normalised(sum(ref[...].astype(f32) for ref in row_refs))
    grad = sum(ref[...].astype(f32) for ref in part_refs)
    scaled = grad * gain_ref[...]
    centred = (
        scaled
        - jnp.mean(scaled, axis=-1, keepdims=True)
        - normed * jnp.mean(scaled * normed, axis=-1, keepdims=True)
    )
    total = past_ref[...].astype(f32) + inverse * centred
    grad_ref[...] = total
    low_ref[...] = total.astype(bf16)

    @pl.when(pl.program_id(0) == 0)
    def _():
        sum_ref[...] = jnp.zeros_like(sum_ref)

    sum_ref[0:1] += jnp.sum(grad * normed, axis=0, keepdims=True)
    sum_ref[1:2] += jnp.sum(grad, axis=0, keepdims=True)


def norm_back(summands, parts, gain, past):
    rows, width = past.shape
    block = min(64, rows)
    of_rows = pl.BlockSpec((block, width), lambda i: (i, 0))
    of_gain = pl.BlockSpec((1, width), lambda i: (0, 0))
    shape = jax.ShapeDtypeStruct
    return pl.pallas_call(
        partial(norm_back_kernel, len(summands)),
        grid=(rows // block,),
        in_specs=[of_rows] * (len(summands) + 3) + [of_gain, of_rows],
        out_specs=[of_rows, of_rows, pl.BlockSpec((2, width), lambda i: (0, 0))],
        out_shape=[shape((rows, width), f32), shape((rows, width), bf16), shape((2, width), f32)],
        cost_estimate=LIGHT,
        name="norm_back",
    )(*summands, *parts, gain[None], past)


def rope_tables(positions):
    half = ROT // 2
    lane = jnp.arange(2 * HD, dtype=jnp.int32) % HD
    power = (lane % half).astype(f32) * (-2.0 * math.log(10000.0) / ROT)
    inverse_freq = jnp.where(lane < ROT, jnp.exp(power), 0.0)
    angles = positions.astype(f32)[..., None] * inverse_freq
    return jnp.cos(angles), jnp.sin(angles)


def turn(values, cosine, sine):
    half = ROT // 2
    lane = lax.broadcasted_iota(jnp.int32, (1, 2 * HD), 1) % HD
    ahead = pltpu.roll(values, 2 * HD - half, 1)
    behind = pltpu.roll(values, half, 1)
    return values * cosine + jnp.where(lane < half, -ahead, behind) * sine


def allowed_keys(row_ref, col_ref):
    row_seg, parent_one, parent_two, row_id = [row_ref[0, i : i + 1, :] for i in range(4)]
    key_seg = col_ref[0, :, 0:1]
    key_id = col_ref[0, :, 1:2]
    related = (key_seg == row_seg) | (key_seg == parent_one) | (key_seg == parent_two)
    return (related & (key_id <= row_id)) | (key_id == row_id)


def dot_nt(a, b):
    return lax.dot_general(a, b, (((1,), (1,)), ((), ())), preferred_element_type=f32)


def dot_nn(a, b):
    return jnp.dot(a, b, preferred_element_type=f32)


def head_lanes(head):
    lane = lax.broadcasted_iota(jnp.int32, (1, 2 * HD), 1)
    return lane < HD if head == 0 else lane >= HD


def forward_kernel(
    core_ref, other_ref, weight_ref, bias_ref, row_ref, col_ref, keep_ref, cos_ref, sin_ref,
    qkv_ref, context_ref, log_ref, core_out_ref, other_out_ref, linear,
):
    half = core_ref.shape[0]
    width = context_ref.shape[3]
    linear[:half] = dot_nn(core_ref[...], weight_ref[:, : 3 * width]) + bias_ref[...]
    linear[half:] = dot_nn(other_ref[...], weight_ref[:, : 3 * width]) + bias_ref[...]
    mask = allowed_keys(row_ref, col_ref)
    cosine, sine = cos_ref[0], sin_ref[0]
    for pair in range(width // (2 * HD)):
        at = pair * 2 * HD
        lanes = slice(at, at + 2 * HD)
        query = turn(linear[:, lanes], cosine, sine).astype(bf16)
        key = turn(linear[:, width + at : width + at + 2 * HD], cosine, sine).astype(bf16)
        value = linear[:, 2 * width + at : 2 * width + at + 2 * HD]
        value_t = value.T.astype(bf16)
        value = value.astype(bf16)
        for core in range(2):
            rows = slice(core * half, (core + 1) * half)
            qkv_ref[core, 0, :, lanes] = query[rows]
            qkv_ref[core, 0, :, width + at : width + at + 2 * HD] = key[rows]
            qkv_ref[core, 0, :, 2 * width + at : 2 * width + at + 2 * HD] = value[rows]
        context_t = []
        for head in range(2):
            mine = jnp.where(head_lanes(head), query, jnp.zeros_like(query))
            scores = jnp.where(mask, dot_nt(key, mine) * score_scale, masked_fill)
            row_max = jnp.max(scores, axis=0, keepdims=True)
            exponent = jnp.exp(scores - row_max)
            row_sum = jnp.sum(exponent, axis=0, keepdims=True)
            log_ref[0, 2 * pair + head : 2 * pair + head + 1, :] = row_max + jnp.log(row_sum)
            context_t.append(
                dot_nn(value_t[head * HD : (head + 1) * HD], exponent.astype(bf16)) / row_sum
            )
        context = (jnp.concatenate(context_t, axis=0).T * keep_ref[0]).astype(bf16)
        for core in range(2):
            context_ref[core, 0, :, lanes] = context[core * half : (core + 1) * half]
    for core, out_ref in enumerate((core_out_ref, other_out_ref)):
        out_ref[...] = dot_nt(context_ref[core, 0], weight_ref[:, 3 * width :]).astype(bf16)


def backward_kernel(
    core_ref, other_ref, weight_ref, qkv_ref, row_ref, col_ref, keep_ref, cos_ref, sin_ref, log_ref,
    grad_ref, bias_ref, core_out_ref, other_out_ref, grads,
):
    half = core_ref.shape[0]
    width = weight_ref.shape[1] // 4
    grads[:half] = dot_nn(core_ref[...], weight_ref[:, 3 * width :])
    grads[half:] = dot_nn(other_ref[...], weight_ref[:, 3 * width :])
    mask = allowed_keys(row_ref, col_ref)
    cosine, sine = cos_ref[0], sin_ref[0]

    def both(at):
        return jnp.concatenate([qkv_ref[core, 0, :, at : at + 2 * HD] for core in range(2)], axis=0)

    for pair in range(width // (2 * HD)):
        at = pair * 2 * HD
        query, key, value = both(at), both(width + at), both(2 * width + at)
        key_t = key.astype(f32).T.astype(bf16)
        d_context = (grads[:, at : at + 2 * HD] * keep_ref[0]).astype(bf16)
        d_query_t = []
        d_key = jnp.zeros(query.shape, f32)
        d_value = jnp.zeros(query.shape, f32)
        for head in range(2):
            lanes = head_lanes(head)
            my_query = jnp.where(lanes, query, jnp.zeros_like(query))
            my_grad = jnp.where(lanes, d_context, jnp.zeros_like(d_context))
            log_total = log_ref[0, 2 * pair + head : 2 * pair + head + 1, :]
            scores = jnp.where(mask, dot_nt(key, my_query) * score_scale, masked_fill)
            probs = jnp.exp(scores - log_total)
            d_probs = dot_nt(value, my_grad)
            d_value = d_value + dot_nn(probs.astype(bf16), my_grad)
            inner = jnp.sum(probs * d_probs, axis=0, keepdims=True)
            d_scores = (probs * (d_probs - inner)).astype(bf16)
            d_key = d_key + dot_nn(d_scores, my_query)
            d_query_t.append(dot_nn(key_t[head * HD : (head + 1) * HD], d_scores))
        d_query = jnp.concatenate(d_query_t, axis=0).T * score_scale
        pieces = (
            turn(d_query, cosine, -sine).astype(bf16),
            turn(d_key * score_scale, cosine, -sine).astype(bf16),
            d_value.astype(bf16),
        )
        for kind, piece in enumerate(pieces):
            start = kind * width + at
            for core in range(2):
                grad_ref[core, 0, :, start : start + 2 * HD] = piece[core * half : (core + 1) * half]
            bias_ref[0, :, start : start + 2 * HD] = jnp.sum(
                piece.astype(f32), axis=0, keepdims=True
            )
    for core, out_ref in enumerate((core_out_ref, other_out_ref)):
        out_ref[...] = dot_nt(grad_ref[core, 0], weight_ref[:, : 3 * width]).astype(bf16)


def tree_block(*shape):
    return pl.BlockSpec((1,) + shape, lambda t: (t,) + (0,) * len(shape))


def row_block(rows, columns):
    return pl.BlockSpec((rows, columns), lambda t: (t, 0))


def core_block(rows, columns):
    return pl.BlockSpec((2, 1, rows, columns), lambda t: (0, t, 0, 0))


def whole_block(*shape):
    return pl.BlockSpec(shape, lambda t: (0,) * len(shape), pipeline_mode=pl.Buffered(1))


def attention_forward(cores, weights, bias, tree_info):
    row_info, col_info, keep, cosine, sine = tree_info
    model_width = weights.shape[0]
    width = weights.shape[1] // 4
    rows = cores[0].shape[0] // 4
    group = 2 * rows
    heads = width // HD
    shape = jax.ShapeDtypeStruct
    return pl.pallas_call(
        forward_kernel,
        grid=(4,),
        in_specs=[
            row_block(rows, model_width),
            row_block(rows, model_width),
            whole_block(*weights.shape),
            whole_block(1, 3 * width),
            tree_block(*row_info.shape[1:]),
            tree_block(*col_info.shape[1:]),
            tree_block(*keep.shape[1:]),
            tree_block(*cosine.shape[1:]),
            tree_block(*sine.shape[1:]),
        ],
        out_specs=[
            core_block(rows, 3 * width),
            core_block(rows, width),
            tree_block(heads, group),
            row_block(rows, model_width),
            row_block(rows, model_width),
        ],
        out_shape=[
            shape((2, 4, rows, 3 * width), bf16),
            shape((2, 4, rows, width), bf16),
            shape((4, heads, group), f32),
            shape((4 * rows, model_width), bf16),
            shape((4 * rows, model_width), bf16),
        ],
        scratch_shapes=[pltpu.VMEM((group, 3 * width), f32)],
        compiler_params=pltpu.CompilerParams(vmem_limit_bytes=48 << 20),
        cost_estimate=pl.CostEstimate(
            flops=16 * group * model_width * width * 2, bytes_accessed=32 << 20, transcendentals=4 << 20
        ),
        name="attention_forward",
    )(
        *cores,
        weights,
        bias,
        row_info,
        col_info,
        keep,
        cosine,
        sine,
    )


def attention_backward(cores, weights, qkv, log_totals, tree_info):
    row_info, col_info, keep, cosine, sine = tree_info
    model_width = weights.shape[0]
    width = weights.shape[1] // 4
    rows = cores[0].shape[0] // 4
    group = 2 * rows
    heads = width // HD
    shape = jax.ShapeDtypeStruct
    return pl.pallas_call(
        backward_kernel,
        grid=(4,),
        in_specs=[
            row_block(rows, model_width),
            row_block(rows, model_width),
            whole_block(*weights.shape),
            core_block(rows, 3 * width),
            tree_block(*row_info.shape[1:]),
            tree_block(*col_info.shape[1:]),
            tree_block(*keep.shape[1:]),
            tree_block(*cosine.shape[1:]),
            tree_block(*sine.shape[1:]),
            tree_block(heads, group),
        ],
        out_specs=[
            core_block(rows, 3 * width),
            tree_block(1, 3 * width),
            row_block(rows, model_width),
            row_block(rows, model_width),
        ],
        out_shape=[
            shape((2, 4, rows, 3 * width), bf16),
            shape((4, 1, 3 * width), f32),
            shape((4 * rows, model_width), bf16),
            shape((4 * rows, model_width), bf16),
        ],
        scratch_shapes=[pltpu.VMEM((group, width), f32)],
        compiler_params=pltpu.CompilerParams(vmem_limit_bytes=48 << 20),
        cost_estimate=pl.CostEstimate(
            flops=16 * group * model_width * width * 2, bytes_accessed=32 << 20, transcendentals=4 << 20
        ),
        name="attention_backward",
    )(
        *cores,
        weights,
        qkv,
        row_info,
        col_info,
        keep,
        cosine,
        sine,
        log_totals,
    )


def units_kernel(parts, *refs):
    main, mixed = parts
    count = 7 if len(refs) == 11 else 5
    x_refs, dy_refs, weight_ref = refs[0:2], refs[2:4], refs[4]
    before_refs = refs[5:count]
    grad_ref, hidden_ref = refs[count : count + 2]
    out_refs = refs[count + 2 :]
    wide = 2 * main + mixed
    for core in range(2):
        gate_up = dot_nn(x_refs[core][...], weight_ref[:, :wide])
        d_hidden = dot_nn(dy_refs[core][...], weight_ref[:, wide:])

        def unit(gate, up, grad):
            sigmoid = jax.nn.sigmoid(gate)
            active = gate * sigmoid
            d_gate = grad * up * sigmoid * (1.0 + gate * (1.0 - sigmoid))
            return active * up, d_gate, grad * active

        hidden, d_gate, d_up = unit(
            gate_up[:, :main], gate_up[:, main : 2 * main], d_hidden[:, :main]
        )
        hidden_ref[core, 0, :, :main] = hidden.astype(bf16)
        grad_ref[core, 0, :, :main] = d_gate.astype(bf16)
        grad_ref[core, 0, :, main : 2 * main] = d_up.astype(bf16)
        if mixed:
            both = gate_up[:, 2 * main :]
            hidden, d_gate, d_up = unit(both, pltpu.roll(both, 64, 1), d_hidden[:, main:])
            hidden_ref[core, 0, :, main:] = low_lanes(hidden, 0.0).astype(bf16)
            grad_ref[core, 0, :, 2 * main :] = low_lanes(d_gate, pltpu.roll(d_up, 64, 1)).astype(bf16)
        total = dot_nt(grad_ref[core, 0], weight_ref[:, :wide])
        if before_refs:
            total = total + before_refs[core][...].astype(f32)
        out_refs[core][...] = total.astype(bf16)


def hidden_units(xs, dys, weights, parts, before=()):
    model_width = weights.shape[0]
    main, mixed = parts
    wide = 2 * main + mixed
    rows = xs[0].shape[0] // 4
    shape = jax.ShapeDtypeStruct
    rows_of = row_block(rows, model_width)
    return pl.pallas_call(
        partial(units_kernel, parts),
        grid=(4,),
        in_specs=[rows_of] * 4 + [whole_block(*weights.shape)] + [rows_of] * len(before),
        out_specs=[core_block(rows, wide), core_block(rows, main + mixed), rows_of, rows_of],
        out_shape=[
            shape((2, 4, rows, wide), bf16),
            shape((2, 4, rows, main + mixed), bf16),
            shape((4 * rows, model_width), bf16),
            shape((4 * rows, model_width), bf16),
        ],
        compiler_params=pltpu.CompilerParams(vmem_limit_bytes=56 << 20),
        cost_estimate=pl.CostEstimate(
            flops=16 * rows * model_width * 5 * main, bytes_accessed=32 << 20, transcendentals=1 << 20
        ),
        name="hidden_units",
    )(*xs, *dys, weights, *before)


def dot_tn(a, b):
    return lax.dot_general(a, b, (((0,), (0,)), ((), ())), preferred_element_type=f32)


def weight_kernel(*refs):
    left_refs, right_refs, out_ref = (refs[0:2], refs[2:4]), refs[4:6], refs[6]
    start = 0
    for lefts, right_ref in zip(left_refs, right_refs):
        columns = right_ref.shape[-1]
        total = 0.0
        for core in range(2):
            total = total + dot_tn(lefts[core][...], right_ref[core].reshape(-1, columns))
        out_ref[:, start : start + columns] = total.astype(bf16)
        start += columns


def weight_terms(lefts, rights):
    rows, model_width = lefts[0][0].shape
    block = 256
    total = sum(right.shape[-1] for right in rights)
    left_block = pl.BlockSpec((rows, block), lambda i: (0, i))
    return pl.pallas_call(
        weight_kernel,
        grid=(model_width // block,),
        in_specs=[left_block] * 4 + [whole_block(*right.shape) for right in rights],
        out_specs=pl.BlockSpec((block, total), lambda i: (i, 0)),
        out_shape=jax.ShapeDtypeStruct((model_width, total), bf16),
        compiler_params=pltpu.CompilerParams(vmem_limit_bytes=48 << 20),
        cost_estimate=pl.CostEstimate(
            flops=4 * rows * model_width * total, bytes_accessed=32 << 20, transcendentals=0
        ),
        name="weight_terms",
    )(*lefts[0], *lefts[1], *rights)


def out_kernel(first_ref, second_ref, first_weight_ref, second_weight_ref, *out_refs):
    down = [first_ref.shape[-1], second_ref.shape[-1]]
    for core, out_ref in enumerate(out_refs):
        total = dot_nt(first_ref[core, 0], first_weight_ref[:, -down[0] :])
        total = total + dot_nt(second_ref[core, 0], second_weight_ref[:, -down[1] :])
        out_ref[...] = total.astype(bf16)


def units_out(hiddens, weights):
    rows = hiddens[0].shape[2]
    model_width = weights[0].shape[0]
    return pl.pallas_call(
        out_kernel,
        grid=(4,),
        in_specs=[core_block(rows, hidden.shape[-1]) for hidden in hiddens]
        + [whole_block(*weight.shape) for weight in weights],
        out_specs=[row_block(rows, model_width)] * 2,
        out_shape=[jax.ShapeDtypeStruct((4 * rows, model_width), bf16)] * 2,
        compiler_params=pltpu.CompilerParams(vmem_limit_bytes=48 << 20),
        cost_estimate=pl.CostEstimate(
            flops=16 * rows * model_width * sum(hidden.shape[-1] for hidden in hiddens),
            bytes_accessed=24 << 20,
            transcendentals=0,
        ),
        name="units_out",
    )(*hiddens, *weights)


def shards(
    tokens,
    cotangent,
    seg_ids,
    parents,
    valid_mask,
    ln1_gain,
    ln1_bias,
    w_qkv,
    qkv_bias,
    w_out,
    ln2_gain,
    ln2_bias,
    w_gate_up,
    w_down,
):
    own_rows, model_width = tokens.shape
    group_rows = seg_ids.shape[0]
    tp_index = lax.axis_index(TP)
    quarter = place()
    local_width = w_qkv.shape[2]
    width = local_width // 4
    weight_rows, local_units = w_down.shape
    main_a, main_b, rest, _ = unit_columns(local_units)
    mixed = 128 if rest else 0
    always = valid_mask[0] >= 0

    pieces = on_place(
        pack_heads_kernel, "pack_heads", (w_qkv, w_out), [((weight_rows, 4 * width), bf16)] * 4
    )
    attn_pieces = exchange(pieces)
    (normed1,) = norm_rows(tokens, (), ln1_gain, ln1_bias)
    unit_pieces = on_place(
        pack_units_kernel,
        "pack_units",
        (w_gate_up, w_down),
        [((weight_rows, 3 * main_a), bf16)] * 4
        + [((weight_rows, 3 * main_b + 2 * mixed), bf16)] * 4,
    )
    attn_pieces, normed1, unit_pieces = lax.optimization_barrier(
        (attn_pieces, normed1, unit_pieces)
    )
    attn_spread = collected(attn_pieces)
    attn_full = gather_far(attn_spread)

    def prepare(attn_spread, normed1, unit_pieces, cotangent, seg_ids, valid_mask, parents):
        spread1 = gather_rows(normed1)
        spread_a, spread_b = spread(unit_pieces[:4]), spread(unit_pieces[4:])
        cotangent, _, _ = lax.optimization_barrier((cotangent, spread1[0], spread_b))
        dy_state = gather_begin(cotangent)

        ints = jnp.concatenate([seg_ids, valid_mask, parents[0]])
        plane_ints = plane_trees(ints)

        def halves(values):
            parts = values.reshape(4, 2, own_rows)
            return jnp.where(tp_index == 0, parts, parts[:, ::-1]).reshape(4, group_rows)

        plane_segs = halves(plane_ints[:, :group_rows])
        plane_valid = halves(plane_ints[:, group_rows : 2 * group_rows])
        plane_parents = plane_ints[:, 2 * group_rows :]
        row_ids = (jnp.arange(group_rows, dtype=jnp.int32) + tp_index * own_rows) % group_rows
        parent_one, parent_two, positions = jax.vmap(tree_rows, in_axes=(0, 0, 0, None))(
            plane_segs, plane_parents, plane_valid, row_ids
        )
        all_ids = jnp.broadcast_to(row_ids, plane_segs.shape)
        row_info = jnp.stack([plane_segs, parent_one, parent_two, all_ids], axis=1)
        col_info = jnp.stack([jnp.where(plane_valid > 0, plane_segs, -1), all_ids], axis=2)
        keep = plane_valid.astype(f32)[..., None]
        tree_info = (row_info, col_info, keep, *rope_tables(positions))
        return spread1, spread_a, spread_b, dy_state[1:], tree_info

    spread1, spread_a, spread_b, dy_near, tree_info = stage(
        always, prepare, attn_spread, normed1, unit_pieces, cotangent, seg_ids, valid_mask, parents
    )
    own_valid = tree_info[2][0, :own_rows]
    units_a = gather_far(spread_a)
    units_b = gather_far(spread_b)

    def attend(spread1, attn_full, tree_info, tokens, cotangent, dy_near):
        own_bias = lax.dynamic_slice(qkv_bias, (0, quarter * width), (3, width))
        qkv, context, log_totals, *attn_partial = attention_forward(
            spread1, attn_full, own_bias.reshape(1, -1), tree_info
        )
        spread_dy = gather_end((cotangent, *dy_near))
        core = after(scatter_begin(*attn_partial), spread_dy[0])
        normed2, attn_out = norm_rows(tokens, scatter_rest(core), ln2_gain, ln2_bias)
        return qkv, context, log_totals, attn_out, gather_rows(normed2), spread_dy

    qkv, context, log_totals, attn_out, spread2, spread_dy = stage(
        always, attend, spread1, attn_full, tree_info, tokens, cotangent, dy_near
    )

    d_units_a, hidden_a, *d_normed2 = hidden_units(spread2, spread_dy, units_a, (main_a, 0))
    terms_a = weight_terms((spread2, spread_dy), (d_units_a, hidden_a))
    grads_a = scatter_far(terms_a)

    def finish_units(terms_a, spread2, spread_dy, units_a, units_b, d_normed2, hidden_a, attn_out, tokens, cotangent):
        d_units_b, hidden_b, *d_normed2 = hidden_units(
            spread2, spread_dy, units_b, (main_b, mixed), d_normed2
        )
        core = scatter_begin(*d_normed2)
        d_units_b, hidden_b, core = lax.optimization_barrier((d_units_b, hidden_b, core))
        middle = scatter_middle(core)
        mlp_partial = units_out((hidden_a, hidden_b), (units_a, units_b))
        middle, mlp_partial = lax.optimization_barrier((middle, mlp_partial))
        parts = scatter_end(core, middle)
        terms_b = weight_terms((spread2, spread_dy), (d_units_b, hidden_b))
        mlp_core = scatter_begin(*mlp_partial)
        parts, terms_b = lax.optimization_barrier((parts, terms_b))
        d_residual, d_low, norm2_grads = norm_back((tokens, attn_out), parts, ln2_gain, cotangent)
        return mlp_core, terms_b, d_residual, d_low, norm2_grads

    mlp_core, terms_b, d_residual, d_low, norm2_grads = stage(
        always, finish_units, terms_a, spread2, spread_dy, units_a, units_b, d_normed2, hidden_a, attn_out, tokens, cotangent
    )
    grads_a, d_low = lax.optimization_barrier((grads_a, d_low))
    grads_b = scatter_far(terms_b)

    def attend_back(terms_b, d_low, attn_full, qkv, log_totals, tree_info, spread1, context, mlp_core, grads_a):
        spread_grad = gather_rows(d_low)
        mlp_core, grads_a, spread_grad = lax.optimization_barrier((mlp_core, grads_a, spread_grad))
        mlp_middle = scatter_middle(mlp_core)
        pieces_a = returned(grads_a)
        d_linear, bias_terms, *d_normed1 = attention_backward(
            spread_grad, attn_full, qkv, log_totals, tree_info
        )
        mlp_middle, pieces_a, d_linear, d_normed1 = lax.optimization_barrier(
            (mlp_middle, pieces_a, d_linear, d_normed1)
        )
        mlp_parts = scatter_end(mlp_core, mlp_middle)
        core = scatter_begin(*d_normed1)
        terms = weight_terms((spread1, spread_grad), (d_linear, context))
        return terms, bias_terms, core, mlp_parts, pieces_a

    attn_terms, bias_terms, d_normed1_core, mlp_parts, pieces_a = stage(
        always, attend_back, terms_b, d_low, attn_full, qkv, log_totals, tree_info, spread1, context, mlp_core, grads_a
    )
    grads_b, d_normed1_core = lax.optimization_barrier((grads_b, d_normed1_core))
    attn_grads = scatter_far(attn_terms)

    def finish(attn_terms, core, mlp_parts, pieces_a, grads_b, d_residual, attn_out, tokens, bias_terms, norm2_grads, own_valid):
        tokens_grad, _, norm1_grads = norm_back(
            (tokens,), scatter_rest(core), ln1_gain, d_residual
        )
        mlp_out = sum(part.astype(f32) for part in mlp_parts)
        stream_out = tokens.astype(f32) + attn_out + mlp_out
        output = stream_out.astype(bf16)
        gate_up_grad, down_grad = on_place(
            unpack_units_kernel,
            "unpack_units",
            (*pieces_a, *returned(grads_b)),
            [(w_gate_up.shape, f32), (w_down.shape, f32)],
        )

        squares = jnp.stack(
            [
                jnp.sum(own_valid * stream_out * stream_out),
                jnp.sum(own_valid * attn_out * attn_out),
                jnp.sum(own_valid * mlp_out * mlp_out),
                jnp.sum(own_valid),
            ]
        )
        bias_spread = lax.dynamic_update_slice(
            jnp.zeros((3, model_width), f32),
            jnp.sum(bias_terms, axis=0).reshape(3, width),
            (0, tp_index * local_width + quarter * width),
        )
        sums = jnp.concatenate(
            [norm1_grads, norm2_grads, bias_spread, jnp.pad(squares, (0, model_width - 4))[None]]
        )
        return output, tokens_grad, gate_up_grad, down_grad, sums

    output, tokens_grad, gate_up_grad, down_grad, sums = stage(
        always, finish, attn_terms, d_normed1_core, mlp_parts, pieces_a, grads_b, d_residual, attn_out, tokens, bias_terms, norm2_grads, own_valid
    )
    sums = sum_over(sums, (TP, NEAR, MID))
    attn_grads, sums = lax.optimization_barrier((attn_grads, sums))
    sums = sum_over(sums, (FAR,))
    qkv_grad, out_grad = on_place(
        unpack_heads_kernel,
        "unpack_heads",
        returned(attn_grads),
        [(w_qkv.shape, f32), (w_out.shape, f32)],
    )
    norm_sums, bias_sums, square_sums = sums[:4], sums[4:7], sums[7]
    stream_rms = jnp.sqrt(square_sums[:3] / (square_sums[3] * model_width))
    qkv_bias_grad = lax.dynamic_slice(bias_sums, (0, tp_index * local_width), (3, local_width))
    return (
        output,
        tokens_grad,
        norm_sums[0],
        norm_sums[1],
        qkv_grad,
        qkv_bias_grad,
        out_grad,
        norm_sums[2],
        norm_sums[3],
        gate_up_grad,
        down_grad,
        stream_rms,
    )


def solution(mesh):
    planes = mesh.shape["fsdp"] // 4
    grid = Mesh(mesh.devices.reshape(planes, 2, 2, mesh.shape["tp"]), ALL)
    fsdp = (FAR, MID, NEAR)
    return jax.shard_map(
        shards,
        mesh=grid,
        in_specs=(
            P(ALL, None),
            P(ALL, None),
            P(fsdp),
            P(fsdp, None),
            P(fsdp),
            P(),
            P(),
            P(fsdp, None, TP),
            P(None, TP),
            P(fsdp, TP),
            P(),
            P(),
            P(fsdp, None, TP),
            P(fsdp, TP),
        ),
        out_specs=(
            P(ALL, None),
            P(ALL, None),
            P(),
            P(),
            P(fsdp, None, TP),
            P(None, TP),
            P(fsdp, TP),
            P(),
            P(),
            P(fsdp, None, TP),
            P(fsdp, TP),
            P(),
        ),
        check_vma=False,
    )
```

time: 952 us -> 646 us (0.68)
  Pallas kernels: 0 us -> 198 us
  matrix products: 154 us -> 0 us
  local copies, waits for them, and re-layouts: 206 us -> 65.3 us
  blocking collectives: 91.6 us -> 0 us
  waiting for transfers between devices: 314 us -> 241 us
  other arithmetic: 113 us -> 50.8 us
  starting transfers between devices: 47.7 us -> 64.7 us
    pallas_call x0 -> x16, Pallas kernels: none -> 198 us  [the longest x2 50.4 us: hidden_units(): pl.pallas_call(partial(units_kernel, parts), grid=(4,), in_specs=[rows_of...]
    dot_general x40 -> x0, matrix products: 154 us -> none  [the longest x1 19.1 us: shards(): gate_up = jnp.dot(spread2, gate_up_full, preferred_element_type=f32)]
    psum x1 -> x0, blocking collectives: 57.3 us -> none  [shards(): lax.psum((norm_terms, bias_spread, squares), ALL)]
    all_gather x2 -> x3, waiting for transfers between devices: 51.8 us -> 0.06 us  [gather_far(): return lax.all_gather(values, FAR, axis=0, tiled=True)]
    unnamed x195 -> x34, local copies, waits for them, and re-layouts: 56.4 us -> 13.8 us
    ppermute x48 -> x54, waiting for transfers between devices: 262 us -> 224 us  [swap(): return lax.ppermute(values, axis, [(0, 1), (1, 0)])]
    unnamed x1 -> x0, blocking collectives: 34.3 us -> none
    reshape x16 -> x2, local copies, waits for them, and re-layouts: 31.8 us -> 0.03 us  [the longest x1 0.02 us: prepare(): row_info = jnp.stack([plane_segs, parent_one, parent_two, all_ids], axis=1)]
  transfers between devices with their start and end apart: 52 -> 72, of which waited for: 32 -> 35; matrix products, arithmetic and copies ran while one was open for 42% -> 15% of each run, Pallas kernels for 0% -> 31%
where the time goes in v2:
time: 646 us; the launch traced here: 638 us
  waiting for transfers between devices  241 us (37%)
  Pallas kernels  198 us (31%)
  local copies, waits for them, and re-layouts  65.3 us (10%)
  starting transfers between devices  64.7 us (10%)
  other arithmetic  50.8 us (8%)
  between operations  15.9 us (2%)
    ppermute x54, waiting for transfers between devices, swap(): return lax.ppermute(values, axis, [(0, 1), (1, 0)])  224 us
    pallas_call x2, Pallas kernels, hidden_units(): pl.pallas_call(partial(units_kernel, parts), grid=(4,), in_specs=[rows_of...  50.4 us
    ppermute x54, starting transfers between devices, swap(): return lax.ppermute(values, axis, [(0, 1), (1, 0)])  48.2 us
    pallas_call x3, Pallas kernels, weight_terms(): pl.pallas_call(weight_kernel, grid=(model_width // block,), in_specs=[lef...  46.2 us
    pallas_call x1, Pallas kernels, attention_backward(): pl.pallas_call(backward_kernel, grid=(4,), in_specs=[row_block(rows, mode...  29.1 us
    pallas_call x1, Pallas kernels, attention_forward(): pl.pallas_call(forward_kernel, grid=(4,), in_specs=[row_block(rows, model...  27.7 us
    cond x76, local copies, waits for them, and re-layouts  26.6 us
    convert_element_type x8, other arithmetic, add_low(): return (a.astype(f32) + b.astype(f32)).astype(bf16)  22.5 us
  transfers between devices with their start and end apart: 72, of which 35 were waited for; matrix products, arithmetic and copies ran while one was open for 15% of the time, Pallas kernels for 31%

profile of v2, /device:TPU:0, one launch (start us, length us, event | category | flops | bytes accessed | tf_op | source)
XLA Modules:
  0.0 638.1 jit_solution(6074521192855258024)
XLA Ops:
  31.4 94.7 %conditional.5 = (bf16[1024,2048]{1,0:T(8,128)(2,1)}, bf16[1024,2048]{1,0:T(8,128)(2,1)}, bf16[512,1152]{1,0:T(8,128)(2,1)S(1)}, bf16[512,1024]{1,0:T(8,128)(2,1...) conditional(s32[]{:T(128)} %bitcast.14, () %tuple.61, ...), branch_computations={%region_0.1_spmd, %region_1.5_spmd} | conditional | flops 22639580 | bytes 69802856 | solution.py:238
  33.9 21.8 %collective-permute-done = bf16[256,2048]{1,0:T(8,128)(2,1)S(1)} collective-permute-done((bf16[256,2048]{1,0:T(8,128)(2,1)S(1)}, bf16[256,2048]{1,0:T(8,128)(2,1)S(1)}, u32[]{:S(2)}, u32[]{:S(2)}) %collective-permute-start) | collective-permute-done | bytes 1048608 | tf_op jit(solution)/shard_map/cond/branch_1_fun/ppermute | solution.py:26
  106.0 20.1 %collective-permute-done.11 = bf16[256,2048]{1,0:T(8,128)(2,1)} collective-permute-done((bf16[256,2048]{1,0:T(8,128)(2,1)S(1)}, bf16[256,2048]{1,0:T(8,128)(2,1)}, u32[]{:S(2)}, u32[]{:S(2)}) %collective-permute-start.11) | collective-permute-done | bytes 1048608 | tf_op jit(solution)/shard_map/cond/branch_1_fun/ppermute | solution.py:26
  128.0 140.2 %conditional.6 = (bf16[2,4,256,768]{3,2,1,0:T(8,128)(2,1)}, bf16[2,4,256,256]{3,2,1,0:T(8,128)(2,1)}, f32[4,4,512]{2,1,0:T(4,128)S(1)}, f32[256,2048]{1,0:T(8,12...) conditional(s32[]{:T(128)} %bitcast.14, () %tuple.60, ...), branch_computations={%region_5.6_spmd, %region_6.7_spmd} | conditional | flops 8604614656 | bytes 194179872 | solution.py:238
  130.1 27.7 %attention_forward.1 = (bf16[2,4,256,768]{3,2,1,0:T(8,128)(2,1)}, bf16[2,4,256,256]{3,2,1,0:T(8,128)(2,1)}, f32[4,4,512]{2,1,0:T(4,128)S(1)}, bf16[1024,2048]{1,0:T(8,128)(2,1)}, bf16[1024,2048]{1,0:T(8,128)(2,1)}) custom-call(bf16[1024,2048]{1,0:T(8,128)(2,1)} %get-tuple-element.167.core_ref, bf16[1024,2048]{1,0:T(8,128)(2,1)} %get-tuple-element.168.other_ref, ...), custom_call_target="tpu_custom_call" | custom-call | flops 8589934592 | bytes 33554432 | tf_op jit(solution)/shard_map/cond/branch_1_fun/attention_forward/pallas_call | solution.py:519
  180.9 11.4 %collective-permute-done.21 = bf16[128,2048]{1,0:T(8,128)(2,1)S(1)} collective-permute-done((bf16[128,2048]{1,0:T(8,128)(2,1)S(1)}, bf16[128,2048]{1,0:T(8,128)(2,1)S(1)}, u32[]{:S(2)}, u32[]{:S(2)}) %collective-permute-start.21) | collective-permute-done | bytes 524320 | tf_op jit(solution)/shard_map/cond/branch_1_fun/ppermute | solution.py:26
  196.4 21.3 %collective-permute-done.20.refs_2_ = bf16[256,2048]{1,0:T(8,128)(2,1)S(1)} collective-permute-done((bf16[256,2048]{1,0:T(8,128)(2,1)S(1)}, bf16[256,2048]{1,0:T(8,128)(2,1)S(1)}, u32[]{:S(2)}, u32[]{:S(2)}) %collective-permute-start.20) | collective-permute-done | bytes 1048608 | tf_op jit(solution)/shard_map/cond/branch_1_fun/ppermute | solution.py:26
  225.6 21.0 %collective-permute-done.23 = bf16[256,2048]{1,0:T(8,128)(2,1)S(1)} collective-permute-done((bf16[256,2048]{1,0:T(8,128)(2,1)}, bf16[256,2048]{1,0:T(8,128)(2,1)S(1)}, u32[]{:S(2)}, u32[]{:S(2)}) %collective-permute-start.23) | collective-permute-done | bytes 1048608 | tf_op jit(solution)/shard_map/cond/branch_1_fun/ppermute | solution.py:26
  260.5 7.5 %collective-permute-done.27 = bf16[1024,2048]{1,0:T(8,128)(2,1)} collective-permute-done((bf16[1024,2048]{1,0:T(8,128)(2,1)}, bf16[1024,2048]{1,0:T(8,128)(2,1)}, u32[]{:S(2)}, u32[]{:S(2)}) %collective-permute-start.27) | collective-permute-done | bytes 4194336 | tf_op jit(solution)/shard_map/cond/branch_1_fun/ppermute | solution.py:26
  268.2 24.5 %hidden_units.3 = (bf16[2,4,256,768]{3,2,1,0:T(8,128)(2,1)}, bf16[2,4,256,384]{3,2,1,0:T(8,128)(2,1)S(1)}, bf16[1024,2048]{1,0:T(8,128)(2,1)}, bf16[1024,2048]{1,0:T(8,128)(2,1)}) custom-call(bf16[1024,2048]{1,0:T(8,128)(2,1)} %get-tuple-element.400.refs_0_, bf16[1024,2048]{1,0:T(8,128)(2,1)} %get-tuple-element.401.refs_1_, ...), custom_call_target="tpu_custom_call" | custom-call | flops 16106127360 | bytes 33554432 | tf_op jit(solution)/shard_map/hidden_units/pallas_call | solution.py:661
  295.7 15.6 %weight_terms.5 = bf16[2048,1152]{1,0:T(8,128)(2,1)} custom-call(bf16[1024,2048]{1,0:T(8,128)(2,1)} %get-tuple-element.400.refs_0_, bf16[1024,2048]{1,0:T(8,128)(2,1)} %get-tuple-element.401.refs_1_, bf16[1024,2048]{1,0:T(8,128)(2,1)} %get-tuple-element.402.refs_2_, bf16[1024,2048]{1,0:T(8,128)(2,1)} %get-tuple-element.403.refs_3_, ...), custom_call_target="tpu_custom_call" | custom-call | flops 9663676416 | bytes 33554432 | tf_op jit(solution)/shard_map/weight_terms/pallas_call | solution.py:701
  312.0 98.4 %conditional.7 = (bf16[1024,2048]{1,0:T(8,128)(2,1)}, bf16[2048,1024]{1,0:T(8,128)(2,1)}, f32[256,2048]{1,0:T(8,128)S(1)}, bf16[256,2048]{1,0:T(8,128)(2,1)}, f32[2,2048]{1,0:T(2,128)}) conditional(s32[]{:T(128)} %bitcast.14, () %tuple.66, (bf16[1024,2048]{1,0:T(8,128)(2,1)}, bf16[1024,2048]{1,0:T(8,128)(2,1)}, bf16[1024,2048]{1,0:T(8,128)(2,1)}, ...), branch_computations={%region_7.8_spmd, %region_8.9_spmd} | conditional | flops 25792872448 | bytes 225444256 | solution.py:238
  312.0 25.9 %hidden_units.2 = (bf16[2,4,256,640]{3,2,1,0:T(8,128)(2,1)}, bf16[2,4,256,384]{3,2,1,0:T(8,128)(2,1)}, bf16[1024,2048]{1,0:T(8,128)(2,1)}, bf16[1024,2048]{1,0:T(8,128)(2,1)}) custom-call(bf16[1024,2048]{1,0:T(8,128)(2,1)} %get-tuple-element.191.refs_0_, bf16[1024,2048]{1,0:T(8,128)(2,1)} %get-tuple-element.192.refs_1_, ...), custom_call_target="tpu_custom_call" | custom-call | flops 10737418240 | bytes 33554432 | tf_op jit(solution)/shard_map/cond/branch_1_fun/hidden_units/pallas_call | solution.py:661
  338.0 7.2 %collective-permute-done.29 = bf16[1024,2048]{1,0:T(8,128)(2,1)S(1)} collective-permute-done((bf16[1024,2048]{1,0:T(8,128)(2,1)}, bf16[1024,2048]{1,0:T(8,128)(2,1)S(1)}, u32[]{:S(2)}, u32[]{:S(2)}) %collective-permute-start.29) | collective-permute-done | bytes 4194336 | tf_op jit(solution)/shard_map/cond/branch_1_fun/ppermute | solution.py:26
  352.5 14.4 %units_out.1 = (bf16[1024,2048]{1,0:T(8,128)(2,1)S(1)}, bf16[1024,2048]{1,0:T(8,128)(2,1)}) custom-call(bf16[2,4,256,384]{3,2,1,0:T(8,128)(2,1)S(1)} %copy-done.43, bf16[2,4,256,384]{3,2,1,0:T(8,128)(2,1)S(1)} %copy-done.5, bf16[2048,1152]{1,0:T(8,128)(2,1)} %get-tuple-element.205.first_weight_ref, ...), custom_call_target="tpu_custom_call" | custom-call | flops 6442450944 | bytes 25165824 | tf_op jit(solution)/shard_map/cond/branch_1_fun/units_out/pallas_call | solution.py:726
  372.5 15.6 %weight_terms.3 = bf16[2048,1024]{1,0:T(8,128)(2,1)} custom-call(bf16[1024,2048]{1,0:T(8,128)(2,1)} %get-tuple-element.191.refs_0_, bf16[1024,2048]{1,0:T(8,128)(2,1)} %get-tuple-element.192.refs_1_, bf16[1024,2048]{1,0:T(8,128)(2,1)} %get-tuple-element.193.refs_2_, bf16[1024,2048]{1,0:T(8,128)(2,1)} %get-tuple-element.194.refs_3_, ...), custom_call_target="tpu_custom_call" | custom-call | flops 8589934592 | bytes 33554432 | tf_op jit(solution)/shard_map/cond/branch_1_fun/weight_terms/pallas_call | solution.py:701
  402.3 7.8 %add_convert_fusion.4 = bf16[1024,2048]{1,0:T(8,128)(2,1)} fusion(bf16[1024,2048]{1,0:T(8,128)(2,1)} %collective-permute-done.32, bf16[1024,2048]{1,0:T(8,128)(2,1)} %copy-done), kind=kLoop, calls=%fused_computation.73 | loop fusion | flops 8388608 | bytes 12582912 | tf_op jit(solution)/shard_map/cond/branch_1_fun/convert_element_type | solution.py:206
  411.8 116.4 %conditional.8 = (bf16[2048,1024]{1,0:T(8,128)(2,1)}, f32[4,1,768]{2,1,0:T(1,128)S(1)}, bf16[1024,2048]{1,0:T(8,128)(2,1)}, bf16[256,2048]{1,0:T(8,128)(2,1)}, b...) conditional(s32[]{:T(128)} %bitcast.14, () %tuple.65, ...), branch_computations={%region_11.12_spmd, %region_12.13_spmd} | conditional | flops 17194549248 | bytes 207078512 | solution.py:238
  413.3 23.3 %collective-permute-done.35 = bf16[256,2048]{1,0:T(8,128)(2,1)S(1)} collective-permute-done((bf16[256,2048]{1,0:T(8,128)(2,1)}, bf16[256,2048]{1,0:T(8,128)(2,1)S(1)}, u32[]{:S(2)}, u32[]{:S(2)}) %collective-permute-start.35) | collective-permute-done | bytes 1048608 | tf_op jit(solution)/shard_map/cond/branch_1_fun/ppermute | solution.py:26
  468.2 29.1 %attention_backward.1 = (bf16[2,4,256,768]{3,2,1,0:T(8,128)(2,1)S(1)}, f32[4,1,768]{2,1,0:T(1,128)S(1)}, bf16[1024,2048]{1,0:T(8,128)(2,1)}, bf16[1024,2048]{1,0:T(8,128)(2,1)}) custom-call(bf16[1024,2048]{1,0:T(8,128)(2,1)} %constant_dynamic-update-slice_fusion.15.core_ref.refs_2_, bf16[1024,2048]{1,0:T(8,128)(2,1)} %collective-permute-done.39.other_ref.refs_3_, ...), custom_call_target="tpu_custom_call" | custom-call | flops 8589934592 | bytes 33554432 | tf_op jit(solution)/shard_map/cond/branch_1_fun/attention_backward/pallas_call | solution.py:573
  503.0 15.1 %weight_terms.4 = bf16[2048,1024]{1,0:T(8,128)(2,1)} custom-call(bf16[1024,2048]{1,0:T(8,128)(2,1)} %get-tuple-element.224.refs_0_, bf16[1024,2048]{1,0:T(8,128)(2,1)} %get-tuple-element.225.refs_1_, bf16[1024,2048]{1,0:T(8,128)(2,1)} %constant_dynamic-update-slice_fusion.15.core_ref.refs_2_, bf16[1024,2048]{1,0:T(8,128)(2,1)} %collective-permute-done.39.other_ref.refs_3_, ...), custom_call_target="tpu_custom_call" | custom-call | flops 8589934592 | bytes 33554432 | tf_op jit(solution)/shard_map/cond/branch_1_fun/weight_terms/pallas_call | solution.py:701
  528.2 67.5 %conditional.9 = (bf16[256,2048]{1,0:T(8,128)(2,1)}, f32[256,2048]{1,0:T(8,128)}, f32[128,2,2816]{2,1,0:T(2,128)}, f32[128,2816]{1,0:T(8,128)S(1)}, f32[8,2048]{1,0:T(8,128)S(1)}) conditional(s32[]{:T(128)} %bitcast.14, () %tuple.59, (bf16[256,2048]{1,0:T(8,128)(2,1)S(1)}, f32[256,2048]{1,0:T(8,128)}, bf16[256,2048]{1,0:T(8,128)(2,1)}, ...), branch_computations={%region_13.14_spmd, %region_14.20_spmd} | conditional | flops 15796765 | bytes 40567728 | solution.py:238
  532.4 12.2 %collective-permute-done.50 = bf16[128,2048]{1,0:T(8,128)(2,1)S(1)} collective-permute-done((bf16[128,2048]{1,0:T(8,128)(2,1)}, bf16[128,2048]{1,0:T(8,128)(2,1)S(1)}, u32[]{:S(2)}, u32[]{:S(2)}) %collective-permute-start.50) | collective-permute-done | bytes 524320 | tf_op jit(solution)/shard_map/cond/branch_1_fun/ppermute | solution.py:26
  566.8 13.1 %collective-permute-done.52.refs_5_ = bf16[128,1024]{1,0:T(8,128)(2,1)S(1)} collective-permute-done((bf16[128,1024]{1,0:T(8,128)(2,1)S(1)}, bf16[128,1024]{1,0:T(8,128)(2,1)S(1)}, u32[]{:S(2)}, u32[]{:S(2)}) %collective-permute-start.52) | collective-permute-done | bytes 262176 | tf_op jit(solution)/shard_map/cond/branch_1_fun/ppermute | solution.py:26
  (357 shorter events, 285.6 us)
Async XLA Ops:
  7.2 120.8 %all-gather.4.cloned.1.call-start = ((), (), s32[]{:S(2)}) async-start(), calls=%async_computation.3 | async-start | bytes 5242880 | tf_op jit(solution)/shard_map/all_gather | solution.py:242
  30.2 238.0 %all-gather.6.cloned.1.call-start = ((), (), s32[]{:S(2)}) async-start(), calls=%async_computation.4 | async-start | bytes 5898240 | tf_op jit(solution)/shard_map/all_gather | solution.py:242
  69.7 56.4 %collective-permute-start.4 = (bf16[1024,2048]{1,0:T(8,128)(2,1)}, bf16[1024,2048]{1,0:T(8,128)(2,1)}, u32[]{:S(2)}, u32[]{:S(2)}) collective-permute-start(bf16[1024,2048]{1,0:T(8,128)(2,1)} %constant_dynamic-update-slice_fusion), channel_id=1, source_target_pairs={{0,1},{1,0},{2,3},{3,2},{4,5},{5,4},{6,7},{7,6},{8,9},{9,8},{10,11... | collective-permute-start | bytes 12582920 | tf_op jit(solution)/shard_map/cond/branch_1_fun/ppermute | solution.py:26
  98.1 28.1 %collective-permute-start.11 = (bf16[256,2048]{1,0:T(8,128)(2,1)S(1)}, bf16[256,2048]{1,0:T(8,128)(2,1)}, u32[]{:S(2)}, u32[]{:S(2)}) collective-permute-start(bf16[256,2048]{1,0:T(8,128)(2,1)S(1)} %get-tuple-element.162), channel_id=1, source_target_pairs={{0,2},{2,0},{1,3},{3,1},{4,6},{6,4},{5,7},{7,5},{8,10},{10,8},{9,1... | collective-permute-start | bytes 3145736 | tf_op jit(solution)/shard_map/cond/branch_1_fun/ppermute | solution.py:26
  98.8 27.3 %collective-permute-start.12 = (bf16[256,2048]{1,0:T(8,128)(2,1)S(1)}, bf16[256,2048]{1,0:T(8,128)(2,1)}, u32[]{:S(2)}, u32[]{:S(2)}) collective-permute-start(bf16[256,2048]{1,0:T(8,128)(2,1)S(1)} %get-tuple-element.162), channel_id=1, source_target_pairs={{0,4},{4,0},{1,5},{5,1},{2,6},{6,2},{3,7},{7,3},{8,12},{12,8},{9,1... | collective-permute-start | bytes 3145736 | tf_op jit(solution)/shard_map/cond/branch_1_fun/ppermute | solution.py:26
  127.2 184.2 %all-gather.8.cloned.1.call-start = ((), (), s32[]{:S(2)}) async-start(), calls=%async_computation.6 | async-start | bytes 5242880 | tf_op jit(solution)/shard_map/all_gather | solution.py:242
  127.9 282.6 %reduce-scatter.4.cloned.1.call-start = ((), (), s32[]{:S(2)}) async-start(), calls=%async_computation.5 | async-start | bytes 5898240 | tf_op jit(solution)/shard_map/reduce_scatter | solution.py:246
  225.6 35.0 %collective-permute-start.28 = (bf16[1024,2048]{1,0:T(8,128)(2,1)}, bf16[1024,2048]{1,0:T(8,128)(2,1)}, u32[]{:S(2)}, u32[]{:S(2)}) collective-permute-start(bf16[1024,2048]{1,0:T(8,128)(2,1)} %constant_dynamic-update-slice_fusion.5), channel_id=1, source_target_pairs={{0,1},{1,0},{2,3},{3,2},{4,5},{5,4},{6,7},{7,6},{8,9},{9,8},{10,11... | collective-permute-start | bytes 12582920 | tf_op jit(solution)/shard_map/cond/branch_1_fun/ppermute | solution.py:26
  311.3 216.9 %reduce-scatter.6.cloned.1.call-start = ((), (), s32[]{:S(2)}) async-start(), calls=%async_computation.7 | async-start | bytes 5242880 | tf_op jit(solution)/shard_map/reduce_scatter | solution.py:246
  368.9 33.3 %collective-permute-start.32 = (bf16[1024,2048]{1,0:T(8,128)(2,1)}, bf16[1024,2048]{1,0:T(8,128)(2,1)}, u32[]{:S(2)}, u32[]{:S(2)}) collective-permute-start(bf16[1024,2048]{1,0:T(8,128)(2,1)} %get-tuple-element.209), channel_id=1, source_target_pairs={{0,1},{1,0},{2,3},{3,2},{4,5},{5,4},{6,7},{7,6},{8,9},{9,8},{10,11... | collective-permute-start | bytes 12582920 | tf_op jit(solution)/shard_map/cond/branch_1_fun/ppermute | solution.py:26
  369.5 25.6 %collective-permute-start.33 = (bf16[256,2048]{1,0:T(8,128)(2,1)S(1)}, bf16[256,2048]{1,0:T(8,128)(2,1)S(1)}, u32[]{:S(2)}, u32[]{:S(2)}) collective-permute-start(bf16[256,2048]{1,0:T(8,128)(2,1)S(1)} %pad_maximum_fusion.4), channel_id=1, source_target_pairs={{0,2},{2,0},{1,3},{3,1},{4,6},{6,4},{5,7},{7,5},{8,10},{10,8},{9,1... | collective-permute-start | bytes 3145736 | tf_op jit(solution)/shard_map/cond/branch_1_fun/ppermute | solution.py:26
  410.5 196.2 %reduce-scatter.8.cloned.1.call-start = ((), (), s32[]{:S(2)}) async-start(), calls=%async_computation.8 | async-start | bytes 5242880 | tf_op jit(solution)/shard_map/reduce_scatter | solution.py:246
  412.9 26.6 %collective-permute-start.36 = (bf16[256,2048]{1,0:T(8,128)(2,1)}, bf16[256,2048]{1,0:T(8,128)(2,1)S(1)}, u32[]{:S(2)}, u32[]{:S(2)}) collective-permute-start(bf16[256,2048]{1,0:T(8,128)(2,1)} %get-tuple-element.228), channel_id=1, source_target_pairs={{0,4},{4,0},{1,5},{5,1},{2,6},{6,2},{3,7},{7,3},{8,12},{12,8},{9,1... | collective-permute-start | bytes 3145736 | tf_op jit(solution)/shard_map/cond/branch_1_fun/ppermute | solution.py:26
  461.8 35.5 %collective-permute-start.40 = (bf16[128,2048]{1,0:T(8,128)(2,1)S(1)}, bf16[128,2048]{1,0:T(8,128)(2,1)S(1)}, u32[]{:S(2)}, u32[]{:S(2)}) collective-permute-start(bf16[128,2048]{1,0:T(8,128)(2,1)S(1)} %get-tuple-element.704), channel_id=1, source_target_pairs={{0,4},{4,0},{1,5},{5,1},{2,6},{6,2},{3,7},{7,3},{8,12},{12,8},{9,1... | collective-permute-start | bytes 1572872 | tf_op jit(solution)/shard_map/cond/branch_1_fun/ppermute | solution.py:26
  463.6 33.7 %collective-permute-start.41 = (bf16[128,2048]{1,0:T(8,128)(2,1)S(1)}, bf16[128,2048]{1,0:T(8,128)(2,1)S(1)}, u32[]{:S(2)}, u32[]{:S(2)}) collective-permute-start(bf16[128,2048]{1,0:T(8,128)(2,1)S(1)} %get-tuple-element.703), channel_id=1, source_target_pairs={{0,2},{2,0},{1,3},{3,1},{4,6},{6,4},{5,7},{7,5},{8,10},{10,8},{9,1... | collective-permute-start | bytes 1572872 | tf_op jit(solution)/shard_map/cond/branch_1_fun/ppermute | solution.py:26
  464.7 32.6 %collective-permute-start.42 = (bf16[128,1152]{1,0:T(8,128)(2,1)S(1)}, bf16[128,1152]{1,0:T(8,128)(2,1)}, u32[]{:S(2)}, u32[]{:S(2)}) collective-permute-start(bf16[128,1152]{1,0:T(8,128)(2,1)S(1)} %get-tuple-element.709), channel_id=1, source_target_pairs={{0,2},{2,0},{1,3},{3,1},{4,6},{6,4},{5,7},{7,5},{8,10},{10,8},{9,1... | collective-permute-start | bytes 884744 | tf_op jit(solution)/shard_map/cond/branch_1_fun/ppermute | solution.py:26
  465.8 31.5 %collective-permute-start.43 = (bf16[128,1152]{1,0:T(8,128)(2,1)S(1)}, bf16[128,1152]{1,0:T(8,128)(2,1)}, u32[]{:S(2)}, u32[]{:S(2)}) collective-permute-start(bf16[128,1152]{1,0:T(8,128)(2,1)S(1)} %get-tuple-element.708), channel_id=1, source_target_pairs={{0,4},{4,0},{1,5},{5,1},{2,6},{6,2},{3,7},{7,3},{8,12},{12,8},{9,1... | collective-permute-start | bytes 884744 | tf_op jit(solution)/shard_map/cond/branch_1_fun/ppermute | solution.py:26
  466.1 31.2 %collective-permute-start.44 = (bf16[128,1152]{1,0:T(8,128)(2,1)S(1)}, bf16[128,1152]{1,0:T(8,128)(2,1)}, u32[]{:S(2)}, u32[]{:S(2)}) collective-permute-start(bf16[128,1152]{1,0:T(8,128)(2,1)S(1)} %get-tuple-element.707), channel_id=1, source_target_pairs={{0,6},{2,4},{4,2},{6,0},{1,7},{3,5},{5,3},{7,1},{8,14},{10,12},{12... | collective-permute-start | bytes 884744 | tf_op jit(solution)/shard_map/cond/branch_1_fun/ppermute | solution.py:34
  501.4 25.7 %collective-permute-start.46 = (bf16[256,2048]{1,0:T(8,128)(2,1)S(1)}, bf16[256,2048]{1,0:T(8,128)(2,1)}, u32[]{:S(2)}, u32[]{:S(2)}) collective-permute-start(bf16[256,2048]{1,0:T(8,128)(2,1)S(1)} %pad_maximum_fusion.6), channel_id=1, source_target_pairs={{0,2},{2,0},{1,3},{3,1},{4,6},{6,4},{5,7},{7,5},{8,10},{10,8},{9,1... | collective-permute-start | bytes 3145736 | tf_op jit(solution)/shard_map/cond/branch_1_fun/ppermute | solution.py:26
  547.9 41.5 %collective-permute-start.49 = (bf16[256,2048]{1,0:T(8,128)(2,1)}, bf16[256,2048]{1,0:T(8,128)(2,1)}, u32[]{:S(2)}, u32[]{:S(2)}) collective-permute-start(bf16[256,2048]{1,0:T(8,128)(2,1)} %pad_maximum_fusion.8), channel_id=1, source_target_pairs={{0,2},{2,0},{1,3},{3,1},{4,6},{6,4},{5,7},{7,5},{8,10},{10,8},{9,1... | collective-permute-start | bytes 3145736 | tf_op jit(solution)/shard_map/cond/branch_1_fun/ppermute | solution.py:26
  550.1 39.3 %collective-permute-start.51 = (bf16[256,2048]{1,0:T(8,128)(2,1)}, bf16[256,2048]{1,0:T(8,128)(2,1)}, u32[]{:S(2)}, u32[]{:S(2)}) collective-permute-start(bf16[256,2048]{1,0:T(8,128)(2,1)} %pad_maximum_fusion.9), channel_id=1, source_target_pairs={{0,4},{4,0},{1,5},{5,1},{2,6},{6,2},{3,7},{7,3},{8,12},{12,8},{9,1... | collective-permute-start | bytes 3145736 | tf_op jit(solution)/shard_map/cond/branch_1_fun/ppermute | solution.py:26
  551.6 28.2 %collective-permute-start.52 = (bf16[128,1024]{1,0:T(8,128)(2,1)S(1)}, bf16[128,1024]{1,0:T(8,128)(2,1)S(1)}, u32[]{:S(2)}, u32[]{:S(2)}) collective-permute-start(bf16[128,1024]{1,0:T(8,128)(2,1)S(1)} %get-tuple-element.720), channel_id=1, source_target_pairs={{0,2},{2,0},{1,3},{3,1},{4,6},{6,4},{5,7},{7,5},{8,10},{10,8},{9,1... | collective-permute-start | bytes 786440 | tf_op jit(solution)/shard_map/cond/branch_1_fun/ppermute | solution.py:26
  552.6 32.0 %collective-permute-start.53 = (bf16[128,1024]{1,0:T(8,128)(2,1)S(1)}, bf16[128,1024]{1,0:T(8,128)(2,1)S(1)}, u32[]{:S(2)}, u32[]{:S(2)}) collective-permute-start(bf16[128,1024]{1,0:T(8,128)(2,1)S(1)} %get-tuple-element.719), channel_id=1, source_target_pairs={{0,4},{4,0},{1,5},{5,1},{2,6},{6,2},{3,7},{7,3},{8,12},{12,8},{9,1... | collective-permute-start | bytes 786440 | tf_op jit(solution)/shard_map/cond/branch_1_fun/ppermute | solution.py:26
  554.4 30.2 %collective-permute-start.54 = (bf16[128,1024]{1,0:T(8,128)(2,1)S(1)}, bf16[128,1024]{1,0:T(8,128)(2,1)S(1)}, u32[]{:S(2)}, u32[]{:S(2)}) collective-permute-start(bf16[128,1024]{1,0:T(8,128)(2,1)S(1)} %get-tuple-element.718), channel_id=1, source_target_pairs={{0,6},{2,4},{4,2},{6,0},{1,7},{3,5},{5,3},{7,1},{8,14},{10,12},{12... | collective-permute-start | bytes 786440 | tf_op jit(solution)/shard_map/cond/branch_1_fun/ppermute | solution.py:34
  (92 other events, 1190.3 us)
Sparse Core Ops, SparseCore 0:
  30.3 81.0 all-gather.3
  127.3 90.6 all-gather.5
  220.2 79.2 all-gather.7
  311.4 86.1 reduce-scatter.3
  410.6 76.5 reduce-scatter.5
  528.3 76.6 reduce-scatter.7

commit v3 on v2

--- a/solution.py
+++ b/solution.py
@@ -74,7 +74,7 @@
         part = pl.ds(pl.multiple_of((place_ref[0] ^ i) * width, 128), width)
         for kind in range(4):
             piece_ref[:, kind * width : (kind + 1) * width] = (
-                stack_ref[:, kind, part] if kind < 3 else last_ref[:, part]
+                stack_ref[kind, :, part] if kind < 3 else last_ref[:, part]
             )
 
 
@@ -86,7 +86,7 @@
         for kind in range(4):
             piece = piece_ref[:, kind * width : (kind + 1) * width].astype(f32)
             if kind < 3:
-                stack_ref[:, kind, part] = piece
+                stack_ref[kind, :, part] = piece
             else:
                 last_ref[:, part] = piece
 
@@ -106,18 +106,18 @@
         chip = place_ref[0] ^ i
         first_ref, second_ref = piece_refs[i], piece_refs[4 + i]
         part = pl.ds(pl.multiple_of(chip * first, 128), first)
-        for kind in range(3):
-            first_ref[:, kind * first : (kind + 1) * first] = read(kind, part)
+        for slot, kind in enumerate((2, 0, 1)):
+            first_ref[:, slot * first : (slot + 1) * first] = read(kind, part)
         part = pl.ds(pl.multiple_of(4 * first + chip * second, 128), second)
-        mixed = 2 * second
-        down = mixed + (128 if rest else 0)
-        for kind, start in enumerate((0, second, down)):
+        gates = second + (128 if rest else 0)
+        mixed = gates + 2 * second
+        for kind, start in enumerate((gates, gates + second, 0)):
             second_ref[:, start : start + second] = read(kind, part)
         if rest:
             part = pl.ds(pl.multiple_of(rest_start + (chip // 2) * 128, 128), 128)
             gate, up, last = [half_tile(read(kind, part), chip % 2 == 1) for kind in range(3)]
             second_ref[:, mixed : mixed + 128] = low_lanes(gate, pltpu.roll(up, 64, 1)).astype(bf16)
-            second_ref[:, down + second :] = low_lanes(last, 0.0).astype(bf16)
+            second_ref[:, second:gates] = low_lanes(last, 0.0).astype(bf16)
 
 
 def unpack_units_kernel(place_ref, *refs):
@@ -134,12 +134,12 @@
         chip = place_ref[0] ^ i
         first_ref, second_ref = piece_refs[i], piece_refs[4 + i]
         part = pl.ds(pl.multiple_of(chip * first, 128), first)
-        for kind in range(3):
-            write(kind, part, first_ref[:, kind * first : (kind + 1) * first].astype(f32))
+        for slot, kind in enumerate((2, 0, 1)):
+            write(kind, part, first_ref[:, slot * first : (slot + 1) * first].astype(f32))
         part = pl.ds(pl.multiple_of(4 * first + chip * second, 128), second)
-        mixed = 2 * second
-        down = mixed + (128 if rest else 0)
-        for kind, start in enumerate((0, second, down)):
+        gates = second + (128 if rest else 0)
+        mixed = gates + 2 * second
+        for kind, start in enumerate((gates, gates + second, 0)):
             write(kind, part, second_ref[:, start : start + second].astype(f32))
         if rest:
             part = pl.ds(pl.multiple_of(rest_start + (chip // 2) * 128, 128), 128)
@@ -148,7 +148,7 @@
             mine = (lane >= 64) == odd
             both = second_ref[:, mixed : mixed + 128].astype(f32)
             turned = pltpu.roll(both, 64, 1)
-            last = second_ref[:, down + second :].astype(f32)
+            last = second_ref[:, second:gates].astype(f32)
             last = jnp.where(odd, pltpu.roll(last, 64, 1), last)
             for kind, values in enumerate(
                 (jnp.where(odd, turned, both), jnp.where(odd, both, turned), last)
@@ -178,55 +178,86 @@
     return collected(exchange(pieces))
 
 
+def split_kernel(place_ref, values_ref, *piece_refs):
+    rows = piece_refs[0].shape[0]
+    for i, piece_ref in enumerate(piece_refs):
+        start = pl.multiple_of((place_ref[0] ^ i) * rows, rows)
+        piece_ref[...] = values_ref[pl.ds(start, rows), :]
+
+
 def returned(values):
-    rows = values.shape[0] // 4
-    return exchange(
-        [lax.dynamic_slice_in_dim(values, (place() ^ i) * rows, rows, 0) for i in range(4)]
-    )
+    shape = (values.shape[0] // 4, values.shape[1])
+    return exchange(on_place(split_kernel, "split_rows", (values,), [(shape, bf16)] * 4))
 
 
 def gather_begin(own):
     return own, swap(own, NEAR), swap(own, MID)
 
 
-def gather_end(state):
+def gather_diagonal(state):
     own, near, mid = state
     half = own.shape[0] // 2
-    diagonal_low = swap(near[:half], MID)
-    diagonal_high = swap(mid[half:], NEAR)
-    core = jnp.concatenate([own, near, mid, diagonal_low, diagonal_high], axis=0)
+    return swap(near[:half], MID), swap(mid[half:], NEAR)
+
+
+def gather_end(state, diagonal):
+    core = jnp.concatenate([*state, *diagonal], axis=0)
     return core, swap(core, TP)
 
 
+def halves_begin(halves):
+    return [swap(half, axis) for axis in (NEAR, MID) for half in halves]
+
+
+def halves_diagonal(sides):
+    return swap(sides[0], MID), swap(sides[3], NEAR)
+
+
+def joined(pieces):
+    rows = jnp.concatenate(pieces, axis=0)
+    return rows, swap(rows, TP)
+
+
+def row_pieces(*pairs):
+    return [pair[core] for core in range(2) for pair in pairs]
+
+
 def gather_rows(own):
-    return gather_end(gather_begin(own))
-
-
-def add_low(a, b):
-    return (a.astype(f32) + b.astype(f32)).astype(bf16)
-
-
-def scatter_begin(mine, others):
-    return add_low(mine, swap(others, TP))
-
-
-def scatter_middle(core):
-    rows = core.shape[0] // 4
-    half = rows // 2
-    return swap(core[3 * rows : 3 * rows + half], MID), swap(core[3 * rows + half :], NEAR)
-
-
-def scatter_end(core, middle):
-    rows = core.shape[0] // 4
-    half = rows // 2
-    own, near, mid = [core[i * rows : (i + 1) * rows] for i in range(3)]
-    near = jnp.concatenate([add_low(near[:half], middle[0]), near[half:]], axis=0)
-    mid = jnp.concatenate([mid[:half], add_low(mid[half:], middle[1])], axis=0)
-    return own, swap(near, NEAR), swap(mid, MID)
-
-
-def scatter_rest(core):
-    return scatter_end(core, scatter_middle(core))
+    state = gather_begin(own)
+    return gather_end(state, gather_diagonal(state))
+
+
+def add_low(*values):
+    return sum(value.astype(f32) for value in values).astype(bf16)
+
+
+def add_halves(mine, others):
+    half = mine.shape[0] // 2
+    return add_low(mine[:half], others[:half]), add_low(mine[half:], others[half:])
+
+
+def scatter_cores(mine, others):
+    others = swap(others, TP)
+    start = 3 * (mine.shape[0] // 4)
+    return others, *add_halves(mine[start:], others[start:])
+
+
+def scatter_middle(low, high):
+    return swap(low, MID), swap(high, NEAR)
+
+
+def side_sums(mine, others, first, middle):
+    half = middle[0].shape[0]
+    start = 2 * half * first
+    near, mid = slice(start, start + 2 * half), slice(start + 2 * half, start + 4 * half)
+    near = add_low(mine[near], others[near], jnp.pad(middle[0], ((0, half), (0, 0))))
+    mid = add_low(mine[mid], others[mid], jnp.pad(middle[1], ((half, 0), (0, 0))))
+    return near, mid
+
+
+def scatter_end(mine, others, first, middle):
+    near, mid = side_sums(mine, others, first, middle)
+    return swap(near, NEAR), swap(mid, MID)
 
 
 def stage(always, step, *operands):
@@ -287,6 +318,34 @@
     centre = values - jnp.mean(values, axis=-1, keepdims=True)
     inverse = lax.rsqrt(jnp.mean(centre * centre, axis=-1, keepdims=True) + epsilon)
     return centre * inverse, inverse
+
+
+def write_halves(refs, values):
+    whole_ref, low_ref, high_ref = refs
+    values = values.astype(bf16)
+    whole_ref[...] = values
+    half = pl.num_programs(0) // 2
+
+    @pl.when(pl.program_id(0) < half)
+    def _():
+        low_ref[...] = values
+
+    @pl.when(pl.program_id(0) >= half)
+    def _():
+        high_ref[...] = values
+
+
+def halves_specs(block, width, steps):
+    half = steps // 2
+    return [
+        pl.BlockSpec((block, width), lambda i: (i, 0)),
+        pl.BlockSpec((block, width), lambda i: (jnp.minimum(i, half - 1), 0)),
+        pl.BlockSpec((block, width), lambda i: (jnp.maximum(i - half, 0), 0)),
+    ]
+
+
+def halves_shapes(rows, width):
+    return [jax.ShapeDtypeStruct((size, width), bf16) for size in (rows, rows // 2, rows // 2)]
 
 
 def norm_kernel(*refs):
@@ -322,8 +381,8 @@
 
 
 def norm_back_kernel(count, *refs):
-    row_refs, part_refs = refs[:count], refs[count : count + 3]
-    gain_ref, past_ref, grad_ref, low_ref, sum_ref = refs[count + 3 :]
+    row_refs, part_refs = refs[:count], refs[count:-7]
+    gain_ref, past_ref, *low_refs, grad_ref, sum_ref = refs[-7:]
     normed, inverse = normalised(sum(ref[...].astype(f32) for ref in row_refs))
     grad = sum(ref[...].astype(f32) for ref in part_refs)
     scaled = grad * gain_ref[...]
@@ -334,7 +393,7 @@
     )
     total = past_ref[...].astype(f32) + inverse * centred
     grad_ref[...] = total
-    low_ref[...] = total.astype(bf16)
+    write_halves(low_refs, total)
 
     @pl.when(pl.program_id(0) == 0)
     def _():
@@ -346,16 +405,17 @@
 
 def norm_back(summands, parts, gain, past):
     rows, width = past.shape
-    block = min(64, rows)
+    block = min(64, rows // 2)
     of_rows = pl.BlockSpec((block, width), lambda i: (i, 0))
     of_gain = pl.BlockSpec((1, width), lambda i: (0, 0))
     shape = jax.ShapeDtypeStruct
     return pl.pallas_call(
         partial(norm_back_kernel, len(summands)),
         grid=(rows // block,),
-        in_specs=[of_rows] * (len(summands) + 3) + [of_gain, of_rows],
-        out_specs=[of_rows, of_rows, pl.BlockSpec((2, width), lambda i: (0, 0))],
-        out_shape=[shape((rows, width), f32), shape((rows, width), bf16), shape((2, width), f32)],
+        in_specs=[of_rows] * (len(summands) + len(parts)) + [of_gain, of_rows],
+        out_specs=halves_specs(block, width, rows // block)
+        + [of_rows, pl.BlockSpec((2, width), lambda i: (0, 0))],
+        out_shape=halves_shapes(rows, width) + [shape((rows, width), f32), shape((2, width), f32)],
         cost_estimate=LIGHT,
         name="norm_back",
     )(*summands, *parts, gain[None], past)
@@ -492,16 +552,16 @@
         out_ref[...] = dot_nt(grad_ref[core, 0], weight_ref[:, : 3 * width]).astype(bf16)
 
 
-def tree_block(*shape):
-    return pl.BlockSpec((1,) + shape, lambda t: (t,) + (0,) * len(shape))
-
-
-def row_block(rows, columns):
-    return pl.BlockSpec((rows, columns), lambda t: (t, 0))
-
-
-def core_block(rows, columns):
-    return pl.BlockSpec((2, 1, rows, columns), lambda t: (0, t, 0, 0))
+def tree_block(*shape, first=0):
+    return pl.BlockSpec((1,) + shape, lambda t: (first + t,) + (0,) * len(shape))
+
+
+def row_block(rows, columns, first=0):
+    return pl.BlockSpec((rows, columns), lambda t: (first + t, 0))
+
+
+def core_block(rows, columns, first=0):
+    return pl.BlockSpec((2, 1, rows, columns), lambda t: (0, first + t, 0, 0))
 
 
 def whole_block(*shape):
@@ -562,28 +622,28 @@
     )
 
 
-def attention_backward(cores, weights, qkv, log_totals, tree_info):
+def attention_backward(cores, weights, qkv, log_totals, tree_info, first, count):
     row_info, col_info, keep, cosine, sine = tree_info
     model_width = weights.shape[0]
     width = weights.shape[1] // 4
-    rows = cores[0].shape[0] // 4
+    rows = cores[0].shape[0] // count
     group = 2 * rows
     heads = width // HD
     shape = jax.ShapeDtypeStruct
     return pl.pallas_call(
         backward_kernel,
-        grid=(4,),
+        grid=(count,),
         in_specs=[
             row_block(rows, model_width),
             row_block(rows, model_width),
             whole_block(*weights.shape),
-            core_block(rows, 3 * width),
-            tree_block(*row_info.shape[1:]),
-            tree_block(*col_info.shape[1:]),
-            tree_block(*keep.shape[1:]),
-            tree_block(*cosine.shape[1:]),
-            tree_block(*sine.shape[1:]),
-            tree_block(heads, group),
+            core_block(rows, 3 * width, first=first),
+            tree_block(*row_info.shape[1:], first=first),
+            tree_block(*col_info.shape[1:], first=first),
+            tree_block(*keep.shape[1:], first=first),
+            tree_block(*cosine.shape[1:], first=first),
+            tree_block(*sine.shape[1:], first=first),
+            tree_block(heads, group, first=first),
         ],
         out_specs=[
             core_block(rows, 3 * width),
@@ -592,15 +652,19 @@
             row_block(rows, model_width),
         ],
         out_shape=[
-            shape((2, 4, rows, 3 * width), bf16),
-            shape((4, 1, 3 * width), f32),
-            shape((4 * rows, model_width), bf16),
-            shape((4 * rows, model_width), bf16),
+            shape((2, count, rows, 3 * width), bf16),
+            shape((count, 1, 3 * width), f32),
+            shape((count * rows, model_width), bf16),
+            shape((count * rows, model_width), bf16),
         ],
         scratch_shapes=[pltpu.VMEM((group, width), f32)],
         compiler_params=pltpu.CompilerParams(vmem_limit_bytes=48 << 20),
-        cost_estimate=pl.CostEstimate(
-            flops=16 * group * model_width * width * 2, bytes_accessed=32 << 20, transcendentals=4 << 20
+        cost_estimate=LIGHT
+        if first == 3
+        else pl.CostEstimate(
+            flops=4 * count * group * model_width * width * 2,
+            bytes_accessed=8 * count << 20,
+            transcendentals=count << 20,
         ),
         name="attention_backward",
     )(
@@ -618,15 +682,13 @@
 
 def units_kernel(parts, *refs):
     main, mixed = parts
-    count = 7 if len(refs) == 11 else 5
     x_refs, dy_refs, weight_ref = refs[0:2], refs[2:4], refs[4]
-    before_refs = refs[5:count]
-    grad_ref, hidden_ref = refs[count : count + 2]
-    out_refs = refs[count + 2 :]
-    wide = 2 * main + mixed
+    before_refs, out_refs = refs[5:-4], refs[-2:]
+    grad_ref, hidden_ref = refs[-4:-2]
+    down = main + mixed
     for core in range(2):
-        gate_up = dot_nn(x_refs[core][...], weight_ref[:, :wide])
-        d_hidden = dot_nn(dy_refs[core][...], weight_ref[:, wide:])
+        gate_up = dot_nn(x_refs[core][...], weight_ref[:, down:])
+        d_hidden = dot_nn(dy_refs[core][...], weight_ref[:, :down])
 
         def unit(gate, up, grad):
             sigmoid = jax.nn.sigmoid(gate)
@@ -645,33 +707,37 @@
             hidden, d_gate, d_up = unit(both, pltpu.roll(both, 64, 1), d_hidden[:, main:])
             hidden_ref[core, 0, :, main:] = low_lanes(hidden, 0.0).astype(bf16)
             grad_ref[core, 0, :, 2 * main :] = low_lanes(d_gate, pltpu.roll(d_up, 64, 1)).astype(bf16)
-        total = dot_nt(grad_ref[core, 0], weight_ref[:, :wide])
+        total = dot_nt(grad_ref[core, 0], weight_ref[:, down:])
         if before_refs:
             total = total + before_refs[core][...].astype(f32)
         out_refs[core][...] = total.astype(bf16)
 
 
-def hidden_units(xs, dys, weights, parts, before=()):
+def hidden_units(xs, dys, weights, parts, trees=(0, 4), before=()):
+    first, count = trees
     model_width = weights.shape[0]
     main, mixed = parts
     wide = 2 * main + mixed
     rows = xs[0].shape[0] // 4
     shape = jax.ShapeDtypeStruct
     rows_of = row_block(rows, model_width)
+    given = row_block(rows, model_width, first=first)
     return pl.pallas_call(
         partial(units_kernel, parts),
-        grid=(4,),
-        in_specs=[rows_of] * 4 + [whole_block(*weights.shape)] + [rows_of] * len(before),
+        grid=(count,),
+        in_specs=[given] * 4 + [whole_block(*weights.shape)] + [given] * len(before),
         out_specs=[core_block(rows, wide), core_block(rows, main + mixed), rows_of, rows_of],
         out_shape=[
-            shape((2, 4, rows, wide), bf16),
-            shape((2, 4, rows, main + mixed), bf16),
-            shape((4 * rows, model_width), bf16),
-            shape((4 * rows, model_width), bf16),
+            shape((2, count, rows, wide), bf16),
+            shape((2, count, rows, main + mixed), bf16),
+            shape((count * rows, model_width), bf16),
+            shape((count * rows, model_width), bf16),
         ],
         compiler_params=pltpu.CompilerParams(vmem_limit_bytes=56 << 20),
         cost_estimate=pl.CostEstimate(
-            flops=16 * rows * model_width * 5 * main, bytes_accessed=32 << 20, transcendentals=1 << 20
+            flops=4 * count * rows * model_width * 5 * main,
+            bytes_accessed=8 * count << 20,
+            transcendentals=count << 18,
         ),
         name="hidden_units",
     )(*xs, *dys, weights, *before)
@@ -681,61 +747,76 @@
     return lax.dot_general(a, b, (((0,), (0,)), ((), ())), preferred_element_type=f32)
 
 
-def weight_kernel(*refs):
-    left_refs, right_refs, out_ref = (refs[0:2], refs[2:4]), refs[4:6], refs[6]
+def weight_kernel(counts, *refs):
+    refs, out_ref = list(refs[:-1]), refs[-1]
     start = 0
-    for lefts, right_ref in zip(left_refs, right_refs):
-        columns = right_ref.shape[-1]
+    for left_count, right_count in counts:
+        lefts, refs = refs[:left_count], refs[left_count:]
+        rights, refs = refs[:right_count], refs[right_count:]
+        columns = rights[0].shape[-1]
+        rows = rights[0].shape[2]
+        pieces = left_count // 2
+        left_ends = [sum(left.shape[0] for left in lefts[: i + 1]) // rows for i in range(pieces)]
+        right_ends = [sum(right.shape[1] for right in rights[: i + 1]) for i in range(right_count)]
         total = 0.0
         for core in range(2):
-            total = total + dot_tn(lefts[core][...], right_ref[core].reshape(-1, columns))
+            tree = 0
+            for end in sorted({*left_ends, *right_ends}):
+                i = sum(tree >= left_end for left_end in left_ends)
+                j = sum(tree >= right_end for right_end in right_ends)
+                at = tree - ([0] + left_ends)[i]
+                left = lefts[core * pieces + i][at * rows : (at + end - tree) * rows]
+                at = tree - ([0] + right_ends)[j]
+                right = rights[j][core, at : at + end - tree].reshape(-1, columns)
+                total = total + dot_tn(left, right)
+                tree = end
         out_ref[:, start : start + columns] = total.astype(bf16)
         start += columns
 
 
-def weight_terms(lefts, rights):
-    rows, model_width = lefts[0][0].shape
+def weight_terms(*products):
+    model_width = products[0][0][0].shape[1]
     block = 256
-    total = sum(right.shape[-1] for right in rights)
-    left_block = pl.BlockSpec((rows, block), lambda i: (0, i))
+    total = sum(rights[0].shape[-1] for _, rights in products)
+    operands, specs = [], []
+    for lefts, rights in products:
+        operands += [*lefts, *rights]
+        specs += [pl.BlockSpec((left.shape[0], block), lambda i: (0, i)) for left in lefts]
+        specs += [whole_block(*right.shape) for right in rights]
     return pl.pallas_call(
-        weight_kernel,
+        partial(weight_kernel, [(len(lefts), len(rights)) for lefts, rights in products]),
         grid=(model_width // block,),
-        in_specs=[left_block] * 4 + [whole_block(*right.shape) for right in rights],
+        in_specs=specs,
         out_specs=pl.BlockSpec((block, total), lambda i: (i, 0)),
         out_shape=jax.ShapeDtypeStruct((model_width, total), bf16),
-        compiler_params=pltpu.CompilerParams(vmem_limit_bytes=48 << 20),
-        cost_estimate=pl.CostEstimate(
-            flops=4 * rows * model_width * total, bytes_accessed=32 << 20, transcendentals=0
-        ),
+        compiler_params=pltpu.CompilerParams(vmem_limit_bytes=60 << 20),
+        cost_estimate=LIGHT,
         name="weight_terms",
-    )(*lefts[0], *lefts[1], *rights)
+    )(*operands)
 
 
 def out_kernel(first_ref, second_ref, first_weight_ref, second_weight_ref, *out_refs):
-    down = [first_ref.shape[-1], second_ref.shape[-1]]
     for core, out_ref in enumerate(out_refs):
-        total = dot_nt(first_ref[core, 0], first_weight_ref[:, -down[0] :])
-        total = total + dot_nt(second_ref[core, 0], second_weight_ref[:, -down[1] :])
+        total = dot_nt(first_ref[core, 0], first_weight_ref[...])
+        total = total + dot_nt(second_ref[core, 0], second_weight_ref[...])
         out_ref[...] = total.astype(bf16)
 
 
-def units_out(hiddens, weights):
-    rows = hiddens[0].shape[2]
+def units_out(hiddens, weights, first):
+    _, count, rows, _ = hiddens[1].shape
     model_width = weights[0].shape[0]
     return pl.pallas_call(
         out_kernel,
-        grid=(4,),
-        in_specs=[core_block(rows, hidden.shape[-1]) for hidden in hiddens]
-        + [whole_block(*weight.shape) for weight in weights],
+        grid=(count,),
+        in_specs=[
+            core_block(rows, hiddens[0].shape[-1], first=first),
+            core_block(rows, hiddens[1].shape[-1]),
+        ]
+        + [whole_block(model_width, hidden.shape[-1]) for hidden in hiddens],
         out_specs=[row_block(rows, model_width)] * 2,
-        out_shape=[jax.ShapeDtypeStruct((4 * rows, model_width), bf16)] * 2,
+        out_shape=[jax.ShapeDtypeStruct((count * rows, model_width), bf16)] * 2,
         compiler_params=pltpu.CompilerParams(vmem_limit_bytes=48 << 20),
-        cost_estimate=pl.CostEstimate(
-            flops=16 * rows * model_width * sum(hidden.shape[-1] for hidden in hiddens),
-            bytes_accessed=24 << 20,
-            transcendentals=0,
-        ),
+        cost_estimate=LIGHT,
         name="units_out",
     )(*hiddens, *weights)
 
@@ -768,7 +849,7 @@
     always = valid_mask[0] >= 0
 
     pieces = on_place(
-        pack_heads_kernel, "pack_heads", (w_qkv, w_out), [((weight_rows, 4 * width), bf16)] * 4
+        pack_heads_kernel, "pack_heads", (w_qkv.transpose(1, 0, 2), w_out), [((weight_rows, 4 * width), bf16)] * 4
     )
     attn_pieces = exchange(pieces)
     (normed1,) = norm_rows(tokens, (), ln1_gain, ln1_bias)
@@ -785,12 +866,9 @@
     attn_spread = collected(attn_pieces)
     attn_full = gather_far(attn_spread)
 
-    def prepare(attn_spread, normed1, unit_pieces, cotangent, seg_ids, valid_mask, parents):
+    def prepare(attn_spread, normed1, unit_pieces, seg_ids, valid_mask, parents):
         spread1 = gather_rows(normed1)
         spread_a, spread_b = spread(unit_pieces[:4]), spread(unit_pieces[4:])
-        cotangent, _, _ = lax.optimization_barrier((cotangent, spread1[0], spread_b))
-        dy_state = gather_begin(cotangent)
-
         ints = jnp.concatenate([seg_ids, valid_mask, parents[0]])
         plane_ints = plane_trees(ints)
 
@@ -810,91 +888,124 @@
         col_info = jnp.stack([jnp.where(plane_valid > 0, plane_segs, -1), all_ids], axis=2)
         keep = plane_valid.astype(f32)[..., None]
         tree_info = (row_info, col_info, keep, *rope_tables(positions))
-        return spread1, spread_a, spread_b, dy_state[1:], tree_info
-
-    spread1, spread_a, spread_b, dy_near, tree_info = stage(
-        always, prepare, attn_spread, normed1, unit_pieces, cotangent, seg_ids, valid_mask, parents
+        return spread1, spread_a, spread_b, tree_info
+
+    spread1, spread_a, spread_b, tree_info = stage(
+        always, prepare, attn_spread, normed1, unit_pieces, seg_ids, valid_mask, parents
     )
     own_valid = tree_info[2][0, :own_rows]
     units_a = gather_far(spread_a)
     units_b = gather_far(spread_b)
 
-    def attend(spread1, attn_full, tree_info, tokens, cotangent, dy_near):
+    def attend(spread1, attn_full, tree_info):
         own_bias = lax.dynamic_slice(qkv_bias, (0, quarter * width), (3, width))
-        qkv, context, log_totals, *attn_partial = attention_forward(
-            spread1, attn_full, own_bias.reshape(1, -1), tree_info
+        return attention_forward(spread1, attn_full, own_bias.reshape(1, -1), tree_info)
+
+    dy_state = gather_begin(after(cotangent, spread1, spread_a, spread_b))
+    qkv, context, log_totals, *attn_partial = stage(always, attend, spread1, attn_full, tree_info)
+
+    def renorm(attn_partial, dy_state, tokens):
+        dy_diagonal = gather_diagonal(dy_state)
+        others, low, high = scatter_cores(*attn_partial)
+        middle = scatter_middle(low, high)
+        middle, dy_state, dy_diagonal = lax.optimization_barrier((middle, dy_state, dy_diagonal))
+        spread_dy = gather_end(dy_state, dy_diagonal)
+        parts = attn_partial[0], others, *scatter_end(attn_partial[0], others, 1, middle)
+        normed2, attn_out = norm_rows(tokens, parts, ln2_gain, ln2_bias)
+        return attn_out, gather_rows(normed2), spread_dy
+
+    attn_out, spread2, spread_dy = stage(always, renorm, attn_partial, dy_state, tokens)
+
+    d_units_a, hidden_a, *d_normed2 = hidden_units(spread2, spread_dy, units_a, (main_a, 0))
+    terms_a = weight_terms((spread_dy, (hidden_a,)), (spread2, (d_units_a,)))
+    grads_a = scatter_far(terms_a)
+
+    def finish_units(terms_a, spread2, spread_dy, units_a, units_b, d_normed2, hidden_a, attn_out, tokens, cotangent):
+        def run(xs, first, count):
+            return hidden_units(xs, spread_dy, units_b, (main_b, mixed), (first, count), d_normed2)
+
+        def out(hidden, first):
+            return units_out((hidden_a, hidden), (units_a, units_b), first)
+
+        last = run(spread2, 3, 1)
+        low, high = add_halves(last[2], swap(last[3], TP))
+        xs, low, high = lax.optimization_barrier((spread2, low, high))
+        middle = scatter_middle(low, high)
+        sides = run(xs, 1, 2)
+        middle, sides = lax.optimization_barrier((middle, sides))
+        others = swap(sides[3], TP)
+        mlp_last = out(last[1], 3)
+        others, mlp_last = lax.optimization_barrier((others, mlp_last))
+        near, mid = side_sums(sides[2], others, 0, middle)
+        xs, near, mid = lax.optimization_barrier((spread2, near, mid))
+        near, mid = swap(near, NEAR), swap(mid, MID)
+        own = run(xs, 0, 1)
+        own_others = swap(own[3], TP)
+        units = own, sides, last
+        terms_b = weight_terms(
+            (spread_dy, [u[1] for u in units]), (spread2, [u[0] for u in units])
         )
-        spread_dy = gather_end((cotangent, *dy_near))
-        core = after(scatter_begin(*attn_partial), spread_dy[0])
-        normed2, attn_out = norm_rows(tokens, scatter_rest(core), ln2_gain, ln2_bias)
-        return qkv, context, log_totals, attn_out, gather_rows(normed2), spread_dy
-
-    qkv, context, log_totals, attn_out, spread2, spread_dy = stage(
-        always, attend, spread1, attn_full, tree_info, tokens, cotangent, dy_near
-    )
-
-    d_units_a, hidden_a, *d_normed2 = hidden_units(spread2, spread_dy, units_a, (main_a, 0))
-    terms_a = weight_terms((spread2, spread_dy), (d_units_a, hidden_a))
-    grads_a = scatter_far(terms_a)
-
-    def finish_units(terms_a, spread2, spread_dy, units_a, units_b, d_normed2, hidden_a, attn_out, tokens, cotangent):
-        d_units_b, hidden_b, *d_normed2 = hidden_units(
-            spread2, spread_dy, units_b, (main_b, mixed), d_normed2
+        mlp_own, mlp_sides = out(own[1], 0), out(sides[1], 1)
+        mlp_cores = add_halves(mlp_last[0], swap(mlp_last[1], TP))
+        near, mid, terms_b, mlp_cores, mlp_own, mlp_sides = lax.optimization_barrier(
+            (near, mid, terms_b, mlp_cores, mlp_own, mlp_sides)
         )
-        core = scatter_begin(*d_normed2)
-        d_units_b, hidden_b, core = lax.optimization_barrier((d_units_b, hidden_b, core))
-        middle = scatter_middle(core)
-        mlp_partial = units_out((hidden_a, hidden_b), (units_a, units_b))
-        middle, mlp_partial = lax.optimization_barrier((middle, mlp_partial))
-        parts = scatter_end(core, middle)
-        terms_b = weight_terms((spread2, spread_dy), (d_units_b, hidden_b))
-        mlp_core = scatter_begin(*mlp_partial)
-        parts, terms_b = lax.optimization_barrier((parts, terms_b))
-        d_residual, d_low, norm2_grads = norm_back((tokens, attn_out), parts, ln2_gain, cotangent)
-        return mlp_core, terms_b, d_residual, d_low, norm2_grads
-
-    mlp_core, terms_b, d_residual, d_low, norm2_grads = stage(
+        mlp_middle = scatter_middle(*mlp_cores)
+        parts = own[2], own_others, near, mid
+        *d_low, d_residual, norm2_grads = norm_back(
+            (tokens, attn_out), parts, ln2_gain, cotangent
+        )
+        return (mlp_own, mlp_sides, mlp_middle), terms_b, d_residual, d_low, norm2_grads
+
+    mlp, terms_b, d_residual, d_low, norm2_grads = stage(
         always, finish_units, terms_a, spread2, spread_dy, units_a, units_b, d_normed2, hidden_a, attn_out, tokens, cotangent
     )
     grads_a, d_low = lax.optimization_barrier((grads_a, d_low))
     grads_b = scatter_far(terms_b)
 
-    def attend_back(terms_b, d_low, attn_full, qkv, log_totals, tree_info, spread1, context, mlp_core, grads_a):
-        spread_grad = gather_rows(d_low)
-        mlp_core, grads_a, spread_grad = lax.optimization_barrier((mlp_core, grads_a, spread_grad))
-        mlp_middle = scatter_middle(mlp_core)
+    def attend_back(terms_b, d_low, attn_full, qkv, log_totals, tree_info, spread1, context, mlp):
+        mlp_own, mlp_sides, mlp_middle = mlp
+
+        def back(cores, first, count):
+            return attention_backward(cores, attn_full, qkv, log_totals, tree_info, first, count)
+
+        state = halves_begin(d_low[1:])
+        own = d_low[0], swap(d_low[0], TP)
+        own_back = back(own, 0, 1)
+        mlp_others = swap(mlp_own[1], TP), swap(mlp_sides[1], TP)
+        near, mid = side_sums(mlp_sides[0], mlp_others[1], 0, mlp_middle)
+        state, own_back, near, mid = lax.optimization_barrier((state, own_back, near, mid))
+        diagonal = halves_diagonal(state)
+        sides = joined(state)
+        sides_back = back(sides, 1, 2)
+        diagonal, sides_back, near, mid = lax.optimization_barrier((diagonal, sides_back, near, mid))
+        mlp_parts = swap(near, NEAR), swap(mid, MID)
+        last = joined(diagonal)
+        last_back = back(last, 3, 1)
+        backs = own_back, sides_back, last_back
+        terms = weight_terms(
+            (spread1, [back[0] for back in backs]), (row_pieces(own, sides, last), (context,))
+        )
+        low, high = add_halves(last_back[2], swap(last_back[3], TP))
+        bias_terms = sum(jnp.sum(back[1], axis=0) for back in backs)
+        d_normed1 = own_back[2:], sides_back[2:], (low, high)
+        return terms, bias_terms, d_normed1, (mlp_own[0], mlp_others[0], *mlp_parts)
+
+    attn_terms, bias_terms, d_normed1, mlp_parts = stage(
+        always, attend_back, terms_b, d_low, attn_full, qkv, log_totals, tree_info, spread1, context, mlp
+    )
+    attn_grads = scatter_far(attn_terms)
+
+    def finish(attn_terms, d_normed1, mlp_parts, grads_a, d_residual, attn_out, tokens, bias_terms, norm2_grads, own_valid):
+        own, sides, last = d_normed1
+        middle = scatter_middle(*last)
+        own_others, sides_others = swap(own[1], TP), swap(sides[1], TP)
         pieces_a = returned(grads_a)
-        d_linear, bias_terms, *d_normed1 = attention_backward(
-            spread_grad, attn_full, qkv, log_totals, tree_info
-        )
-        mlp_middle, pieces_a, d_linear, d_normed1 = lax.optimization_barrier(
-            (mlp_middle, pieces_a, d_linear, d_normed1)
-        )
-        mlp_parts = scatter_end(mlp_core, mlp_middle)
-        core = scatter_begin(*d_normed1)
-        terms = weight_terms((spread1, spread_grad), (d_linear, context))
-        return terms, bias_terms, core, mlp_parts, pieces_a
-
-    attn_terms, bias_terms, d_normed1_core, mlp_parts, pieces_a = stage(
-        always, attend_back, terms_b, d_low, attn_full, qkv, log_totals, tree_info, spread1, context, mlp_core, grads_a
-    )
-    grads_b, d_normed1_core = lax.optimization_barrier((grads_b, d_normed1_core))
-    attn_grads = scatter_far(attn_terms)
-
-    def finish(attn_terms, core, mlp_parts, pieces_a, grads_b, d_residual, attn_out, tokens, bias_terms, norm2_grads, own_valid):
-        tokens_grad, _, norm1_grads = norm_back(
-            (tokens,), scatter_rest(core), ln1_gain, d_residual
-        )
+        parts = own[0], own_others, *scatter_end(sides[0], sides_others, 0, middle)
+        *_, tokens_grad, norm1_grads = norm_back((tokens,), parts, ln1_gain, d_residual)
         mlp_out = sum(part.astype(f32) for part in mlp_parts)
         stream_out = tokens.astype(f32) + attn_out + mlp_out
         output = stream_out.astype(bf16)
-        gate_up_grad, down_grad = on_place(
-            unpack_units_kernel,
-            "unpack_units",
-            (*pieces_a, *returned(grads_b)),
-            [(w_gate_up.shape, f32), (w_down.shape, f32)],
-        )
-
         squares = jnp.stack(
             [
                 jnp.sum(own_valid * stream_out * stream_out),
@@ -905,26 +1016,34 @@
         )
         bias_spread = lax.dynamic_update_slice(
             jnp.zeros((3, model_width), f32),
-            jnp.sum(bias_terms, axis=0).reshape(3, width),
+            bias_terms.reshape(3, width),
             (0, tp_index * local_width + quarter * width),
         )
         sums = jnp.concatenate(
             [norm1_grads, norm2_grads, bias_spread, jnp.pad(squares, (0, model_width - 4))[None]]
         )
-        return output, tokens_grad, gate_up_grad, down_grad, sums
-
-    output, tokens_grad, gate_up_grad, down_grad, sums = stage(
-        always, finish, attn_terms, d_normed1_core, mlp_parts, pieces_a, grads_b, d_residual, attn_out, tokens, bias_terms, norm2_grads, own_valid
-    )
+        return output, tokens_grad, pieces_a, sums
+
+    output, tokens_grad, pieces_a, sums = stage(
+        always, finish, attn_terms, d_normed1, mlp_parts, grads_a, d_residual, attn_out, tokens, bias_terms, norm2_grads, own_valid
+    )
+    pieces_b = returned(after(grads_b, sums))
     sums = sum_over(sums, (TP, NEAR, MID))
-    attn_grads, sums = lax.optimization_barrier((attn_grads, sums))
+    attn_grads, sums, pieces_b = lax.optimization_barrier((attn_grads, sums, pieces_b))
+    gate_up_grad, down_grad = on_place(
+        unpack_units_kernel,
+        "unpack_units",
+        (*pieces_a, *pieces_b),
+        [(w_gate_up.shape, f32), (w_down.shape, f32)],
+    )
     sums = sum_over(sums, (FAR,))
     qkv_grad, out_grad = on_place(
         unpack_heads_kernel,
         "unpack_heads",
         returned(attn_grads),
-        [(w_qkv.shape, f32), (w_out.shape, f32)],
-    )
+        [((3, weight_rows, local_width), f32), (w_out.shape, f32)],
+    )
+    qkv_grad = qkv_grad.transpose(1, 0, 2)
     norm_sums, bias_sums, square_sums = sums[:4], sums[4:7], sums[7]
     stream_rms = jnp.sqrt(square_sums[:3] / (square_sums[3] * model_width))
     qkv_bias_grad = lax.dynamic_slice(bias_sums, (0, tp_index * local_width), (3, local_width))

time: 646 us -> 600 us (0.929)
  waiting for transfers between devices: 241 us -> 187 us
  Pallas kernels: 198 us -> 222 us
  local copies, waits for them, and re-layouts: 65.3 us -> 49.6 us
  starting transfers between devices: 64.7 us -> 71.9 us
    ppermute x54 -> x64, waiting for transfers between devices: 224 us -> 164 us  [swap(): return lax.ppermute(values, axis, [(0, 1), (1, 0)])]
    pallas_call x7 -> x13, Pallas kernels: 140 us -> 162 us  [the longest x4 58.8 us: hidden_units(): pl.pallas_call(partial(units_kernel, parts), grid=(count,), in_specs=[giv...]
    slice x16 -> x6, local copies, waits for them, and re-layouts: 14.1 us -> 2.48 us  [gather_diagonal(): return (swap(near[:half], MID), swap(mid[half:], NEAR))]
    ppermute x54 -> x64, starting transfers between devices: 48.2 us -> 58.5 us  [swap(): return lax.ppermute(values, axis, [(0, 1), (1, 0)])]
    unnamed x34 -> x46, local copies, waits for them, and re-layouts: 13.8 us -> 11.7 us
    cond x76 -> x90, local copies, waits for them, and re-layouts: 26.6 us -> 28.6 us
  transfers between devices with their start and end apart: 72 -> 82, of which waited for: 35 -> 41; matrix products, arithmetic and copies ran while one was open for 15% -> 13% of each run, Pallas kernels for 31% -> 37%
where the time goes in v3:
time: 600 us; the launch traced here: 593 us
  Pallas kernels  222 us (37%)
  waiting for transfers between devices  187 us (31%)
  starting transfers between devices  71.9 us (12%)
  local copies, waits for them, and re-layouts  49.6 us (8%)
  other arithmetic  44.8 us (7%)
  between operations  16.2 us (3%)
    ppermute x64, waiting for transfers between devices, swap(): return lax.ppermute(values, axis, [(0, 1), (1, 0)])  164 us
    pallas_call x4, Pallas kernels, hidden_units(): pl.pallas_call(partial(units_kernel, parts), grid=(count,), in_specs=[giv...  58.8 us
    ppermute x64, starting transfers between devices, swap(): return lax.ppermute(values, axis, [(0, 1), (1, 0)])  58.5 us
    pallas_call x3, Pallas kernels, weight_terms(): pl.pallas_call(partial(weight_kernel, [(len(lefts), len(rights)) for left...  49.8 us
    pallas_call x3, Pallas kernels, attention_backward(): pl.pallas_call(backward_kernel, grid=(count,), in_specs=[row_block(rows,...  35.6 us
    cond x90, local copies, waits for them, and re-layouts  28.6 us
    pallas_call x1, Pallas kernels, attention_forward(): pl.pallas_call(forward_kernel, grid=(4,), in_specs=[row_block(rows, model...  27.6 us
    convert_element_type x8, other arithmetic, add_low(): return sum((value.astype(f32) for value in values)).astype(bf16)  21.6 us
  transfers between devices with their start and end apart: 82, of which 41 were waited for; matrix products, arithmetic and copies ran while one was open for 13% of the time, Pallas kernels for 37%

profile of v3, /device:TPU:0, one launch (start us, length us, event | category | flops | bytes accessed | tf_op | source)
XLA Modules:
  0.0 592.9 jit_solution(11029864919991320003)
XLA Ops:
  28.3 76.0 %conditional.6 = (bf16[1024,2048]{1,0:T(8,128)(2,1)}, bf16[1024,2048]{1,0:T(8,128)(2,1)}, bf16[512,1152]{1,0:T(8,128)(2,1)}, bf16[512,1024]{1,0:T(8,128)(2,1)}, ...) conditional(s32[]{:T(128)} %bitcast.16, () %tuple.71, ...), branch_computations={%region_0.1_spmd, %region_1.5_spmd} | conditional | flops 22639580 | bytes 59183784 | solution.py:269
  30.7 21.9 %collective-permute-done.37 = bf16[256,2048]{1,0:T(8,128)(2,1)S(1)} collective-permute-done((bf16[256,2048]{1,0:T(8,128)(2,1)}, bf16[256,2048]{1,0:T(8,128)(2,1)S(1)}, u32[]{:S(2)}, u32[]{:S(2)}) %collective-permute-start.37) | collective-permute-done | bytes 1048608 | tf_op jit(solution)/shard_map/cond/branch_1_fun/ppermute | solution.py:26
  108.3 30.5 %conditional.7 = ((bf16[2,4,256,768]{3,2,1,0:T(8,128)(2,1)}, bf16[2,4,256,256]{3,2,1,0:T(8,128)(2,1)}, f32[4,4,512]{2,1,0:T(4,128)S(1)}, bf16[1024,2048]{1,0:T(8,128)(2,1)}, bf16[1024,2048]{1,0:T(8,128)(2,1)})) conditional(s32[]{:T(128)} %bitcast.16, () %tuple.70, (s32[]{:T(128)}, f32[3,1024]{1,0:T(4,128)}, bf16[1024,2048]{1,0:T(8,128)(2,1)}, ...), branch_computations={%region_5.6_spmd, %region_6.7_spmd} | conditional | flops 8589934592 | bytes 42070128 | solution.py:269
  111.2 27.6 %attention_forward.1 = (bf16[2,4,256,768]{3,2,1,0:T(8,128)(2,1)}, bf16[2,4,256,256]{3,2,1,0:T(8,128)(2,1)}, f32[4,4,512]{2,1,0:T(4,128)S(1)}, bf16[1024,2048]{1,0:T(8,128)(2,1)}, bf16[1024,2048]{1,0:T(8,128)(2,1)}) custom-call(bf16[1024,2048]{1,0:T(8,128)(2,1)} %get-tuple-element.183.core_ref, bf16[1024,2048]{1,0:T(8,128)(2,1)} %get-tuple-element.184.other_ref, ...), custom_call_target="tpu_custom_call" | custom-call | flops 8589934592 | bytes 33554432 | tf_op jit(solution)/shard_map/cond/branch_1_fun/attention_forward/pallas_call | solution.py:579
  138.9 109.0 %conditional.8 = (f32[256,2048]{1,0:T(8,128)S(1)}, bf16[1024,2048]{1,0:T(8,128)(2,1)}, bf16[1024,2048]{1,0:T(8,128)(2,1)}, bf16[1024,2048]{1,0:T(8,128)(2,1)}, bf16[1024,2048]{1,0:T(8,128)(2,1)}) conditional(s32[]{:T(128)} %bitcast.16, () %tuple.69, (bf16[1024,2048]{1,0:T(8,128)(2,1)}, bf16[1024,2048]{1,0:T(8,128)(2,1)}, bf16[256,2048]{1,0:T(8,128)(2,1)}, ...), branch_computations={%region_7.8_spmd, %region_8.9_spmd} | conditional | flops 8388608 | bytes 165675808 | solution.py:269
  157.7 8.0 %collective-permute-done.1 = bf16[128,2048]{1,0:T(8,128)(2,1)S(1)} collective-permute-done((bf16[128,2048]{1,0:T(8,128)(2,1)S(1)}, bf16[128,2048]{1,0:T(8,128)(2,1)S(1)}, u32[]{:S(2)}, u32[]{:S(2)}) %collective-permute-start.1) | collective-permute-done | bytes 524320 | tf_op jit(solution)/shard_map/cond/branch_1_fun/ppermute | solution.py:26
  171.5 22.5 %collective-permute-done.5.refs_3_ = bf16[256,2048]{1,0:T(8,128)(2,1)S(1)} collective-permute-done((bf16[256,2048]{1,0:T(8,128)(2,1)S(1)}, bf16[256,2048]{1,0:T(8,128)(2,1)S(1)}, u32[]{:S(2)}, u32[]{:S(2)}) %collective-permute-start.5) | collective-permute-done | bytes 1048608 | tf_op jit(solution)/shard_map/cond/branch_1_fun/ppermute | solution.py:26
  210.9 13.6 %collective-permute-done.7 = bf16[256,2048]{1,0:T(8,128)(2,1)S(1)} collective-permute-done((bf16[256,2048]{1,0:T(8,128)(2,1)}, bf16[256,2048]{1,0:T(8,128)(2,1)S(1)}, u32[]{:S(2)}, u32[]{:S(2)}) %collective-permute-start.7) | collective-permute-done | bytes 1048608 | tf_op jit(solution)/shard_map/cond/branch_1_fun/ppermute | solution.py:26
  249.2 24.4 %hidden_units.7 = (bf16[2,4,256,768]{3,2,1,0:T(8,128)(2,1)}, bf16[2,4,256,384]{3,2,1,0:T(8,128)(2,1)S(1)}, bf16[1024,2048]{1,0:T(8,128)(2,1)}, bf16[1024,2048]{1,0:T(8,128)(2,1)}) custom-call(bf16[1024,2048]{1,0:T(8,128)(2,1)} %get-tuple-element.503.refs_0_.refs_3_, bf16[1024,2048]{1,0:T(8,128)(2,1)} %get-tuple-element.504.refs_1_.refs_4_, ...), custom_call_target="tpu_custom_call" | custom-call | flops 16106127360 | bytes 33554432 | tf_op jit(solution)/shard_map/hidden_units/pallas_call | solution.py:725
  274.8 16.8 %weight_terms.5 = bf16[2048,1152]{1,0:T(8,128)(2,1)} custom-call(bf16[1024,2048]{1,0:T(8,128)(2,1)} %get-tuple-element.501.refs_2_.refs_0_, bf16[1024,2048]{1,0:T(8,128)(2,1)} %get-tuple-element.502.refs_3_.refs_1_, bf16[2,4,256,384]{3,2,1,0:T(8,128)(2,1)S(1)} %get-tuple-element.505.refs_2_, bf16[1024,2048]{1,0:T(8,128)(2,1)} %get-tuple-element.503.refs_0_.refs_3_, ...), custom_call_target="tpu_custom_call" | custom-call | tf_op jit(solution)/shard_map/weight_terms/pallas_call | solution.py:786
  291.6 99.3 %conditional.9 = (bf16[256,2048]{1,0:T(8,128)(2,1)}, bf16[256,2048]{1,0:T(8,128)(2,1)}, bf16[512,2048]{1,0:T(8,128)(2,1)}, bf16[512,2048]{1,0:T(8,128)(2,1)}, bf...) conditional(s32[]{:T(128)} %bitcast.16, () %tuple.78, ...), branch_computations={%region_10.11_spmd, %region_11.12_spmd} | conditional | flops 10747904000 | bytes 147849984 | solution.py:269
  291.7 10.0 %hidden_units.4 = (bf16[2,1,256,640]{3,2,1,0:T(8,128)(2,1)}, bf16[2,1,256,384]{3,2,1,0:T(8,128)(2,1)}, bf16[256,2048]{1,0:T(8,128)(2,1)}, bf16[256,2048]{1,0:T(8,128)(2,1)}) custom-call(bf16[1024,2048]{1,0:T(8,128)(2,1)} %get-tuple-element.239.refs_0_.refs_5_, bf16[1024,2048]{1,0:T(8,128)(2,1)} %get-tuple-element.240.refs_1_.refs_6_, ...), custom_call_target="tpu_custom_call" | custom-call | flops 2684354560 | bytes 8388608 | tf_op jit(solution)/shard_map/cond/branch_1_fun/hidden_units/pallas_call | solution.py:725
  308.6 14.5 %hidden_units.5 = (bf16[2,2,256,640]{3,2,1,0:T(8,128)(2,1)}, bf16[2,2,256,384]{3,2,1,0:T(8,128)(2,1)}, bf16[512,2048]{1,0:T(8,128)(2,1)}, bf16[512,2048]{1,0:T(8,128)(2,1)}) custom-call(bf16[1024,2048]{1,0:T(8,128)(2,1)} %get-tuple-element.239.refs_0_.refs_5_, bf16[1024,2048]{1,0:T(8,128)(2,1)} %get-tuple-element.240.refs_1_.refs_6_, ...), custom_call_target="tpu_custom_call" | custom-call | flops 5368709120 | bytes 16777216 | tf_op jit(solution)/shard_map/cond/branch_1_fun/hidden_units/pallas_call | solution.py:725
  333.4 9.9 %hidden_units.6 = (bf16[2,1,256,640]{3,2,1,0:T(8,128)(2,1)}, bf16[2,1,256,384]{3,2,1,0:T(8,128)(2,1)}, bf16[256,2048]{1,0:T(8,128)(2,1)}, bf16[256,2048]{1,0:T(8,128)(2,1)}) custom-call(bf16[1024,2048]{1,0:T(8,128)(2,1)} %get-tuple-element.239.refs_0_.refs_5_, bf16[1024,2048]{1,0:T(8,128)(2,1)} %get-tuple-element.240.refs_1_.refs_6_, ...), custom_call_target="tpu_custom_call" | custom-call | flops 2684354560 | bytes 8388608 | tf_op jit(solution)/shard_map/cond/branch_1_fun/hidden_units/pallas_call | solution.py:725
  343.3 8.5 %units_out.5 = (bf16[512,2048]{1,0:T(8,128)(2,1)}, bf16[512,2048]{1,0:T(8,128)(2,1)}) custom-call(bf16[2,4,256,384]{3,2,1,0:T(8,128)(2,1)S(1)} %copy-done.25, bf16[2,2,256,384]{3,2,1,0:T(8,128)(2,1)S(1)} %copy-done.5, bf16[2048,1152]{1,0:T(8,128)(2,1)} %get-tuple-element.231.first_weight_ref, bf16[2048,1024]{1,0:T(8,128)(2,1)} %get-tuple-element.214.refs_4_.second_weight_ref), custom_call_target="tpu_custom_call" | custom-call | tf_op jit(solution)/shard_map/cond/branch_1_fun/units_out/pallas_call | solution.py:808
  356.6 17.1 %weight_terms.3 = bf16[2048,1024]{1,0:T(8,128)(2,1)} custom-call(bf16[1024,2048]{1,0:T(8,128)(2,1)} %get-tuple-element.212.refs_2_.refs_0_, bf16[1024,2048]{1,0:T(8,128)(2,1)} %get-tuple-element.213.refs_3_.refs_1_, bf16[2,1,256,384]{3,2,1,0:T(8,128)(2,1)} %get-tuple-element.241.refs_2_.second_ref, ...), custom_call_target="tpu_custom_call" | custom-call | tf_op jit(solution)/shard_map/cond/branch_1_fun/weight_terms/pallas_call | solution.py:786
  391.7 93.9 %conditional.10 = (bf16[2048,1024]{1,0:T(8,128)(2,1)}, f32[1,768]{1,0:T(1,128)S(1)}, bf16[256,2048]{1,0:T(8,128)(2,1)}, bf16[256,2048]{1,0:T(8,128)(2,1)}, bf16[...) conditional(s32[]{:T(128)} %bitcast.16, () %tuple.77, ...), branch_computations={%region_12.13_spmd, %region_13.15_spmd} | conditional | flops 6450842112 | bytes 172136480 | solution.py:269
  398.7 10.2 %attention_backward.3 = (bf16[2,1,256,768]{3,2,1,0:T(8,128)(2,1)S(1)}, f32[1,1,768]{2,1,0:T(1,128)S(1)}, bf16[256,2048]{1,0:T(8,128)(2,1)}, bf16[256,2048]{1,0:T(8,128)(2,1)}) custom-call(bf16[256,2048]{1,0:T(8,128)(2,1)} %get-tuple-element.276.core_ref.refs_5_, bf16[256,2048]{1,0:T(8,128)(2,1)S(1)} %collective-permute-done.27.other_ref.refs_8_, ...), custom_call_target="tpu_custom_call" | custom-call | flops 2147483648 | bytes 8388608 | tf_op jit(solution)/shard_map/cond/branch_1_fun/attention_backward/pallas_call | solution.py:633
  427.6 16.2 %attention_backward.4 = (bf16[2,2,256,768]{3,2,1,0:T(8,128)(2,1)S(1)}, f32[2,1,768]{2,1,0:T(1,128)S(1)}, bf16[512,2048]{1,0:T(8,128)(2,1)}, bf16[512,2048]{1,0:T(8,128)(2,1)}) custom-call(bf16[512,2048]{1,0:T(8,128)(2,1)S(1)} %constant_dynamic-update-slice_fusion.15.core_ref.refs_6_, bf16[512,2048]{1,0:T(8,128)(2,1)} %copy-done.36, ...), custom_call_target="tpu_custom_call" | custom-call | flops 4294967296 | bytes 16777216 | tf_op jit(solution)/shard_map/cond/branch_1_fun/attention_backward/pallas_call | solution.py:633
  447.7 9.1 %attention_backward.5 = (bf16[2,1,256,768]{3,2,1,0:T(8,128)(2,1)S(1)}, f32[1,1,768]{2,1,0:T(1,128)S(1)}, bf16[256,2048]{1,0:T(8,128)(2,1)S(1)}, bf16[256,2048]{1,0:T(8,128)(2,1)}) custom-call(bf16[256,2048]{1,0:T(8,128)(2,1)S(1)} %constant_dynamic-update-slice_fusion.19.core_ref.refs_7_, bf16[256,2048]{1,0:T(8,128)(2,1)S(1)} %collective-permute-done.32.other_ref.refs_10_, ...), custom_call_target="tpu_custom_call" | custom-call | tf_op jit(solution)/shard_map/cond/branch_1_fun/attention_backward/pallas_call | solution.py:633
  461.6 16.0 %weight_terms.4 = bf16[2048,1024]{1,0:T(8,128)(2,1)} custom-call(bf16[1024,2048]{1,0:T(8,128)(2,1)} %get-tuple-element.272.refs_0_, bf16[1024,2048]{1,0:T(8,128)(2,1)} %get-tuple-element.273.refs_1_, bf16[2,1,256,768]{3,2,1,0:T(8,128)(2,1)} %copy-done.14, bf16[2,2,256,768]{3,2,1,0:T(8,128)(2,1)} %copy-done.6, bf16[2,1,256,768]{3,2,1,0:T(8,128)(2,1)} %copy-done.15, ...), custom_call_target="tpu_custom_call" | custom-call | tf_op jit(solution)/shard_map/cond/branch_1_fun/weight_terms/pallas_call | solution.py:786
  487.2 57.8 %conditional.11 = (bf16[256,2048]{1,0:T(8,128)(2,1)}, f32[256,2048]{1,0:T(8,128)}, bf16[128,1152]{1,0:T(8,128)(2,1)S(1)}, bf16[128,1152]{1,0:T(8,128)(2,1)}, bf1...) conditional(s32[]{:T(128)} %bitcast.16, () %tuple.68, ...), branch_computations={%region_15.16_spmd, %region_16.21_spmd} | conditional | flops 16843004 | bytes 44621416 | solution.py:269
  489.7 12.0 %collective-permute-done.55 = bf16[128,2048]{1,0:T(8,128)(2,1)S(1)} collective-permute-done((bf16[128,2048]{1,0:T(8,128)(2,1)}, bf16[128,2048]{1,0:T(8,128)(2,1)S(1)}, u32[]{:S(2)}, u32[]{:S(2)}) %collective-permute-start.55) | collective-permute-done | bytes 524320 | tf_op jit(solution)/shard_map/cond/branch_1_fun/ppermute | solution.py:26
  522.4 10.6 %collective-permute-done.54.refs_3_ = bf16[256,2048]{1,0:T(8,128)(2,1)} collective-permute-done((bf16[256,2048]{1,0:T(8,128)(2,1)}, bf16[256,2048]{1,0:T(8,128)(2,1)}, u32[]{:S(2)}, u32[]{:S(2)}) %collective-permute-start.54) | collective-permute-done | bytes 1048608 | tf_op jit(solution)/shard_map/cond/branch_1_fun/ppermute | solution.py:26
  (395 shorter events, 305.7 us)
Async XLA Ops:
  7.2 101.1 %all-gather.4.cloned.1.call-start = ((), (), s32[]{:S(2)}) async-start(), calls=%async_computation.3 | async-start | bytes 5242880 | tf_op jit(solution)/shard_map/all_gather | solution.py:273
  27.1 220.8 %all-gather.6.cloned.1.call-start = ((), (), s32[]{:S(2)}) async-start(), calls=%async_computation.4 | async-start | bytes 5898240 | tf_op jit(solution)/shard_map/all_gather | solution.py:273
  29.8 26.1 %collective-permute-start.38 = (bf16[256,2048]{1,0:T(8,128)(2,1)}, bf16[256,2048]{1,0:T(8,128)(2,1)S(1)}, u32[]{:S(2)}, u32[]{:S(2)}) collective-permute-start(bf16[256,2048]{1,0:T(8,128)(2,1)} %get-tuple-element.170), channel_id=1, source_target_pairs={{0,4},{4,0},{1,5},{5,1},{2,6},{6,2},{3,7},{7,3},{8,12},{12,8},{9,1... | collective-permute-start | bytes 3145736 | tf_op jit(solution)/shard_map/cond/branch_1_fun/ppermute | solution.py:26
  68.3 36.0 %collective-permute-start.41 = (bf16[1024,2048]{1,0:T(8,128)(2,1)}, bf16[1024,2048]{1,0:T(8,128)(2,1)}, u32[]{:S(2)}, u32[]{:S(2)}) collective-permute-start(bf16[1024,2048]{1,0:T(8,128)(2,1)} %constant_dynamic-update-slice_fusion), channel_id=1, source_target_pairs={{0,1},{1,0},{2,3},{3,2},{4,5},{5,4},{6,7},{7,6},{8,9},{9,8},{10,11... | collective-permute-start | bytes 12582920 | tf_op jit(solution)/shard_map/cond/branch_1_fun/ppermute | solution.py:26
  71.9 25.1 %collective-permute-start.42 = (bf16[128,1152]{1,0:T(8,128)(2,1)}, bf16[128,1152]{1,0:T(8,128)(2,1)}, u32[]{:S(2)}, u32[]{:S(2)}) collective-permute-start(bf16[128,1152]{1,0:T(8,128)(2,1)} %get-tuple-element.171), channel_id=1, source_target_pairs={{0,6},{2,4},{4,2},{6,0},{1,7},{3,5},{5,3},{7,1},{8,14},{10,12},{12... | collective-permute-start | bytes 884744 | tf_op jit(solution)/shard_map/cond/branch_1_fun/ppermute | solution.py:34
  104.4 187.3 %all-gather.8.cloned.1.call-start = ((), (), s32[]{:S(2)}) async-start(), calls=%async_computation.6 | async-start | bytes 5242880 | tf_op jit(solution)/shard_map/all_gather | solution.py:273
  105.1 286.0 %reduce-scatter.4.cloned.1.call-start = ((), (), s32[]{:S(2)}) async-start(), calls=%async_computation.5 | async-start | bytes 5898240 | tf_op jit(solution)/shard_map/reduce_scatter | solution.py:277
  105.2 33.7 %collective-permute-start.63 = (bf16[256,2048]{1,0:T(8,128)(2,1)}, bf16[256,2048]{1,0:T(8,128)(2,1)}, u32[]{:S(2)}, u32[]{:S(2)}) collective-permute-start(bf16[256,2048]{1,0:T(8,128)(2,1)} %param.27), channel_id=1, source_target_pairs={{0,2},{2,0},{1,3},{3,1},{4,6},{6,4},{5,7},{7,5},{8,10},{10,8},{9,1... | collective-permute-start | bytes 3145736 | tf_op jit(solution)/shard_map/ppermute | solution.py:26
  106.9 32.0 %collective-permute-start.64 = (bf16[256,2048]{1,0:T(8,128)(2,1)}, bf16[256,2048]{1,0:T(8,128)(2,1)}, u32[]{:S(2)}, u32[]{:S(2)}) collective-permute-start(bf16[256,2048]{1,0:T(8,128)(2,1)} %param.27), channel_id=1, source_target_pairs={{0,4},{4,0},{1,5},{5,1},{2,6},{6,2},{3,7},{7,3},{8,12},{12,8},{9,1... | collective-permute-start | bytes 3145736 | tf_op jit(solution)/shard_map/ppermute | solution.py:26
  203.8 25.9 %collective-permute-start.8 = (bf16[256,2048]{1,0:T(8,128)(2,1)S(1)}, bf16[256,2048]{1,0:T(8,128)(2,1)S(1)}, u32[]{:S(2)}, u32[]{:S(2)}) collective-permute-start(bf16[256,2048]{1,0:T(8,128)(2,1)S(1)} %copy-done.39), channel_id=1, source_target_pairs={{0,4},{4,0},{1,5},{5,1},{2,6},{6,2},{3,7},{7,3},{8,12},{12,8},{9,1... | collective-permute-start | bytes 3145736 | tf_op jit(solution)/shard_map/cond/branch_1_fun/ppermute | solution.py:26
  210.9 29.3 %collective-permute-start.12 = (bf16[1024,2048]{1,0:T(8,128)(2,1)}, bf16[1024,2048]{1,0:T(8,128)(2,1)}, u32[]{:S(2)}, u32[]{:S(2)}) collective-permute-start(bf16[1024,2048]{1,0:T(8,128)(2,1)} %constant_dynamic-update-slice_fusion.10), channel_id=1, source_target_pairs={{0,1},{1,0},{2,3},{3,2},{4,5},{5,4},{6,7},{7,6},{8,9},{9,8},{10,11... | collective-permute-start | bytes 12582920 | tf_op jit(solution)/shard_map/cond/branch_1_fun/ppermute | solution.py:26
  291.6 253.4 %reduce-scatter.8.cloned.1.call-start = ((), (), s32[]{:S(2)}) async-start(), calls=%async_computation.8 | async-start | bytes 5242880 | tf_op jit(solution)/shard_map/reduce_scatter | solution.py:277
  328.4 45.2 %collective-permute-start.19 = (bf16[256,2048]{1,0:T(8,128)(2,1)S(1)}, bf16[256,2048]{1,0:T(8,128)(2,1)}, u32[]{:S(2)}, u32[]{:S(2)}) collective-permute-start(bf16[256,2048]{1,0:T(8,128)(2,1)S(1)} %get-tuple-element.247), channel_id=1, source_target_pairs={{0,1},{1,0},{2,3},{3,2},{4,5},{5,4},{6,7},{7,6},{8,9},{9,8},{10,11... | collective-permute-start | bytes 3145736 | tf_op jit(solution)/shard_map/cond/branch_1_fun/ppermute | solution.py:26
  331.0 45.2 %collective-permute-start.17 = (bf16[256,2048]{1,0:T(8,128)(2,1)}, bf16[256,2048]{1,0:T(8,128)(2,1)}, u32[]{:S(2)}, u32[]{:S(2)}) collective-permute-start(bf16[256,2048]{1,0:T(8,128)(2,1)} %get-tuple-element.237), channel_id=1, source_target_pairs={{0,2},{2,0},{1,3},{3,1},{4,6},{6,4},{5,7},{7,5},{8,10},{10,8},{9,1... | collective-permute-start | bytes 3145736 | tf_op jit(solution)/shard_map/cond/branch_1_fun/ppermute | solution.py:26
  331.9 44.3 %collective-permute-start.18 = (bf16[256,2048]{1,0:T(8,128)(2,1)}, bf16[256,2048]{1,0:T(8,128)(2,1)}, u32[]{:S(2)}, u32[]{:S(2)}) collective-permute-start(bf16[256,2048]{1,0:T(8,128)(2,1)} %get-tuple-element.238), channel_id=1, source_target_pairs={{0,4},{4,0},{1,5},{5,1},{2,6},{6,2},{3,7},{7,3},{8,12},{12,8},{9,1... | collective-permute-start | bytes 3145736 | tf_op jit(solution)/shard_map/cond/branch_1_fun/ppermute | solution.py:26
  343.3 34.5 %collective-permute-start.22 = (bf16[256,2048]{1,0:T(8,128)(2,1)}, bf16[256,2048]{1,0:T(8,128)(2,1)}, u32[]{:S(2)}, u32[]{:S(2)}) collective-permute-start(bf16[256,2048]{1,0:T(8,128)(2,1)} %get-tuple-element.262), channel_id=1, source_target_pairs={{0,1},{1,0},{2,3},{3,2},{4,5},{5,4},{6,7},{7,6},{8,9},{9,8},{10,11... | collective-permute-start | bytes 3145736 | tf_op jit(solution)/shard_map/cond/branch_1_fun/ppermute | solution.py:26
  391.0 173.5 %reduce-scatter.6.cloned.1.call-start = ((), (), s32[]{:S(2)}) async-start(), calls=%async_computation.7 | async-start | bytes 5242880 | tf_op jit(solution)/shard_map/reduce_scatter | solution.py:277
  459.2 25.5 %collective-permute-start.35 = (bf16[256,2048]{1,0:T(8,128)(2,1)}, bf16[256,2048]{1,0:T(8,128)(2,1)}, u32[]{:S(2)}, u32[]{:S(2)}) collective-permute-start(bf16[256,2048]{1,0:T(8,128)(2,1)} %get-tuple-element.320), channel_id=1, source_target_pairs={{0,2},{2,0},{1,3},{3,1},{4,6},{6,4},{5,7},{7,5},{8,10},{10,8},{9,1... | collective-permute-start | bytes 3145736 | tf_op jit(solution)/shard_map/cond/branch_1_fun/ppermute | solution.py:26
  460.1 25.3 %collective-permute-start.36 = (bf16[256,2048]{1,0:T(8,128)(2,1)}, bf16[256,2048]{1,0:T(8,128)(2,1)}, u32[]{:S(2)}, u32[]{:S(2)}) collective-permute-start(bf16[256,2048]{1,0:T(8,128)(2,1)} %get-tuple-element.321), channel_id=1, source_target_pairs={{0,4},{4,0},{1,5},{5,1},{2,6},{6,2},{3,7},{7,3},{8,12},{12,8},{9,1... | collective-permute-start | bytes 3145736 | tf_op jit(solution)/shard_map/cond/branch_1_fun/ppermute | solution.py:26
  489.7 30.9 %collective-permute-start.51 = (bf16[256,2048]{1,0:T(8,128)(2,1)}, bf16[256,2048]{1,0:T(8,128)(2,1)}, u32[]{:S(2)}, u32[]{:S(2)}) collective-permute-start(bf16[256,2048]{1,0:T(8,128)(2,1)} %get-tuple-element.329), channel_id=1, source_target_pairs={{0,1},{1,0},{2,3},{3,2},{4,5},{5,4},{6,7},{7,6},{8,9},{9,8},{10,11... | collective-permute-start | bytes 3145736 | tf_op jit(solution)/shard_map/cond/branch_1_fun/ppermute | solution.py:26
  506.6 26.4 %collective-permute-start.54 = (bf16[256,2048]{1,0:T(8,128)(2,1)}, bf16[256,2048]{1,0:T(8,128)(2,1)}, u32[]{:S(2)}, u32[]{:S(2)}) collective-permute-start(bf16[256,2048]{1,0:T(8,128)(2,1)} %get-tuple-element.789), channel_id=1, source_target_pairs={{0,2},{2,0},{1,3},{3,1},{4,6},{6,4},{5,7},{7,5},{8,10},{10,8},{9,1... | collective-permute-start | bytes 3145736 | tf_op jit(solution)/shard_map/cond/branch_1_fun/ppermute | solution.py:26
  507.5 26.4 %collective-permute-start.56 = (bf16[256,2048]{1,0:T(8,128)(2,1)}, bf16[256,2048]{1,0:T(8,128)(2,1)}, u32[]{:S(2)}, u32[]{:S(2)}) collective-permute-start(bf16[256,2048]{1,0:T(8,128)(2,1)} %get-tuple-element.788), channel_id=1, source_target_pairs={{0,4},{4,0},{1,5},{5,1},{2,6},{6,2},{3,7},{7,3},{8,12},{12,8},{9,1... | collective-permute-start | bytes 3145736 | tf_op jit(solution)/shard_map/cond/branch_1_fun/ppermute | solution.py:26
  509.1 31.9 %collective-permute-start.57 = (bf16[128,1152]{1,0:T(8,128)(2,1)S(1)}, bf16[128,1152]{1,0:T(8,128)(2,1)}, u32[]{:S(2)}, u32[]{:S(2)}) collective-permute-start(bf16[128,1152]{1,0:T(8,128)(2,1)S(1)} %get-tuple-element.339), channel_id=1, source_target_pairs={{0,2},{2,0},{1,3},{3,1},{4,6},{6,4},{5,7},{7,5},{8,10},{10,8},{9,1... | collective-permute-start | bytes 884744 | tf_op jit(solution)/shard_map/cond/branch_1_fun/ppermute | solution.py:26
  510.2 33.5 %collective-permute-start.58 = (bf16[128,1152]{1,0:T(8,128)(2,1)S(1)}, bf16[128,1152]{1,0:T(8,128)(2,1)}, u32[]{:S(2)}, u32[]{:S(2)}) collective-permute-start(bf16[128,1152]{1,0:T(8,128)(2,1)S(1)} %get-tuple-element.340), channel_id=1, source_target_pairs={{0,4},{4,0},{1,5},{5,1},{2,6},{6,2},{3,7},{7,3},{8,12},{12,8},{9,1... | collective-permute-start | bytes 884744 | tf_op jit(solution)/shard_map/cond/branch_1_fun/ppermute | solution.py:26
  (116 other events, 1546.2 us)
Sparse Core Ops, SparseCore 0:
  27.2 81.0 all-gather.3
  110.4 87.9 all-gather.5
  200.6 79.2 all-gather.7
  291.7 84.2 reduce-scatter.3
  391.1 76.1 reduce-scatter.7
  485.8 76.1 reduce-scatter.5

commit v4 on v3

--- a/solution.py
+++ b/solution.py
@@ -164,7 +164,7 @@
         in_specs=[pl.BlockSpec(memory_space=pltpu.SMEM)] + [vmem] * len(operands),
         out_specs=[vmem] * len(outs),
         out_shape=[jax.ShapeDtypeStruct(*out) for out in outs],
-        compiler_params=pltpu.CompilerParams(vmem_limit_bytes=32 << 20),
+        compiler_params=pltpu.CompilerParams(vmem_limit_bytes=16 << 20),
         cost_estimate=LIGHT,
         name=name,
     )(place().reshape(1), *operands)
@@ -281,16 +281,19 @@
     return jnp.stack(exchange([values] * 4))
 
 
+def sum_steps(values, axis, first=0, last=None):
+    size = lax.axis_size(axis)
+    if size & (size - 1):
+        return lax.psum(values, axis) if first == 0 else values
+    for i in range(size.bit_length() - 1)[first:last]:
+        pairs = [(j, j ^ (1 << i)) for j in range(size)]
+        values = values + lax.ppermute(values, axis, pairs)
+    return values
+
+
 def sum_over(values, axes):
     for axis in axes:
-        size = lax.axis_size(axis)
-        if size & (size - 1):
-            values = lax.psum(values, axis)
-            continue
-        step = 1
-        while step < size:
-            values = values + lax.ppermute(values, axis, [(i, i ^ step) for i in range(size)])
-            step *= 2
+        values = sum_steps(values, axis)
     return values
 
 
@@ -375,6 +378,7 @@
         in_specs=[of_rows] * (1 + len(parts)) + [of_gain] * 2,
         out_specs=[of_rows] * len(kinds),
         out_shape=[jax.ShapeDtypeStruct((rows, width), kind) for kind in kinds],
+        compiler_params=pltpu.CompilerParams(vmem_limit_bytes=12 << 20),
         cost_estimate=LIGHT,
         name="norm_rows",
     )(tokens, *parts, gain[None], shift[None])
@@ -416,6 +420,7 @@
         out_specs=halves_specs(block, width, rows // block)
         + [of_rows, pl.BlockSpec((2, width), lambda i: (0, 0))],
         out_shape=halves_shapes(rows, width) + [shape((rows, width), f32), shape((2, width), f32)],
+        compiler_params=pltpu.CompilerParams(vmem_limit_bytes=12 << 20),
         cost_estimate=LIGHT,
         name="norm_back",
     )(*summands, *parts, gain[None], past)
@@ -605,7 +610,7 @@
             shape((4 * rows, model_width), bf16),
         ],
         scratch_shapes=[pltpu.VMEM((group, 3 * width), f32)],
-        compiler_params=pltpu.CompilerParams(vmem_limit_bytes=48 << 20),
+        compiler_params=pltpu.CompilerParams(vmem_limit_bytes=24 << 20),
         cost_estimate=pl.CostEstimate(
             flops=16 * group * model_width * width * 2, bytes_accessed=32 << 20, transcendentals=4 << 20
         ),
@@ -658,7 +663,7 @@
             shape((count * rows, model_width), bf16),
         ],
         scratch_shapes=[pltpu.VMEM((group, width), f32)],
-        compiler_params=pltpu.CompilerParams(vmem_limit_bytes=48 << 20),
+        compiler_params=pltpu.CompilerParams(vmem_limit_bytes=24 << 20),
         cost_estimate=LIGHT
         if first == 3
         else pl.CostEstimate(
@@ -733,7 +738,7 @@
             shape((count * rows, model_width), bf16),
             shape((count * rows, model_width), bf16),
         ],
-        compiler_params=pltpu.CompilerParams(vmem_limit_bytes=56 << 20),
+        compiler_params=pltpu.CompilerParams(vmem_limit_bytes=28 << 20),
         cost_estimate=pl.CostEstimate(
             flops=4 * count * rows * model_width * 5 * main,
             bytes_accessed=8 * count << 20,
@@ -789,7 +794,7 @@
         in_specs=specs,
         out_specs=pl.BlockSpec((block, total), lambda i: (i, 0)),
         out_shape=jax.ShapeDtypeStruct((model_width, total), bf16),
-        compiler_params=pltpu.CompilerParams(vmem_limit_bytes=60 << 20),
+        compiler_params=pltpu.CompilerParams(vmem_limit_bytes=20 << 20),
         cost_estimate=LIGHT,
         name="weight_terms",
     )(*operands)
@@ -815,7 +820,7 @@
         + [whole_block(model_width, hidden.shape[-1]) for hidden in hiddens],
         out_specs=[row_block(rows, model_width)] * 2,
         out_shape=[jax.ShapeDtypeStruct((count * rows, model_width), bf16)] * 2,
-        compiler_params=pltpu.CompilerParams(vmem_limit_bytes=48 << 20),
+        compiler_params=pltpu.CompilerParams(vmem_limit_bytes=14 << 20),
         cost_estimate=LIGHT,
         name="units_out",
     )(*hiddens, *weights)
@@ -942,15 +947,16 @@
         own = run(xs, 0, 1)
         own_others = swap(own[3], TP)
         units = own, sides, last
+        mlp_own, mlp_sides = out(own[1], 0), out(sides[1], 1)
+        mlp_cores = add_halves(mlp_last[0], swap(mlp_last[1], TP))
+        near, mid, mlp_cores, mlp_own, mlp_sides, units = lax.optimization_barrier(
+            (near, mid, mlp_cores, mlp_own, mlp_sides, units)
+        )
+        mlp_middle = scatter_middle(*mlp_cores)
         terms_b = weight_terms(
             (spread_dy, [u[1] for u in units]), (spread2, [u[0] for u in units])
         )
-        mlp_own, mlp_sides = out(own[1], 0), out(sides[1], 1)
-        mlp_cores = add_halves(mlp_last[0], swap(mlp_last[1], TP))
-        near, mid, terms_b, mlp_cores, mlp_own, mlp_sides = lax.optimization_barrier(
-            (near, mid, terms_b, mlp_cores, mlp_own, mlp_sides)
-        )
-        mlp_middle = scatter_middle(*mlp_cores)
+        mlp_middle, terms_b, near, mid = lax.optimization_barrier((mlp_middle, terms_b, near, mid))
         parts = own[2], own_others, near, mid
         *d_low, d_residual, norm2_grads = norm_back(
             (tokens, attn_out), parts, ln2_gain, cotangent
@@ -963,7 +969,7 @@
     grads_a, d_low = lax.optimization_barrier((grads_a, d_low))
     grads_b = scatter_far(terms_b)
 
-    def attend_back(terms_b, d_low, attn_full, qkv, log_totals, tree_info, spread1, context, mlp):
+    def attend_back(terms_b, d_low, attn_full, qkv, log_totals, tree_info, spread1, context, mlp, grads_a):
         mlp_own, mlp_sides, mlp_middle = mlp
 
         def back(cores, first, count):
@@ -978,10 +984,14 @@
         diagonal = halves_diagonal(state)
         sides = joined(state)
         sides_back = back(sides, 1, 2)
-        diagonal, sides_back, near, mid = lax.optimization_barrier((diagonal, sides_back, near, mid))
-        mlp_parts = swap(near, NEAR), swap(mid, MID)
+        diagonal, sides_back, near, mid, grads_a = lax.optimization_barrier(
+            (diagonal, sides_back, near, mid, grads_a)
+        )
+        pieces_a = returned(grads_a)
         last = joined(diagonal)
         last_back = back(last, 3, 1)
+        last_back, pieces_a, near, mid = lax.optimization_barrier((last_back, pieces_a, near, mid))
+        mlp_parts = swap(near, NEAR), swap(mid, MID)
         backs = own_back, sides_back, last_back
         terms = weight_terms(
             (spread1, [back[0] for back in backs]), (row_pieces(own, sides, last), (context,))
@@ -989,19 +999,21 @@
         low, high = add_halves(last_back[2], swap(last_back[3], TP))
         bias_terms = sum(jnp.sum(back[1], axis=0) for back in backs)
         d_normed1 = own_back[2:], sides_back[2:], (low, high)
-        return terms, bias_terms, d_normed1, (mlp_own[0], mlp_others[0], *mlp_parts)
-
-    attn_terms, bias_terms, d_normed1, mlp_parts = stage(
-        always, attend_back, terms_b, d_low, attn_full, qkv, log_totals, tree_info, spread1, context, mlp
+        return terms, bias_terms, d_normed1, (mlp_own[0], mlp_others[0], *mlp_parts), pieces_a
+
+    attn_terms, bias_terms, d_normed1, mlp_parts, pieces_a = stage(
+        always, attend_back, terms_b, d_low, attn_full, qkv, log_totals, tree_info, spread1, context, mlp, grads_a
     )
     attn_grads = scatter_far(attn_terms)
 
-    def finish(attn_terms, d_normed1, mlp_parts, grads_a, d_residual, attn_out, tokens, bias_terms, norm2_grads, own_valid):
+    def finish(attn_terms, d_normed1, mlp_parts, grads_b, d_residual, attn_out, tokens, bias_terms, norm2_grads, own_valid):
         own, sides, last = d_normed1
         middle = scatter_middle(*last)
         own_others, sides_others = swap(own[1], TP), swap(sides[1], TP)
-        pieces_a = returned(grads_a)
-        parts = own[0], own_others, *scatter_end(sides[0], sides_others, 0, middle)
+        from_sides = scatter_end(sides[0], sides_others, 0, middle)
+        from_sides, grads_b = lax.optimization_barrier((from_sides, grads_b))
+        pieces_b = returned(grads_b)
+        parts = own[0], own_others, *from_sides
         *_, tokens_grad, norm1_grads = norm_back((tokens,), parts, ln1_gain, d_residual)
         mlp_out = sum(part.astype(f32) for part in mlp_parts)
         stream_out = tokens.astype(f32) + attn_out + mlp_out
@@ -1022,25 +1034,27 @@
         sums = jnp.concatenate(
             [norm1_grads, norm2_grads, bias_spread, jnp.pad(squares, (0, model_width - 4))[None]]
         )
-        return output, tokens_grad, pieces_a, sums
-
-    output, tokens_grad, pieces_a, sums = stage(
-        always, finish, attn_terms, d_normed1, mlp_parts, grads_a, d_residual, attn_out, tokens, bias_terms, norm2_grads, own_valid
-    )
-    pieces_b = returned(after(grads_b, sums))
-    sums = sum_over(sums, (TP, NEAR, MID))
-    attn_grads, sums, pieces_b = lax.optimization_barrier((attn_grads, sums, pieces_b))
+        return output, tokens_grad, pieces_b, sum_over(sums, (TP,))
+
+    output, tokens_grad, pieces_b, sums = stage(
+        always, finish, attn_terms, d_normed1, mlp_parts, grads_b, d_residual, attn_out, tokens, bias_terms, norm2_grads, own_valid
+    )
+    sums = sum_over(sums, (NEAR, MID))
+    far_sums = sum_steps(sums, FAR, 0, 1)
     gate_up_grad, down_grad = on_place(
         unpack_units_kernel,
         "unpack_units",
         (*pieces_a, *pieces_b),
         [(w_gate_up.shape, f32), (w_down.shape, f32)],
     )
-    sums = sum_over(sums, (FAR,))
+    sums, gate_up_grad, down_grad = lax.optimization_barrier((far_sums, gate_up_grad, down_grad))
+    sums = sum_steps(sums, FAR, 1)
+    attn_grads, sums = lax.optimization_barrier((attn_grads, sums))
+    attn_pieces = returned(attn_grads)
     qkv_grad, out_grad = on_place(
         unpack_heads_kernel,
         "unpack_heads",
-        returned(attn_grads),
+        attn_pieces,
         [((3, weight_rows, local_width), f32), (w_out.shape, f32)],
     )
     qkv_grad = qkv_grad.transpose(1, 0, 2)

time: 600 us -> 578 us (0.963)
  Pallas kernels: 222 us -> 204 us
    pallas_call x3, Pallas kernels: 49.8 us -> 43.6 us  [weight_terms(): pl.pallas_call(partial(weight_kernel, [(len(lefts), len(rights)) for left...]
    pallas_call x4, Pallas kernels: 58.8 us -> 52.7 us  [hidden_units(): pl.pallas_call(partial(units_kernel, parts), grid=(count,), in_specs=[giv...]
    cond x90 -> x80, local copies, waits for them, and re-layouts: 28.6 us -> 33.1 us
  transfers between devices with their start and end apart: 82 -> 82, of which waited for: 41 -> 43; matrix products, arithmetic and copies ran while one was open for 13% -> 12% of each run, Pallas kernels for 37% -> 35%
where the time goes in v4:
time: 578 us; the launch traced here: 571 us
  Pallas kernels  204 us (35%)
  waiting for transfers between devices  183 us (32%)
  starting transfers between devices  74.4 us (13%)
  local copies, waits for them, and re-layouts  51.1 us (9%)
  other arithmetic  40.6 us (7%)
  between operations  16.2 us (3%)
    ppermute x64, waiting for transfers between devices, swap(): return lax.ppermute(values, axis, [(0, 1), (1, 0)])  160 us
    ppermute x64, starting transfers between devices, swap(): return lax.ppermute(values, axis, [(0, 1), (1, 0)])  57.7 us
    pallas_call x4, Pallas kernels, hidden_units(): pl.pallas_call(partial(units_kernel, parts), grid=(count,), in_specs=[giv...  52.7 us
    pallas_call x3, Pallas kernels, weight_terms(): pl.pallas_call(partial(weight_kernel, [(len(lefts), len(rights)) for left...  43.6 us
    pallas_call x3, Pallas kernels, attention_backward(): pl.pallas_call(backward_kernel, grid=(count,), in_specs=[row_block(rows,...  37.8 us
    cond x80, local copies, waits for them, and re-layouts  33.1 us
    pallas_call x1, Pallas kernels, attention_forward(): pl.pallas_call(forward_kernel, grid=(4,), in_specs=[row_block(rows, model...  27.6 us
    convert_element_type x8, other arithmetic, add_low(): return sum((value.astype(f32) for value in values)).astype(bf16)  16.4 us
  transfers between devices with their start and end apart: 82, of which 43 were waited for; matrix products, arithmetic and copies ran while one was open for 12% of the time, Pallas kernels for 35%

profile of v4, /device:TPU:0, one launch (start us, length us, event | category | flops | bytes accessed | tf_op | source)
XLA Modules:
  0.0 571.3 jit_solution(919246839041987218)
XLA Ops:
  28.3 75.7 %conditional.6 = (bf16[1024,2048]{1,0:T(8,128)(2,1)}, bf16[1024,2048]{1,0:T(8,128)(2,1)}, bf16[512,1152]{1,0:T(8,128)(2,1)}, bf16[512,1024]{1,0:T(8,128)(2,1)}, ...) conditional(s32[]{:T(128)} %bitcast.17, () %tuple.74, ...), branch_computations={%region_0.1_spmd, %region_1.5_spmd} | conditional | flops 22639580 | bytes 59183784 | solution.py:269
  30.7 22.0 %collective-permute-done.40 = bf16[256,2048]{1,0:T(8,128)(2,1)S(1)} collective-permute-done((bf16[256,2048]{1,0:T(8,128)(2,1)}, bf16[256,2048]{1,0:T(8,128)(2,1)S(1)}, u32[]{:S(2)}, u32[]{:S(2)}) %collective-permute-start.40) | collective-permute-done | bytes 1048608 | tf_op jit(solution)/shard_map/cond/branch_1_fun/ppermute | solution.py:26
  108.3 30.5 %conditional.7 = ((bf16[2,4,256,768]{3,2,1,0:T(8,128)(2,1)}, bf16[2,4,256,256]{3,2,1,0:T(8,128)(2,1)}, f32[4,4,512]{2,1,0:T(4,128)S(1)}, bf16[1024,2048]{1,0:T(8,128)(2,1)}, bf16[1024,2048]{1,0:T(8,128)(2,1)})) conditional(s32[]{:T(128)} %bitcast.17, () %tuple.73, (s32[]{:T(128)}, f32[3,1024]{1,0:T(4,128)}, bf16[1024,2048]{1,0:T(8,128)(2,1)}, ...), branch_computations={%region_5.6_spmd, %region_6.7_spmd} | conditional | flops 8589934592 | bytes 42070128 | solution.py:269
  111.2 27.6 %attention_forward.1 = (bf16[2,4,256,768]{3,2,1,0:T(8,128)(2,1)}, bf16[2,4,256,256]{3,2,1,0:T(8,128)(2,1)}, f32[4,4,512]{2,1,0:T(4,128)S(1)}, bf16[1024,2048]{1,0:T(8,128)(2,1)}, bf16[1024,2048]{1,0:T(8,128)(2,1)}) custom-call(bf16[1024,2048]{1,0:T(8,128)(2,1)} %get-tuple-element.185.core_ref, bf16[1024,2048]{1,0:T(8,128)(2,1)} %get-tuple-element.186.other_ref, ...), custom_call_target="tpu_custom_call" | custom-call | flops 8589934592 | bytes 33554432 | tf_op jit(solution)/shard_map/cond/branch_1_fun/attention_forward/pallas_call | solution.py:584
  138.9 104.4 %conditional.8 = (f32[256,2048]{1,0:T(8,128)}, bf16[1024,2048]{1,0:T(8,128)(2,1)}, bf16[1024,2048]{1,0:T(8,128)(2,1)}, bf16[1024,2048]{1,0:T(8,128)(2,1)}, bf16[1024,2048]{1,0:T(8,128)(2,1)}) conditional(s32[]{:T(128)} %bitcast.17, () %tuple.72, (bf16[1024,2048]{1,0:T(8,128)(2,1)}, bf16[1024,2048]{1,0:T(8,128)(2,1)}, bf16[256,2048]{1,0:T(8,128)(2,1)}, ...), branch_computations={%region_7.8_spmd, %region_8.9_spmd} | conditional | flops 8388608 | bytes 132121192 | solution.py:269
  157.7 8.0 %collective-permute-done.1 = bf16[128,2048]{1,0:T(8,128)(2,1)S(1)} collective-permute-done((bf16[128,2048]{1,0:T(8,128)(2,1)S(1)}, bf16[128,2048]{1,0:T(8,128)(2,1)S(1)}, u32[]{:S(2)}, u32[]{:S(2)}) %collective-permute-start.1) | collective-permute-done | bytes 524320 | tf_op jit(solution)/shard_map/cond/branch_1_fun/ppermute | solution.py:26
  171.5 22.5 %collective-permute-done.5.refs_3_ = bf16[256,2048]{1,0:T(8,128)(2,1)S(1)} collective-permute-done((bf16[256,2048]{1,0:T(8,128)(2,1)S(1)}, bf16[256,2048]{1,0:T(8,128)(2,1)S(1)}, u32[]{:S(2)}, u32[]{:S(2)}) %collective-permute-start.5) | collective-permute-done | bytes 1048608 | tf_op jit(solution)/shard_map/cond/branch_1_fun/ppermute | solution.py:26
  206.3 15.0 %collective-permute-done.7 = bf16[256,2048]{1,0:T(8,128)(2,1)S(1)} collective-permute-done((bf16[256,2048]{1,0:T(8,128)(2,1)S(1)}, bf16[256,2048]{1,0:T(8,128)(2,1)S(1)}, u32[]{:S(2)}, u32[]{:S(2)}) %collective-permute-start.7) | collective-permute-done | bytes 1048608 | tf_op jit(solution)/shard_map/cond/branch_1_fun/ppermute | solution.py:26
  235.6 7.5 %collective-permute-done.11 = bf16[1024,2048]{1,0:T(8,128)(2,1)} collective-permute-done((bf16[1024,2048]{1,0:T(8,128)(2,1)}, bf16[1024,2048]{1,0:T(8,128)(2,1)}, u32[]{:S(2)}, u32[]{:S(2)}) %collective-permute-start.11) | collective-permute-done | bytes 4194336 | tf_op jit(solution)/shard_map/cond/branch_1_fun/ppermute | solution.py:26
  243.3 24.4 %hidden_units.7 = (bf16[2,4,256,768]{3,2,1,0:T(8,128)(2,1)S(1)}, bf16[2,4,256,384]{3,2,1,0:T(8,128)(2,1)S(1)}, bf16[1024,2048]{1,0:T(8,128)(2,1)}, bf16[1024,2048]{1,0:T(8,128)(2,1)}) custom-call(bf16[1024,2048]{1,0:T(8,128)(2,1)} %get-tuple-element.532.refs_0_.refs_3_, bf16[1024,2048]{1,0:T(8,128)(2,1)} %get-tuple-element.533.refs_1_.refs_4_, ...), custom_call_target="tpu_custom_call" | custom-call | flops 16106127360 | bytes 33554432 | tf_op jit(solution)/shard_map/hidden_units/pallas_call | solution.py:730
  267.6 14.3 %weight_terms.5 = bf16[2048,1152]{1,0:T(8,128)(2,1)S(1)} custom-call(bf16[1024,2048]{1,0:T(8,128)(2,1)} %get-tuple-element.530.refs_2_.refs_0_, bf16[1024,2048]{1,0:T(8,128)(2,1)} %get-tuple-element.531.refs_3_.refs_1_, bf16[2,4,256,384]{3,2,1,0:T(8,128)(2,1)S(1)} %get-tuple-element.534.refs_2_, bf16[1024,2048]{1,0:T(8,128)(2,1)} %get-tuple-element.532.refs_0_.refs_3_, ...), custom_call_target="tpu_custom_call" | custom-call | tf_op jit(solution)/shard_map/weight_terms/pallas_call | solution.py:791
  284.2 82.1 %conditional.9 = (bf16[256,2048]{1,0:T(8,128)(2,1)}, bf16[256,2048]{1,0:T(8,128)(2,1)}, bf16[512,2048]{1,0:T(8,128)(2,1)}, bf16[512,2048]{1,0:T(8,128)(2,1)}, bf...) conditional(s32[]{:T(128)} %bitcast.17, () %tuple.81, ...), branch_computations={%region_10.11_spmd, %region_11.12_spmd} | conditional | flops 10747904000 | bytes 153617024 | solution.py:269
  284.2 9.0 %hidden_units.4 = (bf16[2,1,256,640]{3,2,1,0:T(8,128)(2,1)S(1)}, bf16[2,1,256,384]{3,2,1,0:T(8,128)(2,1)S(1)}, bf16[256,2048]{1,0:T(8,128)(2,1)S(1)}, bf16[256,2048]{1,0:T(8,128)(2,1)S(1)}) custom-call(bf16[1024,2048]{1,0:T(8,128)(2,1)} %get-tuple-element.243.refs_0_.refs_5_, bf16[1024,2048]{1,0:T(8,128)(2,1)} %get-tuple-element.244.refs_1_.refs_6_, ...), custom_call_target="tpu_custom_call" | custom-call | flops 2684354560 | bytes 8388608 | tf_op jit(solution)/shard_map/cond/branch_1_fun/hidden_units/pallas_call | solution.py:730
  298.4 12.4 %hidden_units.5 = (bf16[2,2,256,640]{3,2,1,0:T(8,128)(2,1)S(1)}, bf16[2,2,256,384]{3,2,1,0:T(8,128)(2,1)S(1)}, bf16[512,2048]{1,0:T(8,128)(2,1)S(1)}, bf16[512,2048]{1,0:T(8,128)(2,1)S(1)}) custom-call(bf16[1024,2048]{1,0:T(8,128)(2,1)} %get-tuple-element.243.refs_0_.refs_5_, bf16[1024,2048]{1,0:T(8,128)(2,1)} %get-tuple-element.244.refs_1_.refs_6_, ...), custom_call_target="tpu_custom_call" | custom-call | flops 5368709120 | bytes 16777216 | tf_op jit(solution)/shard_map/cond/branch_1_fun/hidden_units/pallas_call | solution.py:730
  319.1 7.0 %hidden_units.6 = (bf16[2,1,256,640]{3,2,1,0:T(8,128)(2,1)S(1)}, bf16[2,1,256,384]{3,2,1,0:T(8,128)(2,1)S(1)}, bf16[256,2048]{1,0:T(8,128)(2,1)S(1)}, bf16[256,2048]{1,0:T(8,128)(2,1)S(1)}) custom-call(bf16[1024,2048]{1,0:T(8,128)(2,1)} %get-tuple-element.243.refs_0_.refs_5_, bf16[1024,2048]{1,0:T(8,128)(2,1)} %get-tuple-element.244.refs_1_.refs_6_, ...), custom_call_target="tpu_custom_call" | custom-call | flops 2684354560 | bytes 8388608 | tf_op jit(solution)/shard_map/cond/branch_1_fun/hidden_units/pallas_call | solution.py:730
  345.1 15.6 %weight_terms.3 = bf16[2048,1024]{1,0:T(8,128)(2,1)} custom-call(bf16[1024,2048]{1,0:T(8,128)(2,1)} %get-tuple-element.214.refs_2_.refs_0_, bf16[1024,2048]{1,0:T(8,128)(2,1)} %get-tuple-element.215.refs_3_.refs_1_, bf16[2,1,256,384]{3,2,1,0:T(8,128)(2,1)S(1)} %get-tuple-element.262.second_ref.refs_2_, ...), custom_call_target="tpu_custom_call" | custom-call | tf_op jit(solution)/shard_map/cond/branch_1_fun/weight_terms/pallas_call | solution.py:791
  368.5 98.9 %conditional.10 = (bf16[2048,1024]{1,0:T(8,128)(2,1)}, f32[1,768]{1,0:T(1,128)}, bf16[256,2048]{1,0:T(8,128)(2,1)}, bf16[256,2048]{1,0:T(8,128)(2,1)}, bf16[512,...) conditional(s32[]{:T(128)} %bitcast.17, () %tuple.80, ...), branch_computations={%region_12.13_spmd, %region_13.15_spmd} | conditional | flops 6450842112 | bytes 200808800 | solution.py:269
  375.5 11.1 %attention_backward.3 = (bf16[2,1,256,768]{3,2,1,0:T(8,128)(2,1)S(1)}, f32[1,1,768]{2,1,0:T(1,128)S(1)}, bf16[256,2048]{1,0:T(8,128)(2,1)}, bf16[256,2048]{1,0:T(8,128)(2,1)}) custom-call(bf16[256,2048]{1,0:T(8,128)(2,1)} %get-tuple-element.288.core_ref.refs_5_, bf16[256,2048]{1,0:T(8,128)(2,1)S(1)} %collective-permute-done.27.other_ref.refs_8_, ...), custom_call_target="tpu_custom_call" | custom-call | flops 2147483648 | bytes 8388608 | tf_op jit(solution)/shard_map/cond/branch_1_fun/attention_backward/pallas_call | solution.py:638
  403.5 16.5 %attention_backward.4 = (bf16[2,2,256,768]{3,2,1,0:T(8,128)(2,1)S(1)}, f32[2,1,768]{2,1,0:T(1,128)S(1)}, bf16[512,2048]{1,0:T(8,128)(2,1)}, bf16[512,2048]{1,0:T(8,128)(2,1)}) custom-call(bf16[512,2048]{1,0:T(8,128)(2,1)S(1)} %constant_dynamic-update-slice_fusion.15.core_ref.refs_6_, bf16[512,2048]{1,0:T(8,128)(2,1)S(1)} %collective-permute-done.31.other_ref.refs_9_, ...), custom_call_target="tpu_custom_call" | custom-call | flops 4294967296 | bytes 16777216 | tf_op jit(solution)/shard_map/cond/branch_1_fun/attention_backward/pallas_call | solution.py:638
  426.2 10.3 %attention_backward.5 = (bf16[2,1,256,768]{3,2,1,0:T(8,128)(2,1)S(1)}, f32[1,1,768]{2,1,0:T(1,128)S(1)}, bf16[256,2048]{1,0:T(8,128)(2,1)S(1)}, bf16[256,2048]{1,0:T(8,128)(2,1)}) custom-call(bf16[256,2048]{1,0:T(8,128)(2,1)S(1)} %constant_dynamic-update-slice_fusion.19.core_ref.refs_7_, bf16[256,2048]{1,0:T(8,128)(2,1)} %collective-permute-done.32.other_ref.refs_10_, ...), custom_call_target="tpu_custom_call" | custom-call | tf_op jit(solution)/shard_map/cond/branch_1_fun/attention_backward/pallas_call | solution.py:638
  450.3 13.7 %weight_terms.4 = bf16[2048,1024]{1,0:T(8,128)(2,1)} custom-call(bf16[1024,2048]{1,0:T(8,128)(2,1)} %get-tuple-element.284.refs_0_, bf16[1024,2048]{1,0:T(8,128)(2,1)} %get-tuple-element.285.refs_1_, bf16[2,1,256,768]{3,2,1,0:T(8,128)(2,1)S(1)} %copy-done.14, bf16[2,2,256,768]{3,2,1,0:T(8,128)(2,1)S(1)} %copy-done.8, ...), custom_call_target="tpu_custom_call" | custom-call | tf_op jit(solution)/shard_map/cond/branch_1_fun/weight_terms/pallas_call | solution.py:791
  468.2 58.3 %conditional.11 = (bf16[256,2048]{1,0:T(8,128)(2,1)}, f32[256,2048]{1,0:T(8,128)}, bf16[128,1024]{1,0:T(8,128)(2,1)}, bf16[128,1024]{1,0:T(8,128)(2,1)}, bf16[12...) conditional(s32[]{:T(128)} %bitcast.17, () %tuple.71, ...), branch_computations={%region_16.17_spmd, %region_17.22_spmd} | conditional | flops 16859388 | bytes 53108452 | solution.py:269
  469.9 12.8 %collective-permute-done.58 = bf16[128,2048]{1,0:T(8,128)(2,1)S(1)} collective-permute-done((bf16[128,2048]{1,0:T(8,128)(2,1)}, bf16[128,2048]{1,0:T(8,128)(2,1)S(1)}, u32[]{:S(2)}, u32[]{:S(2)}) %collective-permute-start.58) | collective-permute-done | bytes 524320 | tf_op jit(solution)/shard_map/cond/branch_1_fun/ppermute | solution.py:26
  500.1 11.8 %collective-permute-done.57.refs_3_ = bf16[256,2048]{1,0:T(8,128)(2,1)S(1)} collective-permute-done((bf16[256,2048]{1,0:T(8,128)(2,1)}, bf16[256,2048]{1,0:T(8,128)(2,1)S(1)}, u32[]{:S(2)}, u32[]{:S(2)}) %collective-permute-start.57) | collective-permute-done | bytes 1048608 | tf_op jit(solution)/shard_map/cond/branch_1_fun/ppermute | solution.py:26
  (380 shorter events, 291.8 us)
Async XLA Ops:
  7.2 101.1 %all-gather.4.cloned.1.call-start = ((), (), s32[]{:S(2)}) async-start(), calls=%async_computation.3 | async-start | bytes 5242880 | tf_op jit(solution)/shard_map/all_gather | solution.py:273
  27.1 216.2 %all-gather.6.cloned.1.call-start = ((), (), s32[]{:S(2)}) async-start(), calls=%async_computation.4 | async-start | bytes 5898240 | tf_op jit(solution)/shard_map/all_gather | solution.py:273
  29.8 25.8 %collective-permute-start.41 = (bf16[256,2048]{1,0:T(8,128)(2,1)}, bf16[256,2048]{1,0:T(8,128)(2,1)S(1)}, u32[]{:S(2)}, u32[]{:S(2)}) collective-permute-start(bf16[256,2048]{1,0:T(8,128)(2,1)} %get-tuple-element.172), channel_id=1, source_target_pairs={{0,4},{4,0},{1,5},{5,1},{2,6},{6,2},{3,7},{7,3},{8,12},{12,8},{9,1... | collective-permute-start | bytes 3145736 | tf_op jit(solution)/shard_map/cond/branch_1_fun/ppermute | solution.py:26
  67.8 36.3 %collective-permute-start.44 = (bf16[1024,2048]{1,0:T(8,128)(2,1)}, bf16[1024,2048]{1,0:T(8,128)(2,1)}, u32[]{:S(2)}, u32[]{:S(2)}) collective-permute-start(bf16[1024,2048]{1,0:T(8,128)(2,1)} %constant_dynamic-update-slice_fusion), channel_id=1, source_target_pairs={{0,1},{1,0},{2,3},{3,2},{4,5},{5,4},{6,7},{7,6},{8,9},{9,8},{10,11... | collective-permute-start | bytes 12582920 | tf_op jit(solution)/shard_map/cond/branch_1_fun/ppermute | solution.py:26
  71.4 25.0 %collective-permute-start.45 = (bf16[128,1152]{1,0:T(8,128)(2,1)}, bf16[128,1152]{1,0:T(8,128)(2,1)}, u32[]{:S(2)}, u32[]{:S(2)}) collective-permute-start(bf16[128,1152]{1,0:T(8,128)(2,1)} %get-tuple-element.173), channel_id=1, source_target_pairs={{0,6},{2,4},{4,2},{6,0},{1,7},{3,5},{5,3},{7,1},{8,14},{10,12},{12... | collective-permute-start | bytes 884744 | tf_op jit(solution)/shard_map/cond/branch_1_fun/ppermute | solution.py:34
  104.1 180.1 %all-gather.8.cloned.1.call-start = ((), (), s32[]{:S(2)}) async-start(), calls=%async_computation.6 | async-start | bytes 5242880 | tf_op jit(solution)/shard_map/all_gather | solution.py:273
  104.8 263.7 %reduce-scatter.4.cloned.1.call-start = ((), (), s32[]{:S(2)}) async-start(), calls=%async_computation.5 | async-start | bytes 5898240 | tf_op jit(solution)/shard_map/reduce_scatter | solution.py:277
  104.9 33.9 %collective-permute-start.67 = (bf16[256,2048]{1,0:T(8,128)(2,1)}, bf16[256,2048]{1,0:T(8,128)(2,1)}, u32[]{:S(2)}, u32[]{:S(2)}) collective-permute-start(bf16[256,2048]{1,0:T(8,128)(2,1)} %param.27), channel_id=1, source_target_pairs={{0,2},{2,0},{1,3},{3,1},{4,6},{6,4},{5,7},{7,5},{8,10},{10,8},{9,1... | collective-permute-start | bytes 3145736 | tf_op jit(solution)/shard_map/ppermute | solution.py:26
  106.3 32.6 %collective-permute-start.68 = (bf16[256,2048]{1,0:T(8,128)(2,1)}, bf16[256,2048]{1,0:T(8,128)(2,1)}, u32[]{:S(2)}, u32[]{:S(2)}) collective-permute-start(bf16[256,2048]{1,0:T(8,128)(2,1)} %param.27), channel_id=1, source_target_pairs={{0,4},{4,0},{1,5},{5,1},{2,6},{6,2},{3,7},{7,3},{8,12},{12,8},{9,1... | collective-permute-start | bytes 3145736 | tf_op jit(solution)/shard_map/ppermute | solution.py:26
  169.4 24.6 %collective-permute-start.5 = (bf16[256,2048]{1,0:T(8,128)(2,1)S(1)}, bf16[256,2048]{1,0:T(8,128)(2,1)S(1)}, u32[]{:S(2)}, u32[]{:S(2)}) collective-permute-start(bf16[256,2048]{1,0:T(8,128)(2,1)S(1)} %get-tuple-element.793), channel_id=1, source_target_pairs={{0,2},{2,0},{1,3},{3,1},{4,6},{6,4},{5,7},{7,5},{8,10},{10,8},{9,1... | collective-permute-start | bytes 3145736 | tf_op jit(solution)/shard_map/cond/branch_1_fun/ppermute | solution.py:26
  170.9 24.3 %collective-permute-start.6 = (bf16[256,2048]{1,0:T(8,128)(2,1)S(1)}, bf16[256,2048]{1,0:T(8,128)(2,1)S(1)}, u32[]{:S(2)}, u32[]{:S(2)}) collective-permute-start(bf16[256,2048]{1,0:T(8,128)(2,1)S(1)} %get-tuple-element.792), channel_id=1, source_target_pairs={{0,4},{4,0},{1,5},{5,1},{2,6},{6,2},{3,7},{7,3},{8,12},{12,8},{9,1... | collective-permute-start | bytes 3145736 | tf_op jit(solution)/shard_map/cond/branch_1_fun/ppermute | solution.py:26
  206.3 29.3 %collective-permute-start.12 = (bf16[1024,2048]{1,0:T(8,128)(2,1)}, bf16[1024,2048]{1,0:T(8,128)(2,1)}, u32[]{:S(2)}, u32[]{:S(2)}) collective-permute-start(bf16[1024,2048]{1,0:T(8,128)(2,1)} %constant_dynamic-update-slice_fusion.10), channel_id=1, source_target_pairs={{0,1},{1,0},{2,3},{3,2},{4,5},{5,4},{6,7},{7,6},{8,9},{9,8},{10,11... | collective-permute-start | bytes 12582920 | tf_op jit(solution)/shard_map/cond/branch_1_fun/ppermute | solution.py:26
  284.1 183.4 %reduce-scatter.6.cloned.1.call-start = ((), (), s32[]{:S(2)}) async-start(), calls=%async_computation.7 | async-start | bytes 5242880 | tf_op jit(solution)/shard_map/reduce_scatter | solution.py:277
  316.5 25.5 %collective-permute-start.17 = (bf16[256,2048]{1,0:T(8,128)(2,1)S(1)}, bf16[256,2048]{1,0:T(8,128)(2,1)S(1)}, u32[]{:S(2)}, u32[]{:S(2)}) collective-permute-start(bf16[256,2048]{1,0:T(8,128)(2,1)S(1)} %get-tuple-element.239), channel_id=1, source_target_pairs={{0,2},{2,0},{1,3},{3,1},{4,6},{6,4},{5,7},{7,5},{8,10},{10,8},{9,1... | collective-permute-start | bytes 3145736 | tf_op jit(solution)/shard_map/cond/branch_1_fun/ppermute | solution.py:26
  317.6 25.1 %collective-permute-start.18 = (bf16[256,2048]{1,0:T(8,128)(2,1)S(1)}, bf16[256,2048]{1,0:T(8,128)(2,1)S(1)}, u32[]{:S(2)}, u32[]{:S(2)}) collective-permute-start(bf16[256,2048]{1,0:T(8,128)(2,1)S(1)} %get-tuple-element.240), channel_id=1, source_target_pairs={{0,4},{4,0},{1,5},{5,1},{2,6},{6,2},{3,7},{7,3},{8,12},{12,8},{9,1... | collective-permute-start | bytes 3145736 | tf_op jit(solution)/shard_map/cond/branch_1_fun/ppermute | solution.py:26
  326.1 34.6 %collective-permute-start.22 = (bf16[256,2048]{1,0:T(8,128)(2,1)S(1)}, bf16[256,2048]{1,0:T(8,128)(2,1)S(1)}, u32[]{:S(2)}, u32[]{:S(2)}) collective-permute-start(bf16[256,2048]{1,0:T(8,128)(2,1)S(1)} %get-tuple-element.253), channel_id=1, source_target_pairs={{0,1},{1,0},{2,3},{3,2},{4,5},{5,4},{6,7},{7,6},{8,9},{9,8},{10,11... | collective-permute-start | bytes 3145736 | tf_op jit(solution)/shard_map/cond/branch_1_fun/ppermute | solution.py:26
  366.3 183.3 %reduce-scatter.8.cloned.1.call-start = ((), (), s32[]{:S(2)}) async-start(), calls=%async_computation.8 | async-start | bytes 5242880 | tf_op jit(solution)/shard_map/reduce_scatter | solution.py:277
  439.3 25.3 %collective-permute-start.36 = (bf16[256,2048]{1,0:T(8,128)(2,1)}, bf16[256,2048]{1,0:T(8,128)(2,1)}, u32[]{:S(2)}, u32[]{:S(2)}) collective-permute-start(bf16[256,2048]{1,0:T(8,128)(2,1)} %get-tuple-element.341), channel_id=1, source_target_pairs={{0,1},{1,0},{2,3},{3,2},{4,5},{5,4},{6,7},{7,6},{8,9},{9,8},{10,11... | collective-permute-start | bytes 3145736 | tf_op jit(solution)/shard_map/cond/branch_1_fun/ppermute | solution.py:26
  439.3 27.8 %collective-permute-start.37 = (bf16[256,2048]{1,0:T(8,128)(2,1)}, bf16[256,2048]{1,0:T(8,128)(2,1)}, u32[]{:S(2)}, u32[]{:S(2)}) collective-permute-start(bf16[256,2048]{1,0:T(8,128)(2,1)} %get-tuple-element.343), channel_id=1, source_target_pairs={{0,1},{1,0},{2,3},{3,2},{4,5},{5,4},{6,7},{7,6},{8,9},{9,8},{10,11... | collective-permute-start | bytes 3145736 | tf_op jit(solution)/shard_map/cond/branch_1_fun/ppermute | solution.py:26
  439.8 27.3 %collective-permute-start.38 = (bf16[256,2048]{1,0:T(8,128)(2,1)}, bf16[256,2048]{1,0:T(8,128)(2,1)}, u32[]{:S(2)}, u32[]{:S(2)}) collective-permute-start(bf16[256,2048]{1,0:T(8,128)(2,1)} %get-tuple-element.344), channel_id=1, source_target_pairs={{0,2},{2,0},{1,3},{3,1},{4,6},{6,4},{5,7},{7,5},{8,10},{10,8},{9,1... | collective-permute-start | bytes 3145736 | tf_op jit(solution)/shard_map/cond/branch_1_fun/ppermute | solution.py:26
  440.7 26.5 %collective-permute-start.39 = (bf16[256,2048]{1,0:T(8,128)(2,1)}, bf16[256,2048]{1,0:T(8,128)(2,1)}, u32[]{:S(2)}, u32[]{:S(2)}) collective-permute-start(bf16[256,2048]{1,0:T(8,128)(2,1)} %get-tuple-element.345), channel_id=1, source_target_pairs={{0,4},{4,0},{1,5},{5,1},{2,6},{6,2},{3,7},{7,3},{8,12},{12,8},{9,1... | collective-permute-start | bytes 3145736 | tf_op jit(solution)/shard_map/cond/branch_1_fun/ppermute | solution.py:26
  487.0 24.8 %collective-permute-start.57 = (bf16[256,2048]{1,0:T(8,128)(2,1)}, bf16[256,2048]{1,0:T(8,128)(2,1)S(1)}, u32[]{:S(2)}, u32[]{:S(2)}) collective-permute-start(bf16[256,2048]{1,0:T(8,128)(2,1)} %get-tuple-element.820), channel_id=1, source_target_pairs={{0,2},{2,0},{1,3},{3,1},{4,6},{6,4},{5,7},{7,5},{8,10},{10,8},{9,1... | collective-permute-start | bytes 3145736 | tf_op jit(solution)/shard_map/cond/branch_1_fun/ppermute | solution.py:26
  488.5 24.5 %collective-permute-start.59 = (bf16[256,2048]{1,0:T(8,128)(2,1)}, bf16[256,2048]{1,0:T(8,128)(2,1)S(1)}, u32[]{:S(2)}, u32[]{:S(2)}) collective-permute-start(bf16[256,2048]{1,0:T(8,128)(2,1)} %get-tuple-element.819), channel_id=1, source_target_pairs={{0,4},{4,0},{1,5},{5,1},{2,6},{6,2},{3,7},{7,3},{8,12},{12,8},{9,1... | collective-permute-start | bytes 3145736 | tf_op jit(solution)/shard_map/cond/branch_1_fun/ppermute | solution.py:26
  489.1 28.2 %collective-permute-start.54 = (bf16[256,2048]{1,0:T(8,128)(2,1)}, bf16[256,2048]{1,0:T(8,128)(2,1)S(1)}, u32[]{:S(2)}, u32[]{:S(2)}) collective-permute-start(bf16[256,2048]{1,0:T(8,128)(2,1)} %get-tuple-element.357), channel_id=1, source_target_pairs={{0,1},{1,0},{2,3},{3,2},{4,5},{5,4},{6,7},{7,6},{8,9},{9,8},{10,11... | collective-permute-start | bytes 3145736 | tf_op jit(solution)/shard_map/cond/branch_1_fun/ppermute | solution.py:26
  (108 other events, 1462.4 us)
Sparse Core Ops, SparseCore 0:
  27.2 81.0 all-gather.3
  110.4 87.9 all-gather.5
  200.6 79.2 all-gather.7
  284.2 84.2 reduce-scatter.3
  370.7 77.2 reduce-scatter.5
  467.6 78.2 reduce-scatter.7

commit v5 on v4

--- a/solution.py
+++ b/solution.py
@@ -779,7 +779,7 @@
         start += columns
 
 
-def weight_terms(*products):
+def weight_terms(*products, grant=20):
     model_width = products[0][0][0].shape[1]
     block = 256
     total = sum(rights[0].shape[-1] for _, rights in products)
@@ -794,7 +794,7 @@
         in_specs=specs,
         out_specs=pl.BlockSpec((block, total), lambda i: (i, 0)),
         out_shape=jax.ShapeDtypeStruct((model_width, total), bf16),
-        compiler_params=pltpu.CompilerParams(vmem_limit_bytes=20 << 20),
+        compiler_params=pltpu.CompilerParams(vmem_limit_bytes=grant << 20),
         cost_estimate=LIGHT,
         name="weight_terms",
     )(*operands)
@@ -994,7 +994,8 @@
         mlp_parts = swap(near, NEAR), swap(mid, MID)
         backs = own_back, sides_back, last_back
         terms = weight_terms(
-            (spread1, [back[0] for back in backs]), (row_pieces(own, sides, last), (context,))
+            (spread1, [back[0] for back in backs]), (row_pieces(own, sides, last), (context,)),
+            grant=48,
         )
         low, high = add_halves(last_back[2], swap(last_back[3], TP))
         bias_terms = sum(jnp.sum(back[1], axis=0) for back in backs)

time: 578 us -> 577 us (level)
    cond x80 -> x74, local copies, waits for them, and re-layouts: 33.1 us -> 28.6 us
  transfers between devices with their start and end apart: 82 -> 82, of which waited for: 43 -> 47; matrix products, arithmetic and copies ran while one was open for 12% -> 12% of each run, Pallas kernels for 35% -> 36%
where the time goes in v5:
time: 577 us; the launch traced here: 570 us
  Pallas kernels  205 us (36%)
  waiting for transfers between devices  185 us (32%)
  starting transfers between devices  74.2 us (13%)
  local copies, waits for them, and re-layouts  46.6 us (8%)
  other arithmetic  40.8 us (7%)
  between operations  16.2 us (3%)
    ppermute x64, waiting for transfers between devices, swap(): return lax.ppermute(values, axis, [(0, 1), (1, 0)])  159 us
    ppermute x64, starting transfers between devices, swap(): return lax.ppermute(values, axis, [(0, 1), (1, 0)])  59.2 us
    pallas_call x4, Pallas kernels, hidden_units(): pl.pallas_call(partial(units_kernel, parts), grid=(count,), in_specs=[giv...  52.7 us
    pallas_call x3, Pallas kernels, weight_terms(): pl.pallas_call(partial(weight_kernel, [(len(lefts), len(rights)) for left...  44.6 us
    pallas_call x3, Pallas kernels, attention_backward(): pl.pallas_call(backward_kernel, grid=(count,), in_specs=[row_block(rows,...  37.7 us
    cond x74, local copies, waits for them, and re-layouts  28.6 us
    pallas_call x1, Pallas kernels, attention_forward(): pl.pallas_call(forward_kernel, grid=(4,), in_specs=[row_block(rows, model...  27.6 us
    convert_element_type x8, other arithmetic, add_low(): return sum((value.astype(f32) for value in values)).astype(bf16)  16.4 us
  transfers between devices with their start and end apart: 82, of which 47 were waited for; matrix products, arithmetic and copies ran while one was open for 12% of the time, Pallas kernels for 36%

profile of v5, /device:TPU:0, one launch (start us, length us, event | category | flops | bytes accessed | tf_op | source)
XLA Modules:
  0.0 569.9 jit_solution(12115661014069261455)
XLA Ops:
  28.3 75.7 %conditional.6 = (bf16[1024,2048]{1,0:T(8,128)(2,1)}, bf16[1024,2048]{1,0:T(8,128)(2,1)}, bf16[512,1152]{1,0:T(8,128)(2,1)}, bf16[512,1024]{1,0:T(8,128)(2,1)}, ...) conditional(s32[]{:T(128)} %bitcast.17, () %tuple.74, ...), branch_computations={%region_0.1_spmd, %region_1.5_spmd} | conditional | flops 22639580 | bytes 59183784 | solution.py:269
  30.7 22.0 %collective-permute-done.40 = bf16[256,2048]{1,0:T(8,128)(2,1)S(1)} collective-permute-done((bf16[256,2048]{1,0:T(8,128)(2,1)}, bf16[256,2048]{1,0:T(8,128)(2,1)S(1)}, u32[]{:S(2)}, u32[]{:S(2)}) %collective-permute-start.40) | collective-permute-done | bytes 1048608 | tf_op jit(solution)/shard_map/cond/branch_1_fun/ppermute | solution.py:26
  108.3 30.5 %conditional.7 = ((bf16[2,4,256,768]{3,2,1,0:T(8,128)(2,1)}, bf16[2,4,256,256]{3,2,1,0:T(8,128)(2,1)}, f32[4,4,512]{2,1,0:T(4,128)S(1)}, bf16[1024,2048]{1,0:T(8,128)(2,1)}, bf16[1024,2048]{1,0:T(8,128)(2,1)})) conditional(s32[]{:T(128)} %bitcast.17, () %tuple.73, (s32[]{:T(128)}, f32[3,1024]{1,0:T(4,128)}, bf16[1024,2048]{1,0:T(8,128)(2,1)}, ...), branch_computations={%region_5.6_spmd, %region_6.7_spmd} | conditional | flops 8589934592 | bytes 42070128 | solution.py:269
  111.2 27.6 %attention_forward.1 = (bf16[2,4,256,768]{3,2,1,0:T(8,128)(2,1)}, bf16[2,4,256,256]{3,2,1,0:T(8,128)(2,1)}, f32[4,4,512]{2,1,0:T(4,128)S(1)}, bf16[1024,2048]{1,0:T(8,128)(2,1)}, bf16[1024,2048]{1,0:T(8,128)(2,1)}) custom-call(bf16[1024,2048]{1,0:T(8,128)(2,1)} %get-tuple-element.185.core_ref, bf16[1024,2048]{1,0:T(8,128)(2,1)} %get-tuple-element.186.other_ref, ...), custom_call_target="tpu_custom_call" | custom-call | flops 8589934592 | bytes 33554432 | tf_op jit(solution)/shard_map/cond/branch_1_fun/attention_forward/pallas_call | solution.py:584
  138.9 104.4 %conditional.8 = (f32[256,2048]{1,0:T(8,128)}, bf16[1024,2048]{1,0:T(8,128)(2,1)}, bf16[1024,2048]{1,0:T(8,128)(2,1)}, bf16[1024,2048]{1,0:T(8,128)(2,1)}, bf16[1024,2048]{1,0:T(8,128)(2,1)}) conditional(s32[]{:T(128)} %bitcast.17, () %tuple.72, (bf16[1024,2048]{1,0:T(8,128)(2,1)}, bf16[1024,2048]{1,0:T(8,128)(2,1)}, bf16[256,2048]{1,0:T(8,128)(2,1)}, ...), branch_computations={%region_7.8_spmd, %region_8.9_spmd} | conditional | flops 8388608 | bytes 132121192 | solution.py:269
  157.7 8.0 %collective-permute-done.1 = bf16[128,2048]{1,0:T(8,128)(2,1)S(1)} collective-permute-done((bf16[128,2048]{1,0:T(8,128)(2,1)S(1)}, bf16[128,2048]{1,0:T(8,128)(2,1)S(1)}, u32[]{:S(2)}, u32[]{:S(2)}) %collective-permute-start.1) | collective-permute-done | bytes 524320 | tf_op jit(solution)/shard_map/cond/branch_1_fun/ppermute | solution.py:26
  171.5 22.5 %collective-permute-done.5.refs_3_ = bf16[256,2048]{1,0:T(8,128)(2,1)S(1)} collective-permute-done((bf16[256,2048]{1,0:T(8,128)(2,1)S(1)}, bf16[256,2048]{1,0:T(8,128)(2,1)S(1)}, u32[]{:S(2)}, u32[]{:S(2)}) %collective-permute-start.5) | collective-permute-done | bytes 1048608 | tf_op jit(solution)/shard_map/cond/branch_1_fun/ppermute | solution.py:26
  206.3 15.0 %collective-permute-done.7 = bf16[256,2048]{1,0:T(8,128)(2,1)S(1)} collective-permute-done((bf16[256,2048]{1,0:T(8,128)(2,1)S(1)}, bf16[256,2048]{1,0:T(8,128)(2,1)S(1)}, u32[]{:S(2)}, u32[]{:S(2)}) %collective-permute-start.7) | collective-permute-done | bytes 1048608 | tf_op jit(solution)/shard_map/cond/branch_1_fun/ppermute | solution.py:26
  235.6 7.5 %collective-permute-done.11 = bf16[1024,2048]{1,0:T(8,128)(2,1)} collective-permute-done((bf16[1024,2048]{1,0:T(8,128)(2,1)}, bf16[1024,2048]{1,0:T(8,128)(2,1)}, u32[]{:S(2)}, u32[]{:S(2)}) %collective-permute-start.11) | collective-permute-done | bytes 4194336 | tf_op jit(solution)/shard_map/cond/branch_1_fun/ppermute | solution.py:26
  243.3 24.3 %hidden_units.7 = (bf16[2,4,256,768]{3,2,1,0:T(8,128)(2,1)S(1)}, bf16[2,4,256,384]{3,2,1,0:T(8,128)(2,1)S(1)}, bf16[1024,2048]{1,0:T(8,128)(2,1)}, bf16[1024,2048]{1,0:T(8,128)(2,1)}) custom-call(bf16[1024,2048]{1,0:T(8,128)(2,1)} %get-tuple-element.532.refs_0_.refs_3_, bf16[1024,2048]{1,0:T(8,128)(2,1)} %get-tuple-element.533.refs_1_.refs_4_, ...), custom_call_target="tpu_custom_call" | custom-call | flops 16106127360 | bytes 33554432 | tf_op jit(solution)/shard_map/hidden_units/pallas_call | solution.py:730
  267.6 14.3 %weight_terms.5 = bf16[2048,1152]{1,0:T(8,128)(2,1)S(1)} custom-call(bf16[1024,2048]{1,0:T(8,128)(2,1)} %get-tuple-element.530.refs_2_.refs_0_, bf16[1024,2048]{1,0:T(8,128)(2,1)} %get-tuple-element.531.refs_3_.refs_1_, bf16[2,4,256,384]{3,2,1,0:T(8,128)(2,1)S(1)} %get-tuple-element.534.refs_2_, bf16[1024,2048]{1,0:T(8,128)(2,1)} %get-tuple-element.532.refs_0_.refs_3_, ...), custom_call_target="tpu_custom_call" | custom-call | tf_op jit(solution)/shard_map/weight_terms/pallas_call | solution.py:791
  284.2 82.1 %conditional.9 = (bf16[256,2048]{1,0:T(8,128)(2,1)}, bf16[256,2048]{1,0:T(8,128)(2,1)}, bf16[512,2048]{1,0:T(8,128)(2,1)}, bf16[512,2048]{1,0:T(8,128)(2,1)}, bf...) conditional(s32[]{:T(128)} %bitcast.17, () %tuple.81, ...), branch_computations={%region_10.11_spmd, %region_11.12_spmd} | conditional | flops 10747904000 | bytes 153617024 | solution.py:269
  284.2 9.0 %hidden_units.4 = (bf16[2,1,256,640]{3,2,1,0:T(8,128)(2,1)S(1)}, bf16[2,1,256,384]{3,2,1,0:T(8,128)(2,1)S(1)}, bf16[256,2048]{1,0:T(8,128)(2,1)S(1)}, bf16[256,2048]{1,0:T(8,128)(2,1)S(1)}) custom-call(bf16[1024,2048]{1,0:T(8,128)(2,1)} %get-tuple-element.243.refs_0_.refs_5_, bf16[1024,2048]{1,0:T(8,128)(2,1)} %get-tuple-element.244.refs_1_.refs_6_, ...), custom_call_target="tpu_custom_call" | custom-call | flops 2684354560 | bytes 8388608 | tf_op jit(solution)/shard_map/cond/branch_1_fun/hidden_units/pallas_call | solution.py:730
  298.4 12.4 %hidden_units.5 = (bf16[2,2,256,640]{3,2,1,0:T(8,128)(2,1)S(1)}, bf16[2,2,256,384]{3,2,1,0:T(8,128)(2,1)S(1)}, bf16[512,2048]{1,0:T(8,128)(2,1)S(1)}, bf16[512,2048]{1,0:T(8,128)(2,1)S(1)}) custom-call(bf16[1024,2048]{1,0:T(8,128)(2,1)} %get-tuple-element.243.refs_0_.refs_5_, bf16[1024,2048]{1,0:T(8,128)(2,1)} %get-tuple-element.244.refs_1_.refs_6_, ...), custom_call_target="tpu_custom_call" | custom-call | flops 5368709120 | bytes 16777216 | tf_op jit(solution)/shard_map/cond/branch_1_fun/hidden_units/pallas_call | solution.py:730
  319.1 7.0 %hidden_units.6 = (bf16[2,1,256,640]{3,2,1,0:T(8,128)(2,1)S(1)}, bf16[2,1,256,384]{3,2,1,0:T(8,128)(2,1)S(1)}, bf16[256,2048]{1,0:T(8,128)(2,1)S(1)}, bf16[256,2048]{1,0:T(8,128)(2,1)S(1)}) custom-call(bf16[1024,2048]{1,0:T(8,128)(2,1)} %get-tuple-element.243.refs_0_.refs_5_, bf16[1024,2048]{1,0:T(8,128)(2,1)} %get-tuple-element.244.refs_1_.refs_6_, ...), custom_call_target="tpu_custom_call" | custom-call | flops 2684354560 | bytes 8388608 | tf_op jit(solution)/shard_map/cond/branch_1_fun/hidden_units/pallas_call | solution.py:730
  345.1 15.6 %weight_terms.3 = bf16[2048,1024]{1,0:T(8,128)(2,1)} custom-call(bf16[1024,2048]{1,0:T(8,128)(2,1)} %get-tuple-element.214.refs_2_.refs_0_, bf16[1024,2048]{1,0:T(8,128)(2,1)} %get-tuple-element.215.refs_3_.refs_1_, bf16[2,1,256,384]{3,2,1,0:T(8,128)(2,1)S(1)} %get-tuple-element.262.second_ref.refs_2_, ...), custom_call_target="tpu_custom_call" | custom-call | tf_op jit(solution)/shard_map/cond/branch_1_fun/weight_terms/pallas_call | solution.py:791
  368.5 97.4 %conditional.10 = (bf16[2048,1024]{1,0:T(8,128)(2,1)}, f32[1,768]{1,0:T(1,128)}, bf16[256,2048]{1,0:T(8,128)(2,1)}, bf16[256,2048]{1,0:T(8,128)(2,1)}, bf16[512,...) conditional(s32[]{:T(128)} %bitcast.17, () %tuple.80, ...), branch_computations={%region_12.13_spmd, %region_13.15_spmd} | conditional | flops 6450842112 | bytes 177740064 | solution.py:269
  375.5 11.0 %attention_backward.3 = (bf16[2,1,256,768]{3,2,1,0:T(8,128)(2,1)S(1)}, f32[1,1,768]{2,1,0:T(1,128)S(1)}, bf16[256,2048]{1,0:T(8,128)(2,1)}, bf16[256,2048]{1,0:T(8,128)(2,1)}) custom-call(bf16[256,2048]{1,0:T(8,128)(2,1)} %get-tuple-element.288.core_ref.refs_5_, bf16[256,2048]{1,0:T(8,128)(2,1)S(1)} %collective-permute-done.27.other_ref.refs_8_, ...), custom_call_target="tpu_custom_call" | custom-call | flops 2147483648 | bytes 8388608 | tf_op jit(solution)/shard_map/cond/branch_1_fun/attention_backward/pallas_call | solution.py:638
  403.5 16.4 %attention_backward.4 = (bf16[2,2,256,768]{3,2,1,0:T(8,128)(2,1)S(1)}, f32[2,1,768]{2,1,0:T(1,128)S(1)}, bf16[512,2048]{1,0:T(8,128)(2,1)}, bf16[512,2048]{1,0:T(8,128)(2,1)}) custom-call(bf16[512,2048]{1,0:T(8,128)(2,1)S(1)} %constant_dynamic-update-slice_fusion.15.core_ref.refs_6_, bf16[512,2048]{1,0:T(8,128)(2,1)S(1)} %collective-permute-done.31.other_ref.refs_9_, ...), custom_call_target="tpu_custom_call" | custom-call | flops 4294967296 | bytes 16777216 | tf_op jit(solution)/shard_map/cond/branch_1_fun/attention_backward/pallas_call | solution.py:638
  426.1 10.3 %attention_backward.5 = (bf16[2,1,256,768]{3,2,1,0:T(8,128)(2,1)S(1)}, f32[1,1,768]{2,1,0:T(1,128)S(1)}, bf16[256,2048]{1,0:T(8,128)(2,1)S(1)}, bf16[256,2048]{1,0:T(8,128)(2,1)}) custom-call(bf16[256,2048]{1,0:T(8,128)(2,1)S(1)} %constant_dynamic-update-slice_fusion.19.core_ref.refs_7_, bf16[256,2048]{1,0:T(8,128)(2,1)} %collective-permute-done.32.other_ref.refs_10_, ...), custom_call_target="tpu_custom_call" | custom-call | tf_op jit(solution)/shard_map/cond/branch_1_fun/attention_backward/pallas_call | solution.py:638
  445.7 14.8 %weight_terms.4 = bf16[2048,1024]{1,0:T(8,128)(2,1)} custom-call(bf16[1024,2048]{1,0:T(8,128)(2,1)} %get-tuple-element.284.refs_0_, bf16[1024,2048]{1,0:T(8,128)(2,1)} %get-tuple-element.285.refs_1_, bf16[2,1,256,768]{3,2,1,0:T(8,128)(2,1)S(1)} %copy-done.11, bf16[2,2,256,768]{3,2,1,0:T(8,128)(2,1)} %copy-done.5, bf16[2,1,256,768]{3,2,1,0:T(8,128)(2,1)S(1)} %copy-done.13, ...), custom_call_target="tpu_custom_call" | custom-call | tf_op jit(solution)/shard_map/cond/branch_1_fun/weight_terms/pallas_call | solution.py:791
  466.7 58.9 %conditional.11 = (bf16[256,2048]{1,0:T(8,128)(2,1)}, f32[256,2048]{1,0:T(8,128)}, bf16[128,1024]{1,0:T(8,128)(2,1)}, bf16[128,1024]{1,0:T(8,128)(2,1)}, bf16[12...) conditional(s32[]{:T(128)} %bitcast.17, () %tuple.71, ...), branch_computations={%region_16.17_spmd, %region_17.22_spmd} | conditional | flops 16859388 | bytes 53108452 | solution.py:269
  468.7 12.5 %collective-permute-done.58 = bf16[128,2048]{1,0:T(8,128)(2,1)S(1)} collective-permute-done((bf16[128,2048]{1,0:T(8,128)(2,1)}, bf16[128,2048]{1,0:T(8,128)(2,1)S(1)}, u32[]{:S(2)}, u32[]{:S(2)}) %collective-permute-start.58) | collective-permute-done | bytes 524320 | tf_op jit(solution)/shard_map/cond/branch_1_fun/ppermute | solution.py:26
  499.6 11.3 %collective-permute-done.57.refs_3_ = bf16[256,2048]{1,0:T(8,128)(2,1)S(1)} collective-permute-done((bf16[256,2048]{1,0:T(8,128)(2,1)}, bf16[256,2048]{1,0:T(8,128)(2,1)S(1)}, u32[]{:S(2)}, u32[]{:S(2)}) %collective-permute-start.57) | collective-permute-done | bytes 1048608 | tf_op jit(solution)/shard_map/cond/branch_1_fun/ppermute | solution.py:26
  (374 shorter events, 290.2 us)
Async XLA Ops:
  7.2 101.1 %all-gather.4.cloned.1.call-start = ((), (), s32[]{:S(2)}) async-start(), calls=%async_computation.3 | async-start | bytes 5242880 | tf_op jit(solution)/shard_map/all_gather | solution.py:273
  27.1 216.2 %all-gather.6.cloned.1.call-start = ((), (), s32[]{:S(2)}) async-start(), calls=%async_computation.4 | async-start | bytes 5898240 | tf_op jit(solution)/shard_map/all_gather | solution.py:273
  29.8 25.8 %collective-permute-start.41 = (bf16[256,2048]{1,0:T(8,128)(2,1)}, bf16[256,2048]{1,0:T(8,128)(2,1)S(1)}, u32[]{:S(2)}, u32[]{:S(2)}) collective-permute-start(bf16[256,2048]{1,0:T(8,128)(2,1)} %get-tuple-element.172), channel_id=1, source_target_pairs={{0,4},{4,0},{1,5},{5,1},{2,6},{6,2},{3,7},{7,3},{8,12},{12,8},{9,1... | collective-permute-start | bytes 3145736 | tf_op jit(solution)/shard_map/cond/branch_1_fun/ppermute | solution.py:26
  67.8 36.3 %collective-permute-start.44 = (bf16[1024,2048]{1,0:T(8,128)(2,1)}, bf16[1024,2048]{1,0:T(8,128)(2,1)}, u32[]{:S(2)}, u32[]{:S(2)}) collective-permute-start(bf16[1024,2048]{1,0:T(8,128)(2,1)} %constant_dynamic-update-slice_fusion), channel_id=1, source_target_pairs={{0,1},{1,0},{2,3},{3,2},{4,5},{5,4},{6,7},{7,6},{8,9},{9,8},{10,11... | collective-permute-start | bytes 12582920 | tf_op jit(solution)/shard_map/cond/branch_1_fun/ppermute | solution.py:26
  71.4 25.0 %collective-permute-start.45 = (bf16[128,1152]{1,0:T(8,128)(2,1)}, bf16[128,1152]{1,0:T(8,128)(2,1)}, u32[]{:S(2)}, u32[]{:S(2)}) collective-permute-start(bf16[128,1152]{1,0:T(8,128)(2,1)} %get-tuple-element.173), channel_id=1, source_target_pairs={{0,6},{2,4},{4,2},{6,0},{1,7},{3,5},{5,3},{7,1},{8,14},{10,12},{12... | collective-permute-start | bytes 884744 | tf_op jit(solution)/shard_map/cond/branch_1_fun/ppermute | solution.py:34
  104.1 180.0 %all-gather.8.cloned.1.call-start = ((), (), s32[]{:S(2)}) async-start(), calls=%async_computation.6 | async-start | bytes 5242880 | tf_op jit(solution)/shard_map/all_gather | solution.py:273
  104.8 263.7 %reduce-scatter.4.cloned.1.call-start = ((), (), s32[]{:S(2)}) async-start(), calls=%async_computation.5 | async-start | bytes 5898240 | tf_op jit(solution)/shard_map/reduce_scatter | solution.py:277
  104.9 33.9 %collective-permute-start.67 = (bf16[256,2048]{1,0:T(8,128)(2,1)}, bf16[256,2048]{1,0:T(8,128)(2,1)}, u32[]{:S(2)}, u32[]{:S(2)}) collective-permute-start(bf16[256,2048]{1,0:T(8,128)(2,1)} %param.27), channel_id=1, source_target_pairs={{0,2},{2,0},{1,3},{3,1},{4,6},{6,4},{5,7},{7,5},{8,10},{10,8},{9,1... | collective-permute-start | bytes 3145736 | tf_op jit(solution)/shard_map/ppermute | solution.py:26
  106.3 32.6 %collective-permute-start.68 = (bf16[256,2048]{1,0:T(8,128)(2,1)}, bf16[256,2048]{1,0:T(8,128)(2,1)}, u32[]{:S(2)}, u32[]{:S(2)}) collective-permute-start(bf16[256,2048]{1,0:T(8,128)(2,1)} %param.27), channel_id=1, source_target_pairs={{0,4},{4,0},{1,5},{5,1},{2,6},{6,2},{3,7},{7,3},{8,12},{12,8},{9,1... | collective-permute-start | bytes 3145736 | tf_op jit(solution)/shard_map/ppermute | solution.py:26
  169.4 24.6 %collective-permute-start.5 = (bf16[256,2048]{1,0:T(8,128)(2,1)S(1)}, bf16[256,2048]{1,0:T(8,128)(2,1)S(1)}, u32[]{:S(2)}, u32[]{:S(2)}) collective-permute-start(bf16[256,2048]{1,0:T(8,128)(2,1)S(1)} %get-tuple-element.793), channel_id=1, source_target_pairs={{0,2},{2,0},{1,3},{3,1},{4,6},{6,4},{5,7},{7,5},{8,10},{10,8},{9,1... | collective-permute-start | bytes 3145736 | tf_op jit(solution)/shard_map/cond/branch_1_fun/ppermute | solution.py:26
  170.9 24.3 %collective-permute-start.6 = (bf16[256,2048]{1,0:T(8,128)(2,1)S(1)}, bf16[256,2048]{1,0:T(8,128)(2,1)S(1)}, u32[]{:S(2)}, u32[]{:S(2)}) collective-permute-start(bf16[256,2048]{1,0:T(8,128)(2,1)S(1)} %get-tuple-element.792), channel_id=1, source_target_pairs={{0,4},{4,0},{1,5},{5,1},{2,6},{6,2},{3,7},{7,3},{8,12},{12,8},{9,1... | collective-permute-start | bytes 3145736 | tf_op jit(solution)/shard_map/cond/branch_1_fun/ppermute | solution.py:26
  199.5 24.2 %collective-permute-start.8 = (bf16[256,2048]{1,0:T(8,128)(2,1)S(1)}, bf16[256,2048]{1,0:T(8,128)(2,1)S(1)}, u32[]{:S(2)}, u32[]{:S(2)}) collective-permute-start(bf16[256,2048]{1,0:T(8,128)(2,1)S(1)} %get-tuple-element.206), channel_id=1, source_target_pairs={{0,4},{4,0},{1,5},{5,1},{2,6},{6,2},{3,7},{7,3},{8,12},{12,8},{9,1... | collective-permute-start | bytes 3145736 | tf_op jit(solution)/shard_map/cond/branch_1_fun/ppermute | solution.py:26
  206.3 29.3 %collective-permute-start.12 = (bf16[1024,2048]{1,0:T(8,128)(2,1)}, bf16[1024,2048]{1,0:T(8,128)(2,1)}, u32[]{:S(2)}, u32[]{:S(2)}) collective-permute-start(bf16[1024,2048]{1,0:T(8,128)(2,1)} %constant_dynamic-update-slice_fusion.10), channel_id=1, source_target_pairs={{0,1},{1,0},{2,3},{3,2},{4,5},{5,4},{6,7},{7,6},{8,9},{9,8},{10,11... | collective-permute-start | bytes 12582920 | tf_op jit(solution)/shard_map/cond/branch_1_fun/ppermute | solution.py:26
  284.1 182.0 %reduce-scatter.6.cloned.1.call-start = ((), (), s32[]{:S(2)}) async-start(), calls=%async_computation.7 | async-start | bytes 5242880 | tf_op jit(solution)/shard_map/reduce_scatter | solution.py:277
  316.5 25.5 %collective-permute-start.17 = (bf16[256,2048]{1,0:T(8,128)(2,1)S(1)}, bf16[256,2048]{1,0:T(8,128)(2,1)S(1)}, u32[]{:S(2)}, u32[]{:S(2)}) collective-permute-start(bf16[256,2048]{1,0:T(8,128)(2,1)S(1)} %get-tuple-element.239), channel_id=1, source_target_pairs={{0,2},{2,0},{1,3},{3,1},{4,6},{6,4},{5,7},{7,5},{8,10},{10,8},{9,1... | collective-permute-start | bytes 3145736 | tf_op jit(solution)/shard_map/cond/branch_1_fun/ppermute | solution.py:26
  317.6 25.1 %collective-permute-start.18 = (bf16[256,2048]{1,0:T(8,128)(2,1)S(1)}, bf16[256,2048]{1,0:T(8,128)(2,1)S(1)}, u32[]{:S(2)}, u32[]{:S(2)}) collective-permute-start(bf16[256,2048]{1,0:T(8,128)(2,1)S(1)} %get-tuple-element.240), channel_id=1, source_target_pairs={{0,4},{4,0},{1,5},{5,1},{2,6},{6,2},{3,7},{7,3},{8,12},{12,8},{9,1... | collective-permute-start | bytes 3145736 | tf_op jit(solution)/shard_map/cond/branch_1_fun/ppermute | solution.py:26
  326.1 34.6 %collective-permute-start.22 = (bf16[256,2048]{1,0:T(8,128)(2,1)S(1)}, bf16[256,2048]{1,0:T(8,128)(2,1)S(1)}, u32[]{:S(2)}, u32[]{:S(2)}) collective-permute-start(bf16[256,2048]{1,0:T(8,128)(2,1)S(1)} %get-tuple-element.253), channel_id=1, source_target_pairs={{0,1},{1,0},{2,3},{3,2},{4,5},{5,4},{6,7},{7,6},{8,9},{9,8},{10,11... | collective-permute-start | bytes 3145736 | tf_op jit(solution)/shard_map/cond/branch_1_fun/ppermute | solution.py:26
  366.3 182.4 %reduce-scatter.8.cloned.1.call-start = ((), (), s32[]{:S(2)}) async-start(), calls=%async_computation.8 | async-start | bytes 5242880 | tf_op jit(solution)/shard_map/reduce_scatter | solution.py:277
  439.3 24.3 %collective-permute-start.37 = (bf16[256,2048]{1,0:T(8,128)(2,1)}, bf16[256,2048]{1,0:T(8,128)(2,1)}, u32[]{:S(2)}, u32[]{:S(2)}) collective-permute-start(bf16[256,2048]{1,0:T(8,128)(2,1)} %get-tuple-element.343), channel_id=1, source_target_pairs={{0,1},{1,0},{2,3},{3,2},{4,5},{5,4},{6,7},{7,6},{8,9},{9,8},{10,11... | collective-permute-start | bytes 3145736 | tf_op jit(solution)/shard_map/cond/branch_1_fun/ppermute | solution.py:26
  439.8 25.4 %collective-permute-start.38 = (bf16[256,2048]{1,0:T(8,128)(2,1)}, bf16[256,2048]{1,0:T(8,128)(2,1)}, u32[]{:S(2)}, u32[]{:S(2)}) collective-permute-start(bf16[256,2048]{1,0:T(8,128)(2,1)} %get-tuple-element.344), channel_id=1, source_target_pairs={{0,2},{2,0},{1,3},{3,1},{4,6},{6,4},{5,7},{7,5},{8,10},{10,8},{9,1... | collective-permute-start | bytes 3145736 | tf_op jit(solution)/shard_map/cond/branch_1_fun/ppermute | solution.py:26
  440.6 25.1 %collective-permute-start.39 = (bf16[256,2048]{1,0:T(8,128)(2,1)}, bf16[256,2048]{1,0:T(8,128)(2,1)}, u32[]{:S(2)}, u32[]{:S(2)}) collective-permute-start(bf16[256,2048]{1,0:T(8,128)(2,1)} %get-tuple-element.345), channel_id=1, source_target_pairs={{0,4},{4,0},{1,5},{5,1},{2,6},{6,2},{3,7},{7,3},{8,12},{12,8},{9,1... | collective-permute-start | bytes 3145736 | tf_op jit(solution)/shard_map/cond/branch_1_fun/ppermute | solution.py:26
  486.2 24.8 %collective-permute-start.57 = (bf16[256,2048]{1,0:T(8,128)(2,1)}, bf16[256,2048]{1,0:T(8,128)(2,1)S(1)}, u32[]{:S(2)}, u32[]{:S(2)}) collective-permute-start(bf16[256,2048]{1,0:T(8,128)(2,1)} %get-tuple-element.820), channel_id=1, source_target_pairs={{0,2},{2,0},{1,3},{3,1},{4,6},{6,4},{5,7},{7,5},{8,10},{10,8},{9,1... | collective-permute-start | bytes 3145736 | tf_op jit(solution)/shard_map/cond/branch_1_fun/ppermute | solution.py:26
  487.0 24.5 %collective-permute-start.59 = (bf16[256,2048]{1,0:T(8,128)(2,1)}, bf16[256,2048]{1,0:T(8,128)(2,1)S(1)}, u32[]{:S(2)}, u32[]{:S(2)}) collective-permute-start(bf16[256,2048]{1,0:T(8,128)(2,1)} %get-tuple-element.819), channel_id=1, source_target_pairs={{0,4},{4,0},{1,5},{5,1},{2,6},{6,2},{3,7},{7,3},{8,12},{12,8},{9,1... | collective-permute-start | bytes 3145736 | tf_op jit(solution)/shard_map/cond/branch_1_fun/ppermute | solution.py:26
  488.5 27.3 %collective-permute-start.54 = (bf16[256,2048]{1,0:T(8,128)(2,1)}, bf16[256,2048]{1,0:T(8,128)(2,1)S(1)}, u32[]{:S(2)}, u32[]{:S(2)}) collective-permute-start(bf16[256,2048]{1,0:T(8,128)(2,1)} %get-tuple-element.357), channel_id=1, source_target_pairs={{0,1},{1,0},{2,3},{3,2},{4,5},{5,4},{6,7},{7,6},{8,9},{9,8},{10,11... | collective-permute-start | bytes 3145736 | tf_op jit(solution)/shard_map/cond/branch_1_fun/ppermute | solution.py:26
  (105 other events, 1450.6 us)
Sparse Core Ops, SparseCore 0:
  27.2 81.0 all-gather.3
  110.4 87.9 all-gather.5
  200.6 79.2 all-gather.7
  284.2 84.2 reduce-scatter.3
  370.7 77.2 reduce-scatter.5
  466.1 78.5 reduce-scatter.7
